TPU v7x, 512 devices: a whole 4x4x16 slice. The times are simulated.
512 devices in a mesh: cuts: 8 (over x, core), strip: 64 (over y, z).
Axes of the slice: x: 4, y: 4, z: 16, core: 2. Of those that a mesh axis runs over, the one named last changes fastest.
Arguments:
- object_slices: bfloat16 [8, 2, 8192, 256], P('cuts', None, 'strip'), may hold values from -6 to 6
- direction: bfloat16 [8, 2, 8192, 256], P('cuts', None, 'strip'), may hold values from -6 to 6
- probe_wave: bfloat16 [2, 128, 128], replicated, may hold values from -6 to 6
- kernel_phase: float32 [128, 128], replicated, may hold values from -3.140625 to 3.140625
- corner_row: int32 [128], P('strip'), may hold values from 0 to 8191, as said below
- corner_col: int32 [128], P('strip'), may hold values from 0 to 128
Outputs:
- hessian_vector: float32 [8, 2, 8192, 256], P('cuts', None, 'strip')
Inputs may be any that keep to these rules, and one draw needn't show every extreme that they name: `corner_row`: position j belongs to strip index j // 2; its corner row lies in the strips from 2 below to 2 above that index, counted around the periodic object, and both extremes occur.
All inputs are finite; a program needn't handle non-finite values.
Results may differ from a plain program's by a relative error of at most 0.03.
Values may be sent and summed in bfloat16 or wider, within the bound.
No kernel may reach another device: no remote copies, remote signals or barrier semaphores. Data moves between devices by JAX's collectives and lax.ppermute only.
A program may use at most 64 MiB of HBM per device.

v0:
```python
import math

import jax
import jax.numpy as jnp
from jax import lax
from jax.sharding import PartitionSpec as P

REACH = 2


def passed_along(block, axis, distance):
    devices = range(lax.axis_size(axis))
    route = [((i - distance) % len(devices), i) for i in devices]
    return lax.ppermute(block, axis, route)


def from_behind(value, axis, steps):
    count = lax.axis_size(axis)
    first, last = (max(0, -steps), min(count, count - steps))
    return lax.ppermute(value, axis, [(source, source + steps) for source in range(first, last)])


def tables(size_value):
    index_line = jnp.arange(size_value, dtype=jnp.int32)
    product = index_line[:, None] * index_line[None, :] % size_value
    angle_table = product.astype(jnp.float32) * (2.0 * math.pi / size_value)
    scale = 1.0 / math.sqrt(size_value)
    return (jnp.cos(angle_table) * scale, jnp.sin(angle_table) * scale)


def left_apply(matrix, values):
    return jnp.einsum(
        "jk,...kl->...jl",
        matrix,
        values,
        precision=lax.Precision.HIGHEST,
        preferred_element_type=jnp.float32,
    )


def right_apply(values, matrix):
    return jnp.einsum(
        "...jk,kl->...jl",
        values,
        matrix,
        precision=lax.Precision.HIGHEST,
        preferred_element_type=jnp.float32,
    )


def transform(real_part, imag_part, cosine_table, sine_table, orientation):
    half_re = left_apply(cosine_table, real_part) - orientation * left_apply(sine_table, imag_part)
    half_im = left_apply(cosine_table, imag_part) + orientation * left_apply(sine_table, real_part)
    full_re = right_apply(half_re, cosine_table) - orientation * right_apply(half_im, sine_table)
    full_im = right_apply(half_im, cosine_table) + orientation * right_apply(half_re, sine_table)
    return (full_re, full_im)


def exits(local_windows, wave_in):
    obj_re, obj_im = (local_windows[:, 0], local_windows[:, 1])
    dir_re, dir_im = (local_windows[:, 2], local_windows[:, 3])
    psi_re, psi_im = (wave_in[:, 0], wave_in[:, 1])
    tan_re, tan_im = (wave_in[:, 2], wave_in[:, 3])
    exit_re = obj_re * psi_re - obj_im * psi_im
    exit_im = obj_re * psi_im + obj_im * psi_re
    delta_re = dir_re * psi_re - dir_im * psi_im + obj_re * tan_re - obj_im * tan_im
    delta_im = dir_re * psi_im + dir_im * psi_re + obj_re * tan_im + obj_im * tan_re
    return (jnp.stack([exit_re, delta_re], 1), jnp.stack([exit_im, delta_im], 1))


def on_device(object_slices, direction, probe_wave, kernel_phase, corner_row, corner_col):
    strip_rows = object_slices.shape[2]
    column_count = object_slices.shape[3]
    patch_size = probe_wave.shape[1]
    slot_count = corner_row.shape[0]
    strip_count = lax.axis_size("strip")
    cuts_count = lax.axis_size("cuts")
    strip_index = lax.axis_index("strip")
    cut_index = lax.axis_index("cuts")
    cosine_table, sine_table = tables(patch_size)
    kernel_cos = jnp.cos(kernel_phase)
    kernel_sin = jnp.sin(kernel_phase)

    def forward_fourier(real_part, imag_part):
        return transform(real_part, imag_part, cosine_table, sine_table, -1.0)

    def inverse_fourier(real_part, imag_part):
        return transform(real_part, imag_part, cosine_table, sine_table, 1.0)

    def apply_kernel(real_part, imag_part, conj_sign):
        kernel_im = conj_sign * kernel_sin
        return (
            real_part * kernel_cos - imag_part * kernel_im,
            real_part * kernel_im + imag_part * kernel_cos,
        )

    def propagate(real_part, imag_part, conj_sign):
        fourier_re, fourier_im = forward_fourier(real_part, imag_part)
        kept_re, kept_im = apply_kernel(fourier_re, fourier_im, conj_sign)
        return inverse_fourier(kept_re, kept_im)

    def far_adjoint(stacked_re, stacked_im):
        fourier_re, fourier_im = forward_fourier(stacked_re, stacked_im)
        far_re, far_im = apply_kernel(fourier_re, fourier_im, 1.0)
        weight = 4.0 / cuts_count * (far_re[:, 0] * far_re[:, 1] + far_im[:, 0] * far_im[:, 1])
        back_re, back_im = apply_kernel(weight * far_re[:, 0], weight * far_im[:, 0], -1.0)
        return inverse_fourier(back_re, back_im)

    stacked_object = jnp.concatenate([object_slices, direction], axis=1)[0]
    pieces = []
    for offset in range(-REACH, REACH + 2):
        if offset == 0:
            pieces.append(stacked_object)
        else:
            pieces.append(passed_along(stacked_object, "strip", -offset))
    object_band = jnp.concatenate(pieces, axis=1)
    quotient = corner_row // strip_rows
    relative = (quotient - strip_index + REACH) % strip_count
    row_start = relative * strip_rows + corner_row % strip_rows

    def cut_window(start_row, start_col):
        rows_band = lax.dynamic_slice_in_dim(object_band, start_row, patch_size, 1)
        doubled = jnp.concatenate([rows_band, rows_band], axis=2)
        return lax.dynamic_slice_in_dim(doubled, start_col, patch_size, 2)

    windows = jax.vmap(cut_window)(row_start, corner_col)
    micro_count = 1
    group_size = slot_count // micro_count
    start_wave = jnp.concatenate([probe_wave, jnp.zeros_like(probe_wave)], axis=0)
    start_wave = jnp.broadcast_to(start_wave[None], (group_size, 4, patch_size, patch_size))

    def forward_section(section_index, received, saved_wave, saved_mu):
        micro_index = section_index - cut_index
        active = (micro_index >= 0) & (micro_index < micro_count)
        clipped = jnp.clip(micro_index, 0, micro_count - 1)

        def forward_active_work(operands):
            received, saved_wave, saved_mu = operands
            incoming = jnp.where(cut_index == 0, start_wave, received)
            local_windows = windows.astype(jnp.float32)
            stacked_re, stacked_im = exits(local_windows, incoming.astype(jnp.float32))

            def middle(values):
                next_re, next_im = propagate(values[0], values[1], 1.0)
                outgoing = jnp.concatenate(
                    [next_re[:, 0:1], next_im[:, 0:1], next_re[:, 1:2], next_im[:, 1:2]], 1
                )
                return (
                    outgoing.astype(jnp.bfloat16),
                    jnp.zeros((group_size, 2, patch_size, patch_size), jnp.float32),
                )

            def last_slice(values):
                adj_re, adj_im = far_adjoint(values[0], values[1])
                return (
                    jnp.zeros((group_size, 4, patch_size, patch_size), jnp.bfloat16),
                    jnp.stack([adj_re, adj_im], 1),
                )

            outgoing, adjoint = lax.cond(
                cut_index == cuts_count - 1, last_slice, middle, (stacked_re, stacked_im)
            )
            saved_wave = incoming[:, 0:2]
            saved_mu = adjoint
            return (outgoing, saved_wave, saved_mu)

        def forward_pass_through(operands):
            return operands

        return lax.cond(
            active, forward_active_work, forward_pass_through, (received, saved_wave, saved_mu)
        )

    zero_wave = jnp.zeros((group_size, 4, patch_size, patch_size), jnp.bfloat16)
    empty_wave = jnp.zeros((slot_count, 2, patch_size, patch_size), jnp.bfloat16)
    empty_mu = jnp.zeros((slot_count, 2, patch_size, patch_size), jnp.float32)
    loop_state = forward_section(0, zero_wave, empty_wave, empty_mu)

    def forward_loop(section_index, loop_state):
        outgoing, saved_wave, saved_mu = loop_state
        received = from_behind(outgoing, "cuts", 1)
        return forward_section(section_index, received, saved_wave, saved_mu)

    outgoing, saved_wave, saved_mu = lax.fori_loop(
        1, cuts_count + micro_count - 1, forward_loop, loop_state
    )

    def backward_section(section_index, received, gradient):
        micro_index = section_index - (cuts_count - 1 - cut_index)
        active = (micro_index >= 0) & (micro_index < micro_count)
        clipped = jnp.clip(micro_index, 0, micro_count - 1)
        offset = clipped * group_size

        def backward_active_work(operands):
            received, gradient = operands

            def from_chain(values):
                lam_in = values.astype(jnp.float32)
                return propagate(lam_in[:, 0], lam_in[:, 1], -1.0)

            def from_store(values):
                return (saved_mu[:, 0], saved_mu[:, 1])

            adj_re, adj_im = lax.cond(cut_index == cuts_count - 1, from_store, from_chain, received)
            wave_in = saved_wave.astype(jnp.float32)
            local_windows = windows.astype(jnp.float32)
            psi_re, psi_im = (wave_in[:, 0], wave_in[:, 1])
            obj_re, obj_im = (local_windows[:, 0], local_windows[:, 1])
            grad_re = psi_re * adj_re + psi_im * adj_im
            grad_im = psi_re * adj_im - psi_im * adj_re
            lam_re = obj_re * adj_re + obj_im * adj_im
            lam_im = obj_re * adj_im - obj_im * adj_re
            outgoing = jnp.stack([lam_re, lam_im], 1).astype(jnp.bfloat16)
            gradient = jnp.stack([grad_re, grad_im], 1)
            return (outgoing, gradient)

        def backward_pass_through(operands):
            return operands

        return lax.cond(active, backward_active_work, backward_pass_through, (received, gradient))

    zero_lam = jnp.zeros((group_size, 2, patch_size, patch_size), jnp.bfloat16)
    loop_state = backward_section(0, zero_lam, empty_mu)

    def backward_loop(section_index, loop_state):
        outgoing, gradient = loop_state
        received = from_behind(outgoing, "cuts", -1)
        return backward_section(section_index, received, gradient)

    outgoing, gradient = lax.fori_loop(1, cuts_count + micro_count - 1, backward_loop, loop_state)
    band_rows = (2 * REACH + 2) * strip_rows
    gradient_band = jnp.zeros((2, band_rows, column_count), jnp.float32)
    for slot_index in range(slot_count):
        wide_patch = jnp.zeros((2, patch_size, 2 * column_count), jnp.float32)
        wide_patch = lax.dynamic_update_slice(
            wide_patch, gradient[slot_index], (0, 0, corner_col[slot_index])
        )
        folded = wide_patch[:, :, :column_count] + wide_patch[:, :, column_count:]
        current = lax.dynamic_slice_in_dim(gradient_band, row_start[slot_index], patch_size, 1)
        gradient_band = lax.dynamic_update_slice_in_dim(
            gradient_band, current + folded, row_start[slot_index], 1
        )
    result_strip = gradient_band[:, REACH * strip_rows : (REACH + 1) * strip_rows]
    for offset in range(-REACH, REACH + 2):
        if offset != 0:
            piece = gradient_band[
                :, (offset + REACH) * strip_rows : (offset + REACH + 1) * strip_rows
            ]
            result_strip = result_strip + passed_along(piece, "strip", offset)
    return result_strip[None]


def solution(mesh):
    in_specs = (
        P("cuts", None, "strip", None),
        P("cuts", None, "strip", None),
        P(),
        P(),
        P("strip"),
        P("strip"),
    )
    out_specs = P("cuts", None, "strip", None)
    return jax.shard_map(
        on_device, mesh=mesh, in_specs=in_specs, out_specs=out_specs, check_vma=False
    )
```

profile of v0, /device:TPU:1, one launch (start us, length us, event | category | flops | bytes accessed | tf_op | source)
XLA Modules:
  0.0 336.5 jit_solution(11137523278834427116)
XLA Ops:
  2.4 5.7 %collective-permute-start.2 = (bf16[4,128,256]{2,0,1:T(4,128)(2,1)S(1)}, bf16[4,128,256]{2,0,1:T(4,128)(2,1)S(1)}, u32[]{:S(2)}, u32[]{:S(2)}) collective-permute-start(bf16[4,128,256]{2,0,1:T(4,128)(2,1)S(1)} %maximum_bitcast_fusion), channel_id=1, source_target_pairs={{62,0},{63,1},{0,2},{1,3},{2,4},{3,5},{4,6},{5,7},{6,8},{7,9},{8,1... | collective-permute-start | bytes 786440 | tf_op jit(solution)/shard_map/ppermute | solution.py:14
  8.1 3.5 %collective-permute-start.3 = (bf16[4,128,256]{2,0,1:T(4,128)(2,1)S(1)}, bf16[4,128,256]{2,0,1:T(4,128)(2,1)S(1)}, u32[]{:S(2)}, u32[]{:S(2)}) collective-permute-start(bf16[4,128,256]{2,0,1:T(4,128)(2,1)S(1)} %maximum_bitcast_fusion), channel_id=1, source_target_pairs={{63,0},{0,1},{1,2},{2,3},{3,4},{4,5},{5,6},{6,7},{7,8},{8,9},{9,10... | collective-permute-start | bytes 786440 | tf_op jit(solution)/shard_map/ppermute | solution.py:14
  11.7 9.0 %collective-permute-start.4 = (bf16[4,128,256]{2,0,1:T(4,128)(2,1)S(1)}, bf16[4,128,256]{2,0,1:T(4,128)(2,1)S(1)}, u32[]{:S(2)}, u32[]{:S(2)}) collective-permute-start(bf16[4,128,256]{2,0,1:T(4,128)(2,1)S(1)} %maximum_bitcast_fusion), channel_id=1, source_target_pairs={{1,0},{2,1},{3,2},{4,3},{5,4},{6,5},{7,6},{8,7},{9,8},{10,9},{11,1... | collective-permute-start | bytes 786440 | tf_op jit(solution)/shard_map/ppermute | solution.py:14
  20.6 4.3 %collective-permute-start.5 = (bf16[4,128,256]{2,0,1:T(4,128)(2,1)S(1)}, bf16[4,128,256]{2,0,1:T(4,128)(2,1)S(1)}, u32[]{:S(2)}, u32[]{:S(2)}) collective-permute-start(bf16[4,128,256]{2,0,1:T(4,128)(2,1)S(1)} %maximum_bitcast_fusion), channel_id=1, source_target_pairs={{2,0},{3,1},{4,2},{5,3},{6,4},{7,5},{8,6},{9,7},{10,8},{11,9},{12,... | collective-permute-start | bytes 786440 | tf_op jit(solution)/shard_map/ppermute | solution.py:14
  37.8 5.5 %collective-permute-start.6 = (bf16[4,128,256]{2,0,1:T(4,128)(2,1)S(1)}, bf16[4,128,256]{2,0,1:T(4,128)(2,1)S(1)}, u32[]{:S(2)}, u32[]{:S(2)}) collective-permute-start(bf16[4,128,256]{2,0,1:T(4,128)(2,1)S(1)} %maximum_bitcast_fusion), channel_id=1, source_target_pairs={{3,0},{4,1},{5,2},{6,3},{7,4},{8,5},{9,6},{10,7},{11,8},{12,9},{13... | collective-permute-start | bytes 786440 | tf_op jit(solution)/shard_map/ppermute | solution.py:14
  44.0 15.5 %collective-permute-done.6 = bf16[4,128,256]{2,0,1:T(4,128)(2,1)S(1)} collective-permute-done((bf16[4,128,256]{2,0,1:T(4,128)(2,1)S(1)}, bf16[4,128,256]{2,0,1:T(4,128)(2,1)S(1)}, u32[]{:S(2)}, u32[]{:S(2)}) %collective-permute-start.6) | collective-permute-done | bytes 262176 | tf_op jit(solution)/shard_map/ppermute | solution.py:14
  65.8 13.0 %conditional.8 = (bf16[2,4,128,128]{3,2,1,0:T(8,128)(2,1)}, bf16[2,2,128,128]{2,3,1,0:T(8,128)(2,1)S(1)}, f32[2,2,128,128]{3,2,0,1:T(8,128)}) conditional(s32[]{:T(128)} %convert_element_type.253, () %tuple.100, (s32[]{:T(128)}, bf16[2,4,128,128]{2,1,3,0:T(4,128)(2,1)S(1)}, bf16[4,128,128]{1,2,0:T(8,128)(2,1)S(1)}, f32[128,128]{1,0:T(8,128)S(1)}, ...), branch_computations={%region_0.1_spmd, %region_1.4_spmd} | conditional | flops 1613692928 | bytes 18416004 | solution.py:170
  78.8 100.8 %while.43 = (s32[]{:T(128)}, bf16[2,4,128,128]{3,2,1,0:T(8,128)(2,1)}, bf16[2,2,128,128]{2,3,1,0:T(8,128)(2,1)S(1)}, f32[2,2,128,128]{3,2,0,1:T(8,128)}, s32[]{:...) while((s32[]{:T(128)}, ...), condition=%wide.region_9.10_spmd.clone.clone, body=%wide.region_4.9_spmd.clone.clone.sunk | while | flops 1614151680 | bytes 22151700 | solution.py:184
  80.0 5.0 %collective-permute-start = (bf16[2,4,128,128]{2,3,1,0:T(8,128)(2,1)S(1)}, bf16[2,4,128,128]{2,3,1,0:T(8,128)(2,1)S(1)}, u32[]{:S(2)}, u32[]{:S(2)}) collective-permute-start(bf16[2,4,128,128]{2,3,1,0:T(8,128)(2,1)S(1)} %copy.271), channel_id=1, source_target_pairs={{0,64},{64,128},{128,192},{192,256},{256,320},{320,384},{384,448},... | collective-permute-start | bytes 786440 | tf_op jit(solution)/shard_map/while/body/eval_jaxpr/ppermute | solution.py:20
  85.1 8.7 %collective-permute-done = bf16[2,4,128,128]{2,3,1,0:T(8,128)(2,1)S(1)} collective-permute-done((bf16[2,4,128,128]{2,3,1,0:T(8,128)(2,1)S(1)}, bf16[2,4,128,128]{2,3,1,0:T(8,128)(2,1)S(1)}, u32[]{:S(2)}, u32[]{:S(2)}) %collective-permute-start) | collective-permute-done | bytes 262176 | tf_op jit(solution)/shard_map/while/body/eval_jaxpr/ppermute | solution.py:20
  93.8 11.0 %conditional.18 = (bf16[2,4,128,128]{3,2,1,0:T(8,128)(2,1)}, bf16[2,2,128,128]{2,3,1,0:T(8,128)(2,1)S(1)}, f32[2,2,128,128]{3,2,0,1:T(8,128)}) conditional(s32[]{:T(128)} %convert_element_type.301, (bf16[2,4,128,128]{2,3,1,0:T(8,128)(2,1)S(1)}, bf16[2,2,128,128]{2,3,1,0:T(8,128)(2,1)S(1)}, f32[2,2,128,128]{3,2,0,1:T(8,128)}) %tuple.243, ...), branch_computations={%region_5.5_spmd, %region_6.8_spmd.clone} | conditional | flops 1613922304 | bytes 20447460 | solution.py:170
  94.5 10.3 %conditional.14 = (bf16[2,4,128,128]{3,2,1,0:T(8,128)(2,1)}, f32[2,2,128,128]{3,2,0,1:T(8,128)}) conditional(s32[]{:T(128)} %convert_element_type.275, (f32[2,2,128,128]{2,3,1,0:T(8,128)S(1)}, f32[128,128]{1,0:T(8,128)S(1)}, f32[2,2,128,128]{2,3,1,0:T(8,128)S(1)}, f32[128,128]{1,0:T(8,128)S(1)}, f32[128,128]{1,0:T(8,128)S(1)}, ...), branch_computations={%region_7.6_spmd, %region_8.7_spmd} | conditional | flops 1612709888 | bytes 14155796 | solution.py:160
  107.9 3.2 collective-permute-done
  113.1 14.6 %collective-permute-start = (bf16[2,4,128,128]{2,3,1,0:T(8,128)(2,1)S(1)}, bf16[2,4,128,128]{2,3,1,0:T(8,128)(2,1)S(1)}, u32[]{:S(2)}, u32[]{:S(2)}) collective-permute-start(bf16[2,4,128,128]{2,3,1,0:T(8,128)(2,1)S(1)} %copy.271), channel_id=1, source_target_pairs={{0,64},{64,128},{128,192},{192,256},{256,320},{320,384},{384,448},... | collective-permute-start | bytes 786440 | tf_op jit(solution)/shard_map/while/body/eval_jaxpr/ppermute | solution.py:20
  133.0 4.4 %collective-permute-start = (bf16[2,4,128,128]{2,3,1,0:T(8,128)(2,1)S(1)}, bf16[2,4,128,128]{2,3,1,0:T(8,128)(2,1)S(1)}, u32[]{:S(2)}, u32[]{:S(2)}) collective-permute-start(bf16[2,4,128,128]{2,3,1,0:T(8,128)(2,1)S(1)} %copy.271), channel_id=1, source_target_pairs={{0,64},{64,128},{128,192},{192,256},{256,320},{320,384},{384,448},... | collective-permute-start | bytes 786440 | tf_op jit(solution)/shard_map/while/body/eval_jaxpr/ppermute | solution.py:20
  142.7 5.7 %collective-permute-start = (bf16[2,4,128,128]{2,3,1,0:T(8,128)(2,1)S(1)}, bf16[2,4,128,128]{2,3,1,0:T(8,128)(2,1)S(1)}, u32[]{:S(2)}, u32[]{:S(2)}) collective-permute-start(bf16[2,4,128,128]{2,3,1,0:T(8,128)(2,1)S(1)} %copy.271), channel_id=1, source_target_pairs={{0,64},{64,128},{128,192},{192,256},{256,320},{320,384},{384,448},... | collective-permute-start | bytes 786440 | tf_op jit(solution)/shard_map/while/body/eval_jaxpr/ppermute | solution.py:20
  153.7 4.4 %collective-permute-start = (bf16[2,4,128,128]{2,3,1,0:T(8,128)(2,1)S(1)}, bf16[2,4,128,128]{2,3,1,0:T(8,128)(2,1)S(1)}, u32[]{:S(2)}, u32[]{:S(2)}) collective-permute-start(bf16[2,4,128,128]{2,3,1,0:T(8,128)(2,1)S(1)} %copy.271), channel_id=1, source_target_pairs={{0,64},{64,128},{128,192},{192,256},{256,320},{320,384},{384,448},... | collective-permute-start | bytes 786440 | tf_op jit(solution)/shard_map/while/body/eval_jaxpr/ppermute | solution.py:20
  163.4 12.1 %collective-permute-start = (bf16[2,4,128,128]{2,3,1,0:T(8,128)(2,1)S(1)}, bf16[2,4,128,128]{2,3,1,0:T(8,128)(2,1)S(1)}, u32[]{:S(2)}, u32[]{:S(2)}) collective-permute-start(bf16[2,4,128,128]{2,3,1,0:T(8,128)(2,1)S(1)} %copy.271), channel_id=1, source_target_pairs={{0,64},{64,128},{128,192},{192,256},{256,320},{320,384},{384,448},... | collective-permute-start | bytes 786440 | tf_op jit(solution)/shard_map/while/body/eval_jaxpr/ppermute | solution.py:20
  181.7 110.0 %while.44 = (s32[]{:T(128)}, bf16[2,2,128,128]{3,2,0,1:T(8,128)(2,1)}, f32[2,2,128,128]{3,2,0,1:T(8,128)S(1)}, s32[]{:T(128)}, bf16[2,4,128,128]{3,2,0,1:T(8,128...) while((s32[]{:T(128)}, ...), condition=%wide.region_19.20_spmd.clone.clone, body=%wide.region_14.19_spmd.clone.clone.sunk | while | flops 807157760 | bytes 11665917 | solution.py:230
  184.7 5.0 %collective-permute-done.1 = bf16[2,2,128,128]{2,3,0,1:T(8,128)(2,1)S(1)} collective-permute-done((bf16[2,2,128,128]{2,3,0,1:T(8,128)(2,1)S(1)}, bf16[2,2,128,128]{2,3,0,1:T(8,128)(2,1)S(1)}, u32[]{:S(2)}, u32[]{:S(2)}) %collective-permute-start.1) | collective-permute-done | bytes 131104 | tf_op jit(solution)/shard_map/while/body/eval_jaxpr/ppermute | solution.py:20
  193.6 6.7 %collective-permute-done.1 = bf16[2,2,128,128]{2,3,0,1:T(8,128)(2,1)S(1)} collective-permute-done((bf16[2,2,128,128]{2,3,0,1:T(8,128)(2,1)S(1)}, bf16[2,2,128,128]{2,3,0,1:T(8,128)(2,1)S(1)}, u32[]{:S(2)}, u32[]{:S(2)}) %collective-permute-start.1) | collective-permute-done | bytes 131104 | tf_op jit(solution)/shard_map/while/body/eval_jaxpr/ppermute | solution.py:20
  204.1 5.0 %collective-permute-done.1 = bf16[2,2,128,128]{2,3,0,1:T(8,128)(2,1)S(1)} collective-permute-done((bf16[2,2,128,128]{2,3,0,1:T(8,128)(2,1)S(1)}, bf16[2,2,128,128]{2,3,0,1:T(8,128)(2,1)S(1)}, u32[]{:S(2)}, u32[]{:S(2)}) %collective-permute-start.1) | collective-permute-done | bytes 131104 | tf_op jit(solution)/shard_map/while/body/eval_jaxpr/ppermute | solution.py:20
  212.9 13.1 %collective-permute-done.1 = bf16[2,2,128,128]{2,3,0,1:T(8,128)(2,1)S(1)} collective-permute-done((bf16[2,2,128,128]{2,3,0,1:T(8,128)(2,1)S(1)}, bf16[2,2,128,128]{2,3,0,1:T(8,128)(2,1)S(1)}, u32[]{:S(2)}, u32[]{:S(2)}) %collective-permute-start.1) | collective-permute-done | bytes 131104 | tf_op jit(solution)/shard_map/while/body/eval_jaxpr/ppermute | solution.py:20
  229.9 5.0 %collective-permute-done.1 = bf16[2,2,128,128]{2,3,0,1:T(8,128)(2,1)S(1)} collective-permute-done((bf16[2,2,128,128]{2,3,0,1:T(8,128)(2,1)S(1)}, bf16[2,2,128,128]{2,3,0,1:T(8,128)(2,1)S(1)}, u32[]{:S(2)}, u32[]{:S(2)}) %collective-permute-start.1) | collective-permute-done | bytes 131104 | tf_op jit(solution)/shard_map/while/body/eval_jaxpr/ppermute | solution.py:20
  238.7 37.8 %collective-permute-done.1 = bf16[2,2,128,128]{2,3,0,1:T(8,128)(2,1)S(1)} collective-permute-done((bf16[2,2,128,128]{2,3,0,1:T(8,128)(2,1)S(1)}, bf16[2,2,128,128]{2,3,0,1:T(8,128)(2,1)S(1)}, u32[]{:S(2)}, u32[]{:S(2)}) %collective-permute-start.1) | collective-permute-done | bytes 131104 | tf_op jit(solution)/shard_map/while/body/eval_jaxpr/ppermute | solution.py:20
  276.5 7.1 %conditional.19 = (bf16[2,2,128,128]{3,2,0,1:T(8,128)(2,1)}, f32[2,2,128,128]{3,2,0,1:T(8,128)S(1)}) conditional(s32[]{:T(128)} %convert_element_type.303, (bf16[2,2,128,128]{2,3,0,1:T(8,128)(2,1)S(1)}, f32[2,2,128,128]{3,2,0,1:T(8,128)S(1)}) %tuple.246, (bf16[2,4,128,128]{3,2,0,1:T(8,128)(2,1)S(1)}, s32[]{:T(128)}, ...), branch_computations={%region_15.15_spmd, %region_16.18_spmd.clone} | conditional | flops 806928384 | bytes 10748102 | solution.py:220
  277.0 5.8 %conditional.15 = (f32[2,128,128]{2,1,0:T(8,128)S(1)}, f32[2,128,128]{2,1,0:T(8,128)S(1)}) conditional(s32[]{:T(128)} %convert_element_type.279, (bf16[2,2,128,128]{2,3,0,1:T(8,128)(2,1)S(1)}, f32[128,128]{1,0:T(8,128)S(1)}, f32[128,128]{1,0:T(8,128)S(1)}, f32[128,128]{1,0:T(8,128)S(1)}, f32[128,128]{1,0:T(8,128)S(1)}, ...), branch_computations={%region_17.16_spmd, %region_18.17_spmd} | conditional | flops 806109184 | bytes 7208976 | solution.py:204
  286.6 4.3 %collective-permute-done.1 = bf16[2,2,128,128]{2,3,0,1:T(8,128)(2,1)S(1)} collective-permute-done((bf16[2,2,128,128]{2,3,0,1:T(8,128)(2,1)S(1)}, bf16[2,2,128,128]{2,3,0,1:T(8,128)(2,1)S(1)}, u32[]{:S(2)}, u32[]{:S(2)}) %collective-permute-start.1) | collective-permute-done | bytes 131104 | tf_op jit(solution)/shard_map/while/body/eval_jaxpr/ppermute | solution.py:20
  299.9 7.6 %collective-permute-start.7 = (f32[2,128,256]{2,1,0:T(8,128)S(1)}, f32[2,128,256]{2,1,0:T(8,128)S(1)}, u32[]{:S(2)}, u32[]{:S(2)}) collective-permute-start(f32[2,128,256]{2,1,0:T(8,128)S(1)} %get-tuple-element.1531), channel_id=1, source_target_pairs={{2,0},{3,1},{4,2},{5,3},{6,4},{7,5},{8,6},{9,7},{10,8},{11,9},{12,... | collective-permute-start | bytes 786440 | tf_op jit(solution)/shard_map/ppermute | solution.py:14
  307.5 3.7 %collective-permute-start.8 = (f32[2,128,256]{2,1,0:T(8,128)S(1)}, f32[2,128,256]{2,1,0:T(8,128)S(1)}, u32[]{:S(2)}, u32[]{:S(2)}) collective-permute-start(f32[2,128,256]{2,1,0:T(8,128)S(1)} %get-tuple-element.1535), channel_id=1, source_target_pairs={{1,0},{2,1},{3,2},{4,3},{5,4},{6,5},{7,6},{8,7},{9,8},{10,9},{11,1... | collective-permute-start | bytes 786440 | tf_op jit(solution)/shard_map/ppermute | solution.py:14
  313.1 15.4 %collective-permute-done.11 = f32[2,128,256]{2,1,0:T(8,128)S(1)} collective-permute-done((f32[2,128,256]{2,1,0:T(8,128)S(1)}, f32[2,128,256]{2,1,0:T(8,128)S(1)}, u32[]{:S(2)}, u32[]{:S(2)}) %collective-permute-start.11) | collective-permute-done | bytes 262176 | tf_op jit(solution)/shard_map/ppermute | solution.py:14
  328.5 6.9 %collective-permute-done.9 = f32[2,128,256]{2,1,0:T(8,128)S(1)} collective-permute-done((f32[2,128,256]{2,1,0:T(8,128)S(1)}, f32[2,128,256]{2,1,0:T(8,128)S(1)}, u32[]{:S(2)}, u32[]{:S(2)}) %collective-permute-start.9) | collective-permute-done | bytes 262176 | tf_op jit(solution)/shard_map/ppermute | solution.py:14
  (183 shorter events, 114.3 us)
Async XLA Ops:
  2.4 40.9 %collective-permute-start.2 = (bf16[4,128,256]{2,0,1:T(4,128)(2,1)S(1)}, bf16[4,128,256]{2,0,1:T(4,128)(2,1)S(1)}, u32[]{:S(2)}, u32[]{:S(2)}) collective-permute-start(bf16[4,128,256]{2,0,1:T(4,128)(2,1)S(1)} %maximum_bitcast_fusion), channel_id=1, source_target_pairs={{62,0},{63,1},{0,2},{1,3},{2,4},{3,5},{4,6},{5,7},{6,8},{7,9},{8,1... | collective-permute-start | bytes 786440 | tf_op jit(solution)/shard_map/ppermute | solution.py:14
  8.1 35.3 %collective-permute-start.3 = (bf16[4,128,256]{2,0,1:T(4,128)(2,1)S(1)}, bf16[4,128,256]{2,0,1:T(4,128)(2,1)S(1)}, u32[]{:S(2)}, u32[]{:S(2)}) collective-permute-start(bf16[4,128,256]{2,0,1:T(4,128)(2,1)S(1)} %maximum_bitcast_fusion), channel_id=1, source_target_pairs={{63,0},{0,1},{1,2},{2,3},{3,4},{4,5},{5,6},{6,7},{7,8},{8,9},{9,10... | collective-permute-start | bytes 786440 | tf_op jit(solution)/shard_map/ppermute | solution.py:14
  11.7 32.1 %collective-permute-start.4 = (bf16[4,128,256]{2,0,1:T(4,128)(2,1)S(1)}, bf16[4,128,256]{2,0,1:T(4,128)(2,1)S(1)}, u32[]{:S(2)}, u32[]{:S(2)}) collective-permute-start(bf16[4,128,256]{2,0,1:T(4,128)(2,1)S(1)} %maximum_bitcast_fusion), channel_id=1, source_target_pairs={{1,0},{2,1},{3,2},{4,3},{5,4},{6,5},{7,6},{8,7},{9,8},{10,9},{11,1... | collective-permute-start | bytes 786440 | tf_op jit(solution)/shard_map/ppermute | solution.py:14
  20.6 23.3 %collective-permute-start.5 = (bf16[4,128,256]{2,0,1:T(4,128)(2,1)S(1)}, bf16[4,128,256]{2,0,1:T(4,128)(2,1)S(1)}, u32[]{:S(2)}, u32[]{:S(2)}) collective-permute-start(bf16[4,128,256]{2,0,1:T(4,128)(2,1)S(1)} %maximum_bitcast_fusion), channel_id=1, source_target_pairs={{2,0},{3,1},{4,2},{5,3},{6,4},{7,5},{8,6},{9,7},{10,8},{11,9},{12,... | collective-permute-start | bytes 786440 | tf_op jit(solution)/shard_map/ppermute | solution.py:14
  37.8 21.7 %collective-permute-start.6 = (bf16[4,128,256]{2,0,1:T(4,128)(2,1)S(1)}, bf16[4,128,256]{2,0,1:T(4,128)(2,1)S(1)}, u32[]{:S(2)}, u32[]{:S(2)}) collective-permute-start(bf16[4,128,256]{2,0,1:T(4,128)(2,1)S(1)} %maximum_bitcast_fusion), channel_id=1, source_target_pairs={{3,0},{4,1},{5,2},{6,3},{7,4},{8,5},{9,6},{10,7},{11,8},{12,9},{13... | collective-permute-start | bytes 786440 | tf_op jit(solution)/shard_map/ppermute | solution.py:14
  59.6 1.2 copy-start
  80.0 13.8 %collective-permute-start = (bf16[2,4,128,128]{2,3,1,0:T(8,128)(2,1)S(1)}, bf16[2,4,128,128]{2,3,1,0:T(8,128)(2,1)S(1)}, u32[]{:S(2)}, u32[]{:S(2)}) collective-permute-start(bf16[2,4,128,128]{2,3,1,0:T(8,128)(2,1)S(1)} %copy.271), channel_id=1, source_target_pairs={{0,64},{64,128},{128,192},{192,256},{256,320},{320,384},{384,448},... | collective-permute-start | bytes 786440 | tf_op jit(solution)/shard_map/while/body/eval_jaxpr/ppermute | solution.py:20
  105.9 5.2 %collective-permute-start = (bf16[2,4,128,128]{2,3,1,0:T(8,128)(2,1)S(1)}, bf16[2,4,128,128]{2,3,1,0:T(8,128)(2,1)S(1)}, u32[]{:S(2)}, u32[]{:S(2)}) collective-permute-start(bf16[2,4,128,128]{2,3,1,0:T(8,128)(2,1)S(1)} %copy.271), channel_id=1, source_target_pairs={{0,64},{64,128},{128,192},{192,256},{256,320},{320,384},{384,448},... | collective-permute-start | bytes 786440 | tf_op jit(solution)/shard_map/while/body/eval_jaxpr/ppermute | solution.py:20
  113.1 17.9 %collective-permute-start = (bf16[2,4,128,128]{2,3,1,0:T(8,128)(2,1)S(1)}, bf16[2,4,128,128]{2,3,1,0:T(8,128)(2,1)S(1)}, u32[]{:S(2)}, u32[]{:S(2)}) collective-permute-start(bf16[2,4,128,128]{2,3,1,0:T(8,128)(2,1)S(1)} %copy.271), channel_id=1, source_target_pairs={{0,64},{64,128},{128,192},{192,256},{256,320},{320,384},{384,448},... | collective-permute-start | bytes 786440 | tf_op jit(solution)/shard_map/while/body/eval_jaxpr/ppermute | solution.py:20
  133.0 7.7 %collective-permute-start = (bf16[2,4,128,128]{2,3,1,0:T(8,128)(2,1)S(1)}, bf16[2,4,128,128]{2,3,1,0:T(8,128)(2,1)S(1)}, u32[]{:S(2)}, u32[]{:S(2)}) collective-permute-start(bf16[2,4,128,128]{2,3,1,0:T(8,128)(2,1)S(1)} %copy.271), channel_id=1, source_target_pairs={{0,64},{64,128},{128,192},{192,256},{256,320},{320,384},{384,448},... | collective-permute-start | bytes 786440 | tf_op jit(solution)/shard_map/while/body/eval_jaxpr/ppermute | solution.py:20
  142.7 9.0 %collective-permute-start = (bf16[2,4,128,128]{2,3,1,0:T(8,128)(2,1)S(1)}, bf16[2,4,128,128]{2,3,1,0:T(8,128)(2,1)S(1)}, u32[]{:S(2)}, u32[]{:S(2)}) collective-permute-start(bf16[2,4,128,128]{2,3,1,0:T(8,128)(2,1)S(1)} %copy.271), channel_id=1, source_target_pairs={{0,64},{64,128},{128,192},{192,256},{256,320},{320,384},{384,448},... | collective-permute-start | bytes 786440 | tf_op jit(solution)/shard_map/while/body/eval_jaxpr/ppermute | solution.py:20
  153.7 7.7 %collective-permute-start = (bf16[2,4,128,128]{2,3,1,0:T(8,128)(2,1)S(1)}, bf16[2,4,128,128]{2,3,1,0:T(8,128)(2,1)S(1)}, u32[]{:S(2)}, u32[]{:S(2)}) collective-permute-start(bf16[2,4,128,128]{2,3,1,0:T(8,128)(2,1)S(1)} %copy.271), channel_id=1, source_target_pairs={{0,64},{64,128},{128,192},{192,256},{256,320},{320,384},{384,448},... | collective-permute-start | bytes 786440 | tf_op jit(solution)/shard_map/while/body/eval_jaxpr/ppermute | solution.py:20
  163.4 15.4 %collective-permute-start = (bf16[2,4,128,128]{2,3,1,0:T(8,128)(2,1)S(1)}, bf16[2,4,128,128]{2,3,1,0:T(8,128)(2,1)S(1)}, u32[]{:S(2)}, u32[]{:S(2)}) collective-permute-start(bf16[2,4,128,128]{2,3,1,0:T(8,128)(2,1)S(1)} %copy.271), channel_id=1, source_target_pairs={{0,64},{64,128},{128,192},{192,256},{256,320},{320,384},{384,448},... | collective-permute-start | bytes 786440 | tf_op jit(solution)/shard_map/while/body/eval_jaxpr/ppermute | solution.py:20
  182.7 7.0 %collective-permute-start.1 = (bf16[2,2,128,128]{2,3,0,1:T(8,128)(2,1)S(1)}, bf16[2,2,128,128]{2,3,0,1:T(8,128)(2,1)S(1)}, u32[]{:S(2)}, u32[]{:S(2)}) collective-permute-start(bf16[2,2,128,128]{2,3,0,1:T(8,128)(2,1)S(1)} %copy.272), channel_id=1, source_target_pairs={{64,0},{128,64},{192,128},{256,192},{320,256},{384,320},{448,384},... | collective-permute-start | bytes 393224 | tf_op jit(solution)/shard_map/while/body/eval_jaxpr/ppermute | solution.py:20
  191.6 8.7 %collective-permute-start.1 = (bf16[2,2,128,128]{2,3,0,1:T(8,128)(2,1)S(1)}, bf16[2,2,128,128]{2,3,0,1:T(8,128)(2,1)S(1)}, u32[]{:S(2)}, u32[]{:S(2)}) collective-permute-start(bf16[2,2,128,128]{2,3,0,1:T(8,128)(2,1)S(1)} %copy.272), channel_id=1, source_target_pairs={{64,0},{128,64},{192,128},{256,192},{320,256},{384,320},{448,384},... | collective-permute-start | bytes 393224 | tf_op jit(solution)/shard_map/while/body/eval_jaxpr/ppermute | solution.py:20
  202.1 7.0 %collective-permute-start.1 = (bf16[2,2,128,128]{2,3,0,1:T(8,128)(2,1)S(1)}, bf16[2,2,128,128]{2,3,0,1:T(8,128)(2,1)S(1)}, u32[]{:S(2)}, u32[]{:S(2)}) collective-permute-start(bf16[2,2,128,128]{2,3,0,1:T(8,128)(2,1)S(1)} %copy.272), channel_id=1, source_target_pairs={{64,0},{128,64},{192,128},{256,192},{320,256},{384,320},{448,384},... | collective-permute-start | bytes 393224 | tf_op jit(solution)/shard_map/while/body/eval_jaxpr/ppermute | solution.py:20
  210.9 15.1 %collective-permute-start.1 = (bf16[2,2,128,128]{2,3,0,1:T(8,128)(2,1)S(1)}, bf16[2,2,128,128]{2,3,0,1:T(8,128)(2,1)S(1)}, u32[]{:S(2)}, u32[]{:S(2)}) collective-permute-start(bf16[2,2,128,128]{2,3,0,1:T(8,128)(2,1)S(1)} %copy.272), channel_id=1, source_target_pairs={{64,0},{128,64},{192,128},{256,192},{320,256},{384,320},{448,384},... | collective-permute-start | bytes 393224 | tf_op jit(solution)/shard_map/while/body/eval_jaxpr/ppermute | solution.py:20
  227.9 7.0 %collective-permute-start.1 = (bf16[2,2,128,128]{2,3,0,1:T(8,128)(2,1)S(1)}, bf16[2,2,128,128]{2,3,0,1:T(8,128)(2,1)S(1)}, u32[]{:S(2)}, u32[]{:S(2)}) collective-permute-start(bf16[2,2,128,128]{2,3,0,1:T(8,128)(2,1)S(1)} %copy.272), channel_id=1, source_target_pairs={{64,0},{128,64},{192,128},{256,192},{320,256},{384,320},{448,384},... | collective-permute-start | bytes 393224 | tf_op jit(solution)/shard_map/while/body/eval_jaxpr/ppermute | solution.py:20
  236.7 39.8 %collective-permute-start.1 = (bf16[2,2,128,128]{2,3,0,1:T(8,128)(2,1)S(1)}, bf16[2,2,128,128]{2,3,0,1:T(8,128)(2,1)S(1)}, u32[]{:S(2)}, u32[]{:S(2)}) collective-permute-start(bf16[2,2,128,128]{2,3,0,1:T(8,128)(2,1)S(1)} %copy.272), channel_id=1, source_target_pairs={{64,0},{128,64},{192,128},{256,192},{320,256},{384,320},{448,384},... | collective-permute-start | bytes 393224 | tf_op jit(solution)/shard_map/while/body/eval_jaxpr/ppermute | solution.py:20
  284.6 6.3 %collective-permute-start.1 = (bf16[2,2,128,128]{2,3,0,1:T(8,128)(2,1)S(1)}, bf16[2,2,128,128]{2,3,0,1:T(8,128)(2,1)S(1)}, u32[]{:S(2)}, u32[]{:S(2)}) collective-permute-start(bf16[2,2,128,128]{2,3,0,1:T(8,128)(2,1)S(1)} %copy.272), channel_id=1, source_target_pairs={{64,0},{128,64},{192,128},{256,192},{320,256},{384,320},{448,384},... | collective-permute-start | bytes 393224 | tf_op jit(solution)/shard_map/while/body/eval_jaxpr/ppermute | solution.py:20
  296.0 17.1 %collective-permute-start.10 = (f32[2,128,256]{2,1,0:T(8,128)S(1)}, f32[2,128,256]{2,1,0:T(8,128)S(1)}, u32[]{:S(2)}, u32[]{:S(2)}) collective-permute-start(f32[2,128,256]{2,1,0:T(8,128)S(1)} %get-tuple-element.1533), channel_id=1, source_target_pairs={{62,0},{63,1},{0,2},{1,3},{2,4},{3,5},{4,6},{5,7},{6,8},{7,9},{8,1... | collective-permute-start | bytes 786440 | tf_op jit(solution)/shard_map/ppermute | solution.py:14
  298.0 30.6 %collective-permute-start.11 = (f32[2,128,256]{2,1,0:T(8,128)S(1)}, f32[2,128,256]{2,1,0:T(8,128)S(1)}, u32[]{:S(2)}, u32[]{:S(2)}) collective-permute-start(f32[2,128,256]{2,1,0:T(8,128)S(1)} %get-tuple-element.1532), channel_id=1, source_target_pairs={{61,0},{62,1},{63,2},{0,3},{1,4},{2,5},{3,6},{4,7},{5,8},{6,9},{7,... | collective-permute-start | bytes 786440 | tf_op jit(solution)/shard_map/ppermute | solution.py:14
  299.9 28.6 %collective-permute-start.7 = (f32[2,128,256]{2,1,0:T(8,128)S(1)}, f32[2,128,256]{2,1,0:T(8,128)S(1)}, u32[]{:S(2)}, u32[]{:S(2)}) collective-permute-start(f32[2,128,256]{2,1,0:T(8,128)S(1)} %get-tuple-element.1531), channel_id=1, source_target_pairs={{2,0},{3,1},{4,2},{5,3},{6,4},{7,5},{8,6},{9,7},{10,8},{11,9},{12,... | collective-permute-start | bytes 786440 | tf_op jit(solution)/shard_map/ppermute | solution.py:14
  307.5 21.1 %collective-permute-start.8 = (f32[2,128,256]{2,1,0:T(8,128)S(1)}, f32[2,128,256]{2,1,0:T(8,128)S(1)}, u32[]{:S(2)}, u32[]{:S(2)}) collective-permute-start(f32[2,128,256]{2,1,0:T(8,128)S(1)} %get-tuple-element.1535), channel_id=1, source_target_pairs={{1,0},{2,1},{3,2},{4,3},{5,4},{6,5},{7,6},{8,7},{9,8},{10,9},{11,1... | collective-permute-start | bytes 786440 | tf_op jit(solution)/shard_map/ppermute | solution.py:14
  311.1 24.3 %collective-permute-start.9 = (f32[2,128,256]{2,1,0:T(8,128)S(1)}, f32[2,128,256]{2,1,0:T(8,128)S(1)}, u32[]{:S(2)}, u32[]{:S(2)}) collective-permute-start(f32[2,128,256]{2,1,0:T(8,128)S(1)} %get-tuple-element.1534), channel_id=1, source_target_pairs={{63,0},{0,1},{1,2},{2,3},{3,4},{4,5},{5,6},{6,7},{7,8},{8,9},{9,10... | collective-permute-start | bytes 786440 | tf_op jit(solution)/shard_map/ppermute | solution.py:14
where the time goes:
time: 342 us; the launch traced here: 336 us
  waiting for transfers between devices  143 us (42%)
  starting transfers between devices  107 us (31%)
  local copies, waits for them, and re-layouts  45.4 us (13%)
  matrix products  14.3 us (4%)
  loops' own time  12.5 us (4%)
  between operations  7.86 us (2%)
  other arithmetic  6.85 us (2%)
    ppermute x14, waiting for transfers between devices, from_behind(): lax.ppermute(value, axis, [(source, source + steps) for source in range(f...  105 us
    ppermute x14, starting transfers between devices, from_behind(): lax.ppermute(value, axis, [(source, source + steps) for source in range(f...  61.6 us
    ppermute x10, starting transfers between devices, passed_along(): return lax.ppermute(block, axis, route)  45 us
    ppermute x10, waiting for transfers between devices, passed_along(): return lax.ppermute(block, axis, route)  37.8 us
    while x14, local copies, waits for them, and re-layouts  15 us
    another operation x34, local copies, waits for them, and re-layouts  12.8 us
    another operation x8, loops' own time, forward_section(): lax.cond(active, forward_active_work, forward_pass_through, (received, sa...  11.6 us
    dot_general x16, matrix products, right_apply(): jnp.einsum('...jk,kl->...jl', values, matrix, precision=lax.Precision.HIG...  7.82 us
  transfers between devices with their start and end apart: 24, of which 17 were waited for; matrix products, arithmetic and copies ran while one was open for 2% of the time, Pallas kernels for 0%

commit v1 on v0

v1 whole, which is shorter than its diff:
```python
import functools
import math

import jax
import jax.numpy as jnp
import ml_dtypes
import numpy as np
from jax import lax
from jax.experimental import pallas as pl
from jax.experimental.pallas import tpu as pltpu
from jax.sharding import PartitionSpec as P

REACH = 2
STRETCH = 1.6236604965019064
BF16 = jnp.bfloat16
F32 = jnp.float32


def transform_tables(size):
    index_line = np.arange(size)
    angle = (index_line[:, None] * index_line[None, :] % size) * (2.0 * math.pi / size)
    cosine, sine = np.cos(angle), np.sin(angle)
    kept_cos = (STRETCH * cosine).astype(ml_dtypes.bfloat16).astype(np.float64)
    kept_sin = (STRETCH * sine).astype(ml_dtypes.bfloat16).astype(np.float64)
    unit = np.sum(kept_cos * cosine + kept_sin * sine) / np.sum(cosine**2 + sine**2)
    unit = unit * math.sqrt(size)
    plus = np.block([[kept_cos, kept_sin], [-kept_sin, kept_cos]])
    minus = np.block([[kept_cos, -kept_sin], [kept_sin, kept_cos]])
    return plus.astype(ml_dtypes.bfloat16), minus.astype(ml_dtypes.bfloat16), unit


def dot(left, right):
    return jnp.dot(left, right, preferred_element_type=F32)


def row_hot(start, rows, columns):
    row_index = lax.broadcasted_iota(jnp.int32, (rows, columns), 0)
    col_index = lax.broadcasted_iota(jnp.int32, (rows, columns), 1)
    return jnp.where(col_index == row_index + start, 1.0, 0.0).astype(BF16)


def col_hot(start, rows, columns):
    row_index = lax.broadcasted_iota(jnp.int32, (rows, columns), 0)
    col_index = lax.broadcasted_iota(jnp.int32, (rows, columns), 1)
    return jnp.where(row_index == col_index + start, 1.0, 0.0).astype(BF16)


def cut_kernel(start_ref, above_ref, own_ref, below_ref, out_ref):
    slots, parts, size, _ = out_ref.shape
    rows, columns = own_ref.shape[1:]
    for slot in range(slots):
        pick_rows = row_hot(start_ref[0, slot], size, 3 * rows)
        pick_cols = col_hot(start_ref[1, slot], columns, size)
        for part in range(parts):
            picked = dot(pick_rows[:, :rows], above_ref[part])
            picked += dot(pick_rows[:, rows : 2 * rows], own_ref[part])
            picked += dot(pick_rows[:, 2 * rows :], below_ref[part])
            out_ref[slot, part] = dot(picked.astype(BF16), pick_cols).astype(BF16)


def chain_kernel(unit, window_ref, probe_ref, cos_ref, sin_ref, plus_ref, minus_ref, out_ref, wave_ref):
    slices = window_ref.shape[0]
    size = window_ref.shape[2]
    plus, minus = plus_ref[...], minus_ref[...]

    def swap(values, waves):
        blocks = [[values[i * size : (i + 1) * size, j * size : (j + 1) * size]
                   for j in range(values.shape[1] // size)] for i in range(values.shape[0] // size)]
        turned = [jnp.concatenate([row[j] for row in blocks], axis=1) for j in range(len(blocks[0]))]
        return jnp.concatenate(turned, axis=0) if len(turned) > 1 else turned[0]

    def forward(columns):
        half = dot(plus, columns.astype(BF16)).astype(BF16)
        return dot(swap(half, None), minus)

    def inverse(rows):
        half = dot(rows.astype(BF16), plus).astype(BF16)
        return dot(minus, swap(half, None))

    def kernel_times(rows, sign, scale):
        kernel_cos, kernel_sin = cos_ref[...] * scale, sin_ref[...] * (sign * scale)
        made = []
        for i in range(rows.shape[0] // size):
            re, im = rows[i * size : (i + 1) * size, :size], rows[i * size : (i + 1) * size, size:]
            made.append(jnp.concatenate(
                [re * kernel_cos - im * kernel_sin, re * kernel_sin + im * kernel_cos], axis=1))
        return jnp.concatenate(made, axis=0) if len(made) > 1 else made[0]

    psi_re, psi_im = probe_ref[0].astype(F32), probe_ref[1].astype(F32)
    tan_re, tan_im = None, None
    far_scale = 1.0 / unit**2
    hop_scale = 1.0 / unit**4
    for layer in range(slices):
        wave_ref[layer, 0], wave_ref[layer, 1] = psi_re, psi_im
        obj_re, obj_im = window_ref[layer, 0].astype(F32), window_ref[layer, 1].astype(F32)
        dir_re, dir_im = window_ref[layer, 2].astype(F32), window_ref[layer, 3].astype(F32)
        exit_re = obj_re * psi_re - obj_im * psi_im
        exit_im = obj_re * psi_im + obj_im * psi_re
        delta_re = dir_re * psi_re - dir_im * psi_im
        delta_im = dir_re * psi_im + dir_im * psi_re
        if layer > 0:
            delta_re += obj_re * tan_re - obj_im * tan_im
            delta_im += obj_re * tan_im + obj_im * tan_re
        columns = jnp.concatenate([
            jnp.concatenate([exit_re, delta_re], axis=1),
            jnp.concatenate([exit_im, delta_im], axis=1)], axis=0)
        spectrum = forward(columns)
        if layer < slices - 1:
            waves = inverse(kernel_times(spectrum, 1.0, hop_scale))
            psi_re, tan_re = waves[:size, :size], waves[:size, size:]
            psi_im, tan_im = waves[size:, :size], waves[size:, size:]
        else:
            far = kernel_times(spectrum, 1.0, far_scale)
    far_re, far_im = far[:size, :size], far[:size, size:]
    weight = (4.0 / slices) * (far_re * far[size:, :size] + far_im * far[size:, size:])
    back = jnp.concatenate([weight * far_re, weight * far_im], axis=1)
    adjoint = inverse(kernel_times(back, -1.0, far_scale))
    for layer in range(slices - 1, -1, -1):
        adj_re, adj_im = adjoint[:size], adjoint[size:]
        psi_re, psi_im = wave_ref[layer, 0], wave_ref[layer, 1]
        out_ref[layer, 0] = (psi_re * adj_re + psi_im * adj_im).astype(BF16)
        out_ref[layer, 1] = (psi_re * adj_im - psi_im * adj_re).astype(BF16)
        if layer > 0:
            obj_re, obj_im = window_ref[layer, 0].astype(F32), window_ref[layer, 1].astype(F32)
            columns = jnp.concatenate(
                [obj_re * adj_re + obj_im * adj_im, obj_re * adj_im - obj_im * adj_re], axis=0)
            adjoint = inverse(kernel_times(forward(columns), -1.0, hop_scale))


def gather_kernel(start_ref, grad_ref, above_ref, own_ref, below_ref):
    slots, parts, size, _ = grad_ref.shape
    rows, columns = own_ref.shape[1:]
    placed = [[], []]
    hots = []
    for slot in range(slots):
        pick_cols = row_hot(start_ref[1, slot], size, columns)
        hots.append(col_hot(start_ref[0, slot], 3 * rows, size))
        for part in range(parts):
            placed[part].append(dot(grad_ref[slot, part], pick_cols).astype(BF16))
    pick_rows = jnp.concatenate(hots, axis=1)
    for part in range(parts):
        total = dot(pick_rows, jnp.concatenate(placed[part], axis=0))
        above_ref[part] = total[:rows].astype(BF16)
        own_ref[part] = total[rows : 2 * rows]
        below_ref[part] = total[2 * rows :].astype(BF16)


def on_device(object_slices, direction, probe_wave, kernel_phase, corner_row, corner_col):
    strip_rows = object_slices.shape[2]
    column_count = object_slices.shape[3]
    patch_size = probe_wave.shape[1]
    slot_count = corner_row.shape[0]
    strip_count = lax.axis_size("strip")
    cuts_count = lax.axis_size("cuts")
    strip_index = lax.axis_index("strip")
    plus, minus, unit = transform_tables(patch_size)

    def shifted(block, distance):
        route = [((i - distance) % strip_count, i) for i in range(strip_count)]
        return lax.ppermute(block, "strip", route)

    vmem = pl.BlockSpec(memory_space=pltpu.VMEM)
    smem = pl.BlockSpec(memory_space=pltpu.SMEM)
    params = pltpu.CompilerParams(vmem_limit_bytes=32 * 1024 * 1024)

    corners = jnp.stack([corner_row, corner_col])
    near = [corners if k == 0 else shifted(corners, -k) for k in range(-REACH, REACH)]
    corners = jnp.concatenate(near, axis=1)
    owner_offset = jnp.asarray(np.repeat(np.arange(-REACH, REACH), slot_count), jnp.int32)
    corner_strip = corners[0] // strip_rows
    behind = (strip_index + owner_offset - corner_strip + REACH) % strip_count - REACH
    place = owner_offset - behind + jnp.clip(behind, 0, 1)
    first_row = (corners[0] - (strip_index - 1) * strip_rows) % (strip_count * strip_rows)
    first_row = jnp.where(place == 0, first_row, 4 * strip_rows)
    start = jnp.stack([first_row, corners[1]])

    stacked = jnp.concatenate([object_slices[0], direction[0]], axis=0)
    above, below = shifted(stacked, 1), shifted(stacked, -1)
    windows = pl.pallas_call(
        cut_kernel,
        out_shape=jax.ShapeDtypeStruct((cuts_count, 4, patch_size, patch_size), BF16),
        in_specs=[smem, vmem, vmem, vmem],
        out_specs=vmem,
        compiler_params=params,
        name="cut_windows",
    )(start, above, stacked, below)
    windows = lax.all_to_all(windows, "cuts", 0, 0, tiled=False)
    gradient = pl.pallas_call(
        functools.partial(chain_kernel, unit),
        out_shape=jax.ShapeDtypeStruct((cuts_count, 2, patch_size, patch_size), BF16),
        in_specs=[vmem] * 6,
        out_specs=vmem,
        scratch_shapes=[pltpu.VMEM((cuts_count, 2, patch_size, patch_size), F32)],
        compiler_params=params,
        name="wave_chain",
    )(windows, probe_wave, jnp.cos(kernel_phase), jnp.sin(kernel_phase), jnp.asarray(plus), jnp.asarray(minus))
    gradient = lax.all_to_all(gradient, "cuts", 0, 0, tiled=False)
    strip_shape = (2, strip_rows, column_count)
    to_above, own, to_below = pl.pallas_call(
        gather_kernel,
        out_shape=(
            jax.ShapeDtypeStruct(strip_shape, BF16),
            jax.ShapeDtypeStruct(strip_shape, F32),
            jax.ShapeDtypeStruct(strip_shape, BF16),
        ),
        in_specs=[smem, vmem],
        out_specs=(vmem, vmem, vmem),
        compiler_params=params,
        name="add_windows",
    )(start, gradient)
    from_below = shifted(to_above, -1).astype(F32)
    from_above = shifted(to_below, 1).astype(F32)
    return (own + from_below + from_above)[None]


def solution(mesh):
    in_specs = (
        P("cuts", None, "strip", None),
        P("cuts", None, "strip", None),
        P(),
        P(),
        P("strip"),
        P("strip"),
    )
    out_specs = P("cuts", None, "strip", None)
    return jax.shard_map(
        on_device, mesh=mesh, in_specs=in_specs, out_specs=out_specs, check_vma=False
    )
```

time: 342 us -> 105 us (0.31); the launches traced: 336 us -> 104 us
  waiting for transfers between devices: 143 us -> 25.5 us
  starting transfers between devices: 107 us -> 42.8 us
  local copies, waits for them, and re-layouts: 45.4 us -> 1.58 us
  Pallas kernels: 0 us -> 20 us
  matrix products: 14.3 us -> 0 us
  blocking collectives: 0 us -> 12.6 us
  loops' own time: 12.5 us -> 0 us
  between operations: 7.86 us -> 0.14 us
  other arithmetic: 6.85 us -> 1.86 us
    ppermute x24 -> x7, waiting for transfers between devices: 143 us -> 10.6 us  [shifted(): return lax.ppermute(block, 'strip', route)]
    ppermute x24 -> x7, starting transfers between devices: 107 us -> 36.2 us  [shifted(): return lax.ppermute(block, 'strip', route)]
    pallas_call x0 -> x3, Pallas kernels: none -> 20 us  [the longest x1 9.85 us: on_device(): pl.pallas_call(functools.partial(chain_kernel, unit), out_shape=jax.Shape...]
    while x14 -> x0, local copies, waits for them, and re-layouts: 15 us -> none
    all_to_all x0 -> x1, waiting for transfers between devices: none -> 14.8 us  [on_device(): windows = lax.all_to_all(windows, 'cuts', 0, 0, tiled=False)]
    dot_general x32 -> x0, matrix products: 14.3 us -> none  [the longest x16 7.82 us: right_apply(): jnp.einsum('...jk,kl->...jl', values, matrix, precision=lax.Precision.HIG...]
    another operation x34 -> x0, local copies, waits for them, and re-layouts: 12.8 us -> none
    all_to_all x0 -> x1, blocking collectives: none -> 12.6 us  [on_device(): gradient = lax.all_to_all(gradient, 'cuts', 0, 0, tiled=False)]
  transfers between devices with their start and end apart: 24 -> 8, of which waited for: 17 -> 4; matrix products, arithmetic and copies ran while one was open for 2% -> 1% of each run, Pallas kernels for 0% -> 0%
where the time goes in v1:
time: 105 us; the launch traced here: 104 us
  starting transfers between devices  42.8 us (41%)
  waiting for transfers between devices  25.5 us (24%)
  Pallas kernels  20 us (19%)
  blocking collectives  12.6 us (12%)
  other arithmetic  1.86 us (2%)
  local copies, waits for them, and re-layouts  1.58 us (2%)
    ppermute x7, starting transfers between devices, shifted(): return lax.ppermute(block, 'strip', route)  36.2 us
    all_to_all x1, waiting for transfers between devices, on_device(): windows = lax.all_to_all(windows, 'cuts', 0, 0, tiled=False)  14.8 us
    all_to_all x1, blocking collectives, on_device(): gradient = lax.all_to_all(gradient, 'cuts', 0, 0, tiled=False)  12.6 us
    ppermute x7, waiting for transfers between devices, shifted(): return lax.ppermute(block, 'strip', route)  10.6 us
    pallas_call x1, Pallas kernels, on_device(): pl.pallas_call(functools.partial(chain_kernel, unit), out_shape=jax.Shape...  9.85 us
    pallas_call x1, Pallas kernels, on_device(): pl.pallas_call(cut_kernel, out_shape=jax.ShapeDtypeStruct((cuts_count, 4,...  8.74 us
    all_to_all x1, starting transfers between devices, on_device(): windows = lax.all_to_all(windows, 'cuts', 0, 0, tiled=False)  6.59 us
  transfers between devices with their start and end apart: 8, of which 4 were waited for; matrix products, arithmetic and copies ran while one was open for 1% of the time, Pallas kernels for 0%

profile of v1, /device:TPU:1, one launch (start us, length us, event | category | flops | bytes accessed | tf_op | source)
XLA Modules:
  0.0 104.4 jit_solution(3314626738013682052)
XLA Ops:
  0.0 0.0 copy-start.4
  0.0 0.7 copy-done.4
  0.7 0.0 copy-done.5
  0.7 5.7 %collective-permute-start = (s32[2,2]{1,0:T(2,128)S(1)}, s32[2,2]{1,0:T(2,128)S(1)}, u32[]{:S(2)}, u32[]{:S(2)}) collective-permute-start(s32[2,2]{1,0:T(2,128)S(1)} %pad_add_fusion), channel_id=1, source_target_pairs={{62,0},{63,1},{0,2},{1,3},{2,4},{3,5},{4,6},{5,7},{6,8},{7,9},{8,1... | collective-permute-start | bytes 56 | tf_op jit(solution)/shard_map/ppermute | solution.py:160
  6.4 3.5 %collective-permute-start.1 = (s32[2,2]{1,0:T(2,128)S(1)}, s32[2,2]{1,0:T(2,128)S(1)}, u32[]{:S(2)}, u32[]{:S(2)}) collective-permute-start(s32[2,2]{1,0:T(2,128)S(1)} %pad_add_fusion), channel_id=1, source_target_pairs={{63,0},{0,1},{1,2},{2,3},{3,4},{4,5},{5,6},{6,7},{7,8},{8,9},{9,10... | collective-permute-start | bytes 56 | tf_op jit(solution)/shard_map/ppermute | solution.py:160
  10.0 9.0 %collective-permute-start.2 = (s32[2,2]{1,0:T(2,128)S(1)}, s32[2,2]{1,0:T(2,128)S(1)}, u32[]{:S(2)}, u32[]{:S(2)}) collective-permute-start(s32[2,2]{1,0:T(2,128)S(1)} %pad_add_fusion), channel_id=1, source_target_pairs={{1,0},{2,1},{3,2},{4,3},{5,4},{6,5},{7,6},{8,7},{9,8},{10,9},{11,1... | collective-permute-start | bytes 56 | tf_op jit(solution)/shard_map/ppermute | solution.py:160
  18.9 1.0 pad_maximum_fusion.own_ref
  19.9 1.9 %collective-permute-start.3 = (bf16[4,128,256]{2,1,0:T(8,128)(2,1)S(1)}, bf16[4,128,256]{2,1,0:T(8,128)(2,1)S(1)}, u32[]{:S(2)}, u32[]{:S(2)}) collective-permute-start(bf16[4,128,256]{2,1,0:T(8,128)(2,1)S(1)} %pad_maximum_fusion.own_ref), channel_id=1, source_target_pairs={{63,0},{0,1},{1,2},{2,3},{3,4},{4,5},{5,6},{6,7},{7,8},{8,9},{9,10... | collective-permute-start | bytes 786440 | tf_op jit(solution)/shard_map/ppermute | solution.py:160
  21.9 6.7 %collective-permute-start.4 = (bf16[4,128,256]{2,1,0:T(8,128)(2,1)S(1)}, bf16[4,128,256]{2,1,0:T(8,128)(2,1)S(1)}, u32[]{:S(2)}, u32[]{:S(2)}) collective-permute-start(bf16[4,128,256]{2,1,0:T(8,128)(2,1)S(1)} %pad_maximum_fusion.own_ref), channel_id=1, source_target_pairs={{1,0},{2,1},{3,2},{4,3},{5,4},{6,5},{7,6},{8,7},{9,8},{10,9},{11,1... | collective-permute-start | bytes 786440 | tf_op jit(solution)/shard_map/ppermute | solution.py:160
  28.6 0.0 collective-permute-done
  28.6 0.0 collective-permute-done.1
  28.6 0.0 collective-permute-done.2
  28.6 0.1 pad_add_fusion.1
  28.7 0.6 copy-done.6
  29.4 2.6 %collective-permute-done.3.above_ref = bf16[4,128,256]{2,1,0:T(8,128)(2,1)S(1)} collective-permute-done((bf16[4,128,256]{2,1,0:T(8,128)(2,1)S(1)}, bf16[4,128,256]{2,1,0:T(8,128)(2,1)S(1)}, u32[]{:S(2)}, u32[]{:S(2)}) %collective-permute-start.3) | collective-permute-done | bytes 262176 | tf_op jit(solution)/shard_map/ppermute | solution.py:160
  32.0 0.9 collective-permute-done.4.below_ref
  32.9 8.7 %cut_windows.1 = bf16[8,4,128,128]{3,2,1,0:T(8,128)(2,1)} custom-call(s32[2,8]{1,0:T(2,128)S(1)} %pad_add_fusion.2.start_ref, bf16[4,128,256]{2,1,0:T(8,128)(2,1)S(1)} %collective-permute-done.3.above_ref, bf16[4,128,256]{2,1,0:T(8,128)(2,1)S(1)} %pad_maximum_fusion.own_ref, bf16[4,128,256]{2,1,0:T(8,128)(2,1)S(1)} %collective-permute-done.4.below_ref), custom_call_target="tpu_custom_call" | custom-call | tf_op jit(solution)/shard_map/cut_windows/pallas_call | solution.py:179
  41.6 6.6 %all-to-all-start = ((bf16[8,4,128,128]{3,2,1,0:T(8,128)(2,1)}), bf16[8,4,128,128]{3,2,1,0:T(8,128)(2,1)S(1)}, u32[]{:S(2)}, u32[]{:S(2)}) async-start(bf16[8,4,128,128]{3,2,1,0:T(8,128)(2,1)} %cut_windows.1), calls=%async_computation | async-start | bytes 2097152 | tf_op jit(solution)/shard_map/all_to_all | solution.py:187
  48.2 0.0 copy-done.3
  48.2 0.2 fusion.4
  48.5 14.8 %all-to-all-done.window_ref = bf16[8,4,128,128]{3,2,1,0:T(8,128)(2,1)S(1)} async-done(((bf16[8,4,128,128]{3,2,1,0:T(8,128)(2,1)}), bf16[8,4,128,128]{3,2,1,0:T(8,128)(2,1)S(1)}, u32[]{:S(2)}, u32[]{:S(2)}) %all-to-all-start) | async-done | bytes 1048608 | tf_op jit(solution)/shard_map/all_to_all | solution.py:187
  63.3 0.0 copy-done.1
  63.3 0.0 copy-done
  63.3 0.0 copy-done.2
  63.3 9.8 %wave_chain.1 = bf16[8,2,128,128]{3,2,1,0:T(8,128)(2,1)S(1)} custom-call(bf16[8,4,128,128]{3,2,1,0:T(8,128)(2,1)S(1)} %all-to-all-done.window_ref, bf16[2,128,128]{2,1,0:T(8,128)(2,1)S(1)} %copy-done.2, f32[128,128]{1,0:T(8,128)S(1)} %get-tuple-element.12.cos_ref, f32[128,128]{1,0:T(8,128)S(1)} %get-tuple-element.11.sin_ref, bf16[256,256]{1,0:T(8,128)(2,1)S(1)} %copy-done, ...), custom_call_target="tpu_custom_call" | custom-call | tf_op jit(solution)/shard_map/wave_chain/pallas_call | solution.py:188
  73.2 12.6 %all_to_all.10.grad_ref = bf16[8,2,128,128]{3,2,1,0:T(8,128)(2,1)S(1)} all-to-all(bf16[8,2,128,128]{3,2,1,0:T(8,128)(2,1)S(1)} %wave_chain.1), channel_id=1, replica_groups=mesh['cuts'=8,'strip'=64] {'cuts'}, dimensions={0} | all-to-all | bytes 1048576 | tf_op jit(solution)/shard_map/all_to_all | solution.py:197
  85.8 1.4 %add_windows.1 = (bf16[2,128,256]{2,1,0:T(8,128)(2,1)S(1)}, f32[2,128,256]{2,1,0:T(8,128)S(1)}, bf16[2,128,256]{2,1,0:T(8,128)(2,1)S(1)}) custom-call(s32[2,8]{1,0:T(2,128)S(1)} %pad_add_fusion.2.start_ref, bf16[8,2,128,128]{3,2,1,0:T(8,128)(2,1)S(1)} %all_to_all.10.grad_ref), custom_call_target="tpu_custom_call" | custom-call | tf_op jit(solution)/shard_map/add_windows/pallas_call | solution.py:199
  87.2 7.4 %collective-permute-start.5 = (bf16[2,128,256]{2,1,0:T(8,128)(2,1)S(1)}, bf16[2,128,256]{2,1,0:T(8,128)(2,1)S(1)}, u32[]{:S(2)}, u32[]{:S(2)}) collective-permute-start(bf16[2,128,256]{2,1,0:T(8,128)(2,1)S(1)} %get-tuple-element.9), channel_id=1, source_target_pairs={{1,0},{2,1},{3,2},{4,3},{5,4},{6,5},{7,6},{8,7},{9,8},{10,9},{11,1... | collective-permute-start | bytes 393224 | tf_op jit(solution)/shard_map/ppermute | solution.py:160
  94.6 1.9 %collective-permute-start.6 = (bf16[2,128,256]{2,1,0:T(8,128)(2,1)S(1)}, bf16[2,128,256]{2,1,0:T(8,128)(2,1)S(1)}, u32[]{:S(2)}, u32[]{:S(2)}) collective-permute-start(bf16[2,128,256]{2,1,0:T(8,128)(2,1)S(1)} %get-tuple-element.10), channel_id=1, source_target_pairs={{63,0},{0,1},{1,2},{2,3},{3,4},{4,5},{5,6},{6,7},{7,8},{8,9},{9,10... | collective-permute-start | bytes 393224 | tf_op jit(solution)/shard_map/ppermute | solution.py:160
  96.6 0.0 collective-permute-done.5
  96.6 7.1 %collective-permute-done.6 = bf16[2,128,256]{2,1,0:T(8,128)(2,1)S(1)} collective-permute-done((bf16[2,128,256]{2,1,0:T(8,128)(2,1)S(1)}, bf16[2,128,256]{2,1,0:T(8,128)(2,1)S(1)}, u32[]{:S(2)}, u32[]{:S(2)}) %collective-permute-start.6) | collective-permute-done | bytes 131104 | tf_op jit(solution)/shard_map/ppermute | solution.py:160
  103.7 0.7 add_bitcast_fusion
  (10 shorter events, 0.1 us)
Async XLA Ops:
  0.0 0.7 copy-start.4
  0.0 0.7 copy-start.5
  0.7 27.9 %collective-permute-start = (s32[2,2]{1,0:T(2,128)S(1)}, s32[2,2]{1,0:T(2,128)S(1)}, u32[]{:S(2)}, u32[]{:S(2)}) collective-permute-start(s32[2,2]{1,0:T(2,128)S(1)} %pad_add_fusion), channel_id=1, source_target_pairs={{62,0},{63,1},{0,2},{1,3},{2,4},{3,5},{4,6},{5,7},{6,8},{7,9},{8,1... | collective-permute-start | bytes 56 | tf_op jit(solution)/shard_map/ppermute | solution.py:160
  6.4 22.2 %collective-permute-start.1 = (s32[2,2]{1,0:T(2,128)S(1)}, s32[2,2]{1,0:T(2,128)S(1)}, u32[]{:S(2)}, u32[]{:S(2)}) collective-permute-start(s32[2,2]{1,0:T(2,128)S(1)} %pad_add_fusion), channel_id=1, source_target_pairs={{63,0},{0,1},{1,2},{2,3},{3,4},{4,5},{5,6},{6,7},{7,8},{8,9},{9,10... | collective-permute-start | bytes 56 | tf_op jit(solution)/shard_map/ppermute | solution.py:160
  10.0 18.6 %collective-permute-start.2 = (s32[2,2]{1,0:T(2,128)S(1)}, s32[2,2]{1,0:T(2,128)S(1)}, u32[]{:S(2)}, u32[]{:S(2)}) collective-permute-start(s32[2,2]{1,0:T(2,128)S(1)} %pad_add_fusion), channel_id=1, source_target_pairs={{1,0},{2,1},{3,2},{4,3},{5,4},{6,5},{7,6},{8,7},{9,8},{10,9},{11,1... | collective-permute-start | bytes 56 | tf_op jit(solution)/shard_map/ppermute | solution.py:160
  19.9 12.1 %collective-permute-start.3 = (bf16[4,128,256]{2,1,0:T(8,128)(2,1)S(1)}, bf16[4,128,256]{2,1,0:T(8,128)(2,1)S(1)}, u32[]{:S(2)}, u32[]{:S(2)}) collective-permute-start(bf16[4,128,256]{2,1,0:T(8,128)(2,1)S(1)} %pad_maximum_fusion.own_ref), channel_id=1, source_target_pairs={{63,0},{0,1},{1,2},{2,3},{3,4},{4,5},{5,6},{6,7},{7,8},{8,9},{9,10... | collective-permute-start | bytes 786440 | tf_op jit(solution)/shard_map/ppermute | solution.py:160
  21.9 11.0 %collective-permute-start.4 = (bf16[4,128,256]{2,1,0:T(8,128)(2,1)S(1)}, bf16[4,128,256]{2,1,0:T(8,128)(2,1)S(1)}, u32[]{:S(2)}, u32[]{:S(2)}) collective-permute-start(bf16[4,128,256]{2,1,0:T(8,128)(2,1)S(1)} %pad_maximum_fusion.own_ref), channel_id=1, source_target_pairs={{1,0},{2,1},{3,2},{4,3},{5,4},{6,5},{7,6},{8,7},{9,8},{10,9},{11,1... | collective-permute-start | bytes 786440 | tf_op jit(solution)/shard_map/ppermute | solution.py:160
  28.7 0.7 copy-start.6
  41.6 6.6 %copy-start.3 = (f32[128,128]{1,0:T(8,128)S(1)}, f32[128,128]{1,0:T(8,128)}, u32[]{:S(2)}) copy-start(f32[128,128]{1,0:T(8,128)} %param.12) | copy-start | bytes 196612
  41.6 21.7 %copy-start.1 = (bf16[256,256]{1,0:T(8,128)(2,1)S(1)}, bf16[256,256]{1,0:T(8,128)(2,1)}, u32[]{:S(2)}) copy-start(bf16[256,256]{1,0:T(8,128)(2,1)} %constant.64.clone.minus_ref) | copy-start | bytes 393220
  41.6 21.7 %all-to-all-start = ((bf16[8,4,128,128]{3,2,1,0:T(8,128)(2,1)}), bf16[8,4,128,128]{3,2,1,0:T(8,128)(2,1)S(1)}, u32[]{:S(2)}, u32[]{:S(2)}) async-start(bf16[8,4,128,128]{3,2,1,0:T(8,128)(2,1)} %cut_windows.1), calls=%async_computation | async-start | bytes 2097152 | tf_op jit(solution)/shard_map/all_to_all | solution.py:187
  48.2 15.1 %copy-start = (bf16[256,256]{1,0:T(8,128)(2,1)S(1)}, bf16[256,256]{1,0:T(8,128)(2,1)}, u32[]{:S(2)}) copy-start(bf16[256,256]{1,0:T(8,128)(2,1)} %constant.63.clone.plus_ref) | copy-start | bytes 393220
  48.2 15.1 %copy-start.2 = (bf16[2,128,128]{2,1,0:T(8,128)(2,1)S(1)}, bf16[2,128,128]{2,1,0:T(8,128)(2,1)}, u32[]{:S(2)}) copy-start(bf16[2,128,128]{2,1,0:T(8,128)(2,1)} %probe_ref.1) | copy-start | bytes 196612
  87.2 9.4 %collective-permute-start.5 = (bf16[2,128,256]{2,1,0:T(8,128)(2,1)S(1)}, bf16[2,128,256]{2,1,0:T(8,128)(2,1)S(1)}, u32[]{:S(2)}, u32[]{:S(2)}) collective-permute-start(bf16[2,128,256]{2,1,0:T(8,128)(2,1)S(1)} %get-tuple-element.9), channel_id=1, source_target_pairs={{1,0},{2,1},{3,2},{4,3},{5,4},{6,5},{7,6},{8,7},{9,8},{10,9},{11,1... | collective-permute-start | bytes 393224 | tf_op jit(solution)/shard_map/ppermute | solution.py:160
  94.6 9.0 %collective-permute-start.6 = (bf16[2,128,256]{2,1,0:T(8,128)(2,1)S(1)}, bf16[2,128,256]{2,1,0:T(8,128)(2,1)S(1)}, u32[]{:S(2)}, u32[]{:S(2)}) collective-permute-start(bf16[2,128,256]{2,1,0:T(8,128)(2,1)S(1)} %get-tuple-element.10), channel_id=1, source_target_pairs={{63,0},{0,1},{1,2},{2,3},{3,4},{4,5},{5,6},{6,7},{7,8},{8,9},{9,10... | collective-permute-start | bytes 393224 | tf_op jit(solution)/shard_map/ppermute | solution.py:160

commit v2 on v1

--- a/solution.py
+++ b/solution.py
@@ -11,6 +11,7 @@
 from jax.sharding import PartitionSpec as P
 
 REACH = 2
+NOTE_ROWS = 16
 STRETCH = 1.6236604965019064
 BF16 = jnp.bfloat16
 F32 = jnp.float32
@@ -36,26 +37,42 @@
 def row_hot(start, rows, columns):
     row_index = lax.broadcasted_iota(jnp.int32, (rows, columns), 0)
     col_index = lax.broadcasted_iota(jnp.int32, (rows, columns), 1)
-    return jnp.where(col_index == row_index + start, 1.0, 0.0).astype(BF16)
+    return jnp.where((col_index - row_index).astype(F32) == start, 1.0, 0.0).astype(BF16)
 
 
 def col_hot(start, rows, columns):
     row_index = lax.broadcasted_iota(jnp.int32, (rows, columns), 0)
     col_index = lax.broadcasted_iota(jnp.int32, (rows, columns), 1)
-    return jnp.where(row_index == col_index + start, 1.0, 0.0).astype(BF16)
-
-
-def cut_kernel(start_ref, above_ref, own_ref, below_ref, out_ref):
+    return jnp.where((row_index - col_index).astype(F32) == start, 1.0, 0.0).astype(BF16)
+
+
+def cut_kernel(rows, far_ref, above_ref, own_ref, below_ref, out_ref, start_ref):
     slots, parts, size, _ = out_ref.shape
-    rows, columns = own_ref.shape[1:]
+    columns = own_ref.shape[1]
+    near = slots // 4
+    hots = []
+    for owner, note_ref in enumerate((far_ref, above_ref, own_ref, below_ref)):
+        note = note_ref[note_ref.shape[0] - NOTE_ROWS :, :].astype(F32)[0:1]
+        for position in range(near):
+            here = note[:, 2 * near + position : 2 * near + position + 1] == owner - REACH
+            first_row = jnp.where(here, note[:, position : position + 1], 4.0 * rows)
+            first_col = note[:, near + position : near + position + 1]
+            slot = owner * near + position
+            start_ref[2 * slot : 2 * slot + 1, :] = jnp.broadcast_to(first_row, (1, 128))
+            start_ref[2 * slot + 1 : 2 * slot + 2, :] = jnp.broadcast_to(first_col, (1, 128))
+            hots.append((row_hot(first_row, size, 3 * rows), col_hot(first_col, columns, size)))
+    bands = [
+        jnp.concatenate(
+            [ref[part * rows : (part + 1) * rows, :] for ref in (above_ref, own_ref, below_ref)], axis=0
+        )
+        for part in range(parts)
+    ]
+    pick_rows = jnp.concatenate([hot for hot, _ in hots], axis=0)
+    picked = [dot(pick_rows, band).astype(BF16) for band in bands]
     for slot in range(slots):
-        pick_rows = row_hot(start_ref[0, slot], size, 3 * rows)
-        pick_cols = col_hot(start_ref[1, slot], columns, size)
-        for part in range(parts):
-            picked = dot(pick_rows[:, :rows], above_ref[part])
-            picked += dot(pick_rows[:, rows : 2 * rows], own_ref[part])
-            picked += dot(pick_rows[:, 2 * rows :], below_ref[part])
-            out_ref[slot, part] = dot(picked.astype(BF16), pick_cols).astype(BF16)
+        lines = [part[slot * size : (slot + 1) * size] for part in picked]
+        window = dot(jnp.concatenate(lines, axis=0), hots[slot][1]).astype(BF16)
+        out_ref[slot] = window.reshape(parts, size, size)
 
 
 def chain_kernel(unit, window_ref, probe_ref, cos_ref, sin_ref, plus_ref, minus_ref, out_ref, wave_ref):
@@ -130,13 +147,16 @@
 def gather_kernel(start_ref, grad_ref, above_ref, own_ref, below_ref):
     slots, parts, size, _ = grad_ref.shape
     rows, columns = own_ref.shape[1:]
-    placed = [[], []]
+    placed = [[] for _ in range(parts)]
     hots = []
     for slot in range(slots):
-        pick_cols = row_hot(start_ref[1, slot], size, columns)
-        hots.append(col_hot(start_ref[0, slot], 3 * rows, size))
+        first_row = start_ref[2 * slot : 2 * slot + 1, 0:1]
+        first_col = start_ref[2 * slot + 1 : 2 * slot + 2, 0:1]
+        hots.append(col_hot(first_row, 3 * rows, size))
+        values = grad_ref[slot].reshape(parts * size, size)
+        spread = dot(values, row_hot(first_col, size, columns)).astype(BF16)
         for part in range(parts):
-            placed[part].append(dot(grad_ref[slot, part], pick_cols).astype(BF16))
+            placed[part].append(spread[part * size : (part + 1) * size])
     pick_rows = jnp.concatenate(hots, axis=1)
     for part in range(parts):
         total = dot(pick_rows, jnp.concatenate(placed[part], axis=0))
@@ -149,7 +169,6 @@
     strip_rows = object_slices.shape[2]
     column_count = object_slices.shape[3]
     patch_size = probe_wave.shape[1]
-    slot_count = corner_row.shape[0]
     strip_count = lax.axis_size("strip")
     cuts_count = lax.axis_size("cuts")
     strip_index = lax.axis_index("strip")
@@ -160,30 +179,35 @@
         return lax.ppermute(block, "strip", route)
 
     vmem = pl.BlockSpec(memory_space=pltpu.VMEM)
-    smem = pl.BlockSpec(memory_space=pltpu.SMEM)
     params = pltpu.CompilerParams(vmem_limit_bytes=32 * 1024 * 1024)
 
-    corners = jnp.stack([corner_row, corner_col])
-    near = [corners if k == 0 else shifted(corners, -k) for k in range(-REACH, REACH)]
-    corners = jnp.concatenate(near, axis=1)
-    owner_offset = jnp.asarray(np.repeat(np.arange(-REACH, REACH), slot_count), jnp.int32)
-    corner_strip = corners[0] // strip_rows
-    behind = (strip_index + owner_offset - corner_strip + REACH) % strip_count - REACH
-    place = owner_offset - behind + jnp.clip(behind, 0, 1)
-    first_row = (corners[0] - (strip_index - 1) * strip_rows) % (strip_count * strip_rows)
-    first_row = jnp.where(place == 0, first_row, 4 * strip_rows)
-    start = jnp.stack([first_row, corners[1]])
-
-    stacked = jnp.concatenate([object_slices[0], direction[0]], axis=0)
-    above, below = shifted(stacked, 1), shifted(stacked, -1)
-    windows = pl.pallas_call(
-        cut_kernel,
-        out_shape=jax.ShapeDtypeStruct((cuts_count, 4, patch_size, patch_size), BF16),
-        in_specs=[smem, vmem, vmem, vmem],
-        out_specs=vmem,
+    total_rows = strip_count * strip_rows
+    inside = (corner_row - (strip_index - REACH) * strip_rows) % total_rows - REACH * strip_rows
+    ahead = REACH - (inside + REACH * strip_rows) // strip_rows
+    to_owner = ahead - jnp.clip(ahead, 0, 1)
+    first_row = inside + (to_owner + 1) * strip_rows
+    note = jnp.concatenate([first_row, corner_col, to_owner]).astype(BF16)
+    note = jnp.pad(note[None], ((0, NOTE_ROWS - 1), (0, column_count - note.shape[0])))
+    block = jnp.concatenate(
+        [
+            object_slices.reshape(2 * strip_rows, column_count),
+            direction.reshape(2 * strip_rows, column_count),
+            note,
+        ],
+        axis=0,
+    )
+    above, below = shifted(block, 1), shifted(block, -1)
+    windows, start = pl.pallas_call(
+        functools.partial(cut_kernel, strip_rows),
+        out_shape=(
+            jax.ShapeDtypeStruct((cuts_count, 4, patch_size, patch_size), BF16),
+            jax.ShapeDtypeStruct((2 * cuts_count, 128), F32),
+        ),
+        in_specs=[vmem] * 4,
+        out_specs=(vmem, vmem),
         compiler_params=params,
         name="cut_windows",
-    )(start, above, stacked, below)
+    )(shifted(note, REACH), above, block, below)
     windows = lax.all_to_all(windows, "cuts", 0, 0, tiled=False)
     gradient = pl.pallas_call(
         functools.partial(chain_kernel, unit),
@@ -203,7 +227,7 @@
             jax.ShapeDtypeStruct(strip_shape, F32),
             jax.ShapeDtypeStruct(strip_shape, BF16),
         ),
-        in_specs=[smem, vmem],
+        in_specs=[vmem, vmem],
         out_specs=(vmem, vmem, vmem),
         compiler_params=params,
         name="add_windows",

time: 105 us -> 87 us (0.83)
  starting transfers between devices: 42.8 us -> 33.4 us
  Pallas kernels: 20 us -> 13.6 us
  waiting for transfers between devices: 25.5 us -> 23.5 us
    ppermute x7 -> x5, starting transfers between devices: 36.2 us -> 26.8 us  [shifted(): return lax.ppermute(block, 'strip', route)]
    pallas_call x1, Pallas kernels: 8.74 us -> 2.92 us  [on_device(): pl.pallas_call(functools.partial(cut_kernel, strip_rows), out_shape=(jax....]
    ppermute x7 -> x5, waiting for transfers between devices: 10.6 us -> 8.62 us  [shifted(): return lax.ppermute(block, 'strip', route)]
  transfers between devices with their start and end apart: 8 -> 6, of which waited for: 4 -> 4; matrix products, arithmetic and copies ran while one was open for 1% -> 0% of each run, Pallas kernels for 0% -> 0%
where the time goes in v2:
time: 87 us; the launch traced here: 86.6 us
  starting transfers between devices  33.4 us (38%)
  waiting for transfers between devices  23.5 us (27%)
  Pallas kernels  13.6 us (16%)
  blocking collectives  12.6 us (14%)
  other arithmetic  1.85 us (2%)
  local copies, waits for them, and re-layouts  1.56 us (2%)
    ppermute x5, starting transfers between devices, shifted(): return lax.ppermute(block, 'strip', route)  26.8 us
    all_to_all x1, waiting for transfers between devices, on_device(): windows = lax.all_to_all(windows, 'cuts', 0, 0, tiled=False)  14.8 us
    all_to_all x1, blocking collectives, on_device(): gradient = lax.all_to_all(gradient, 'cuts', 0, 0, tiled=False)  12.6 us
    pallas_call x1, Pallas kernels, on_device(): pl.pallas_call(functools.partial(chain_kernel, unit), out_shape=jax.Shape...  9.85 us
    ppermute x5, waiting for transfers between devices, shifted(): return lax.ppermute(block, 'strip', route)  8.62 us
    all_to_all x1, starting transfers between devices, on_device(): windows = lax.all_to_all(windows, 'cuts', 0, 0, tiled=False)  6.54 us
    pallas_call x1, Pallas kernels, on_device(): pl.pallas_call(functools.partial(cut_kernel, strip_rows), out_shape=(jax....  2.92 us
  transfers between devices with their start and end apart: 6, of which 4 were waited for; matrix products, arithmetic and copies ran while one was open for 0% of the time, Pallas kernels for 0%

profile of v2, /device:TPU:1, one launch (start us, length us, event | category | flops | bytes accessed | tf_op | source)
XLA Modules:
  0.0 86.6 jit_solution(2708065785311969165)
XLA Ops:
  0.0 0.0 copy-start.4
  0.0 0.7 copy-done.4
  0.7 0.0 copy-start.5
  0.7 0.6 copy-done.5
  1.3 0.1 fusion.8
  1.4 1.0 %pad_maximum_fusion.own_ref = bf16[528,256]{1,0:T(8,128)(2,1)S(1)} fusion(bf16[16,256]{1,0:T(8,128)(2,1)S(1)} %fusion.8, bf16[256,256]{1,0:T(8,128)(2,1)} %bitcast.10, bf16[256,256]{1,0:T(8,128)(2,1)} %bitcast.11), kind=kLoop, calls=%fused_computation | loop fusion | flops 811008 | bytes 540672 | tf_op jit(solution)/shard_map/concatenate | solution.py:191
  2.4 4.4 %collective-permute-start.1 = (bf16[528,256]{1,0:T(8,128)(2,1)S(1)}, bf16[528,256]{1,0:T(8,128)(2,1)S(1)}, u32[]{:S(2)}, u32[]{:S(2)}) collective-permute-start(bf16[528,256]{1,0:T(8,128)(2,1)S(1)} %pad_maximum_fusion.own_ref), channel_id=1, source_target_pairs={{63,0},{0,1},{1,2},{2,3},{3,4},{4,5},{5,6},{6,7},{7,8},{8,9},{9,10... | collective-permute-start | bytes 811016 | tf_op jit(solution)/shard_map/ppermute | solution.py:179
  6.8 11.9 %collective-permute-start.2 = (bf16[528,256]{1,0:T(8,128)(2,1)S(1)}, bf16[528,256]{1,0:T(8,128)(2,1)S(1)}, u32[]{:S(2)}, u32[]{:S(2)}) collective-permute-start(bf16[528,256]{1,0:T(8,128)(2,1)S(1)} %pad_maximum_fusion.own_ref), channel_id=1, source_target_pairs={{1,0},{2,1},{3,2},{4,3},{5,4},{6,5},{7,6},{8,7},{9,8},{10,9},{11,1... | collective-permute-start | bytes 811016 | tf_op jit(solution)/shard_map/ppermute | solution.py:179
  18.8 1.9 %collective-permute-start = (bf16[16,256]{1,0:T(8,128)(2,1)S(1)}, bf16[16,256]{1,0:T(8,128)(2,1)S(1)}, u32[]{:S(2)}, u32[]{:S(2)}) collective-permute-start(bf16[16,256]{1,0:T(8,128)(2,1)S(1)} %fusion.8), channel_id=1, source_target_pairs={{62,0},{63,1},{0,2},{1,3},{2,4},{3,5},{4,6},{5,7},{6,8},{7,9},{8,1... | collective-permute-start | bytes 24584 | tf_op jit(solution)/shard_map/ppermute | solution.py:179
  20.7 6.7 %collective-permute-done.far_ref = bf16[16,256]{1,0:T(8,128)(2,1)S(1)} collective-permute-done((bf16[16,256]{1,0:T(8,128)(2,1)S(1)}, bf16[16,256]{1,0:T(8,128)(2,1)S(1)}, u32[]{:S(2)}, u32[]{:S(2)}) %collective-permute-start) | collective-permute-done | bytes 8224 | tf_op jit(solution)/shard_map/ppermute | solution.py:179
  27.4 0.0 collective-permute-done.1.above_ref
  27.4 0.0 collective-permute-done.2.below_ref
  27.4 2.9 %cut_windows.1 = (bf16[8,4,128,128]{3,2,1,0:T(8,128)(2,1)}, f32[16,128]{1,0:T(8,128)S(1)}) custom-call(bf16[16,256]{1,0:T(8,128)(2,1)S(1)} %collective-permute-done.far_ref, bf16[528,256]{1,0:T(8,128)(2,1)S(1)} %collective-permute-done.1.above_ref, bf16[528,256]{1,0:T(8,128)(2,1)S(1)} %pad_maximum_fusion.own_ref, ...), custom_call_target="tpu_custom_call" | custom-call | tf_op jit(solution)/shard_map/cut_windows/pallas_call | solution.py:200
  30.3 0.0 copy-start.3
  30.3 0.0 copy-start.1
  30.3 6.5 %all-to-all-start = ((bf16[8,4,128,128]{3,2,1,0:T(8,128)(2,1)}), bf16[8,4,128,128]{3,2,1,0:T(8,128)(2,1)S(1)}, u32[]{:S(2)}, u32[]{:S(2)}) async-start(bf16[8,4,128,128]{3,2,1,0:T(8,128)(2,1)} %get-tuple-element.11), calls=%async_computation | async-start | bytes 2097152 | tf_op jit(solution)/shard_map/all_to_all | solution.py:211
  36.8 0.0 copy-done.3
  36.9 0.0 copy-start
  36.9 0.0 copy-start.2
  36.9 0.2 fusion.10
  37.1 14.8 %all-to-all-done.window_ref = bf16[8,4,128,128]{3,2,1,0:T(8,128)(2,1)S(1)} async-done(((bf16[8,4,128,128]{3,2,1,0:T(8,128)(2,1)}), bf16[8,4,128,128]{3,2,1,0:T(8,128)(2,1)S(1)}, u32[]{:S(2)}, u32[]{:S(2)}) %all-to-all-start) | async-done | bytes 1048608 | tf_op jit(solution)/shard_map/all_to_all | solution.py:211
  51.9 0.0 copy-done.1
  52.0 0.0 copy-done
  52.0 0.0 copy-done.2
  52.0 9.8 %wave_chain.1 = bf16[8,2,128,128]{3,2,1,0:T(8,128)(2,1)S(1)} custom-call(bf16[8,4,128,128]{3,2,1,0:T(8,128)(2,1)S(1)} %all-to-all-done.window_ref, bf16[2,128,128]{2,1,0:T(8,128)(2,1)S(1)} %copy-done.2, f32[128,128]{1,0:T(8,128)S(1)} %get-tuple-element.18.cos_ref, f32[128,128]{1,0:T(8,128)S(1)} %get-tuple-element.17.sin_ref, bf16[256,256]{1,0:T(8,128)(2,1)S(1)} %copy-done, ...), custom_call_target="tpu_custom_call" | custom-call | tf_op jit(solution)/shard_map/wave_chain/pallas_call | solution.py:212
  61.8 12.6 %all_to_all.10.grad_ref = bf16[8,2,128,128]{3,2,1,0:T(8,128)(2,1)S(1)} all-to-all(bf16[8,2,128,128]{3,2,1,0:T(8,128)(2,1)S(1)} %wave_chain.1), channel_id=1, replica_groups=mesh['cuts'=8,'strip'=64] {'cuts'}, dimensions={0} | all-to-all | bytes 1048576 | tf_op jit(solution)/shard_map/all_to_all | solution.py:221
  74.4 0.9 add_windows.1
  75.3 1.9 %collective-permute-start.4 = (bf16[2,128,256]{2,1,0:T(8,128)(2,1)S(1)}, bf16[2,128,256]{2,1,0:T(8,128)(2,1)S(1)}, u32[]{:S(2)}, u32[]{:S(2)}) collective-permute-start(bf16[2,128,256]{2,1,0:T(8,128)(2,1)S(1)} %get-tuple-element.14), channel_id=1, source_target_pairs={{63,0},{0,1},{1,2},{2,3},{3,4},{4,5},{5,6},{6,7},{7,8},{8,9},{9,10... | collective-permute-start | bytes 393224 | tf_op jit(solution)/shard_map/ppermute | solution.py:179
  77.2 6.7 %collective-permute-start.3 = (bf16[2,128,256]{2,1,0:T(8,128)(2,1)S(1)}, bf16[2,128,256]{2,1,0:T(8,128)(2,1)S(1)}, u32[]{:S(2)}, u32[]{:S(2)}) collective-permute-start(bf16[2,128,256]{2,1,0:T(8,128)(2,1)S(1)} %get-tuple-element.13), channel_id=1, source_target_pairs={{1,0},{2,1},{3,2},{4,3},{5,4},{6,5},{7,6},{8,7},{9,8},{10,9},{11,1... | collective-permute-start | bytes 393224 | tf_op jit(solution)/shard_map/ppermute | solution.py:179
  83.9 0.4 collective-permute-done.4
  84.3 1.5 %collective-permute-done.3 = bf16[2,128,256]{2,1,0:T(8,128)(2,1)S(1)} collective-permute-done((bf16[2,128,256]{2,1,0:T(8,128)(2,1)S(1)}, bf16[2,128,256]{2,1,0:T(8,128)(2,1)S(1)}, u32[]{:S(2)}, u32[]{:S(2)}) %collective-permute-start.3) | collective-permute-done | bytes 131104 | tf_op jit(solution)/shard_map/ppermute | solution.py:179
  85.9 0.7 add_bitcast_fusion
  (2 shorter events, 0.0 us)
Async XLA Ops:
  0.0 0.7 copy-start.4
  0.7 0.7 copy-start.5
  2.4 25.0 %collective-permute-start.1 = (bf16[528,256]{1,0:T(8,128)(2,1)S(1)}, bf16[528,256]{1,0:T(8,128)(2,1)S(1)}, u32[]{:S(2)}, u32[]{:S(2)}) collective-permute-start(bf16[528,256]{1,0:T(8,128)(2,1)S(1)} %pad_maximum_fusion.own_ref), channel_id=1, source_target_pairs={{63,0},{0,1},{1,2},{2,3},{3,4},{4,5},{5,6},{6,7},{7,8},{8,9},{9,10... | collective-permute-start | bytes 811016 | tf_op jit(solution)/shard_map/ppermute | solution.py:179
  6.8 20.6 %collective-permute-start.2 = (bf16[528,256]{1,0:T(8,128)(2,1)S(1)}, bf16[528,256]{1,0:T(8,128)(2,1)S(1)}, u32[]{:S(2)}, u32[]{:S(2)}) collective-permute-start(bf16[528,256]{1,0:T(8,128)(2,1)S(1)} %pad_maximum_fusion.own_ref), channel_id=1, source_target_pairs={{1,0},{2,1},{3,2},{4,3},{5,4},{6,5},{7,6},{8,7},{9,8},{10,9},{11,1... | collective-permute-start | bytes 811016 | tf_op jit(solution)/shard_map/ppermute | solution.py:179
  18.8 8.6 %collective-permute-start = (bf16[16,256]{1,0:T(8,128)(2,1)S(1)}, bf16[16,256]{1,0:T(8,128)(2,1)S(1)}, u32[]{:S(2)}, u32[]{:S(2)}) collective-permute-start(bf16[16,256]{1,0:T(8,128)(2,1)S(1)} %fusion.8), channel_id=1, source_target_pairs={{62,0},{63,1},{0,2},{1,3},{2,4},{3,5},{4,6},{5,7},{6,8},{7,9},{8,1... | collective-permute-start | bytes 24584 | tf_op jit(solution)/shard_map/ppermute | solution.py:179
  30.3 6.6 %copy-start.3 = (f32[128,128]{1,0:T(8,128)S(1)}, f32[128,128]{1,0:T(8,128)}, u32[]{:S(2)}) copy-start(f32[128,128]{1,0:T(8,128)} %param.11) | copy-start | bytes 196612
  30.3 21.6 %copy-start.1 = (bf16[256,256]{1,0:T(8,128)(2,1)S(1)}, bf16[256,256]{1,0:T(8,128)(2,1)}, u32[]{:S(2)}) copy-start(bf16[256,256]{1,0:T(8,128)(2,1)} %constant.55.clone.minus_ref) | copy-start | bytes 393220
  30.3 21.6 %all-to-all-start = ((bf16[8,4,128,128]{3,2,1,0:T(8,128)(2,1)}), bf16[8,4,128,128]{3,2,1,0:T(8,128)(2,1)S(1)}, u32[]{:S(2)}, u32[]{:S(2)}) async-start(bf16[8,4,128,128]{3,2,1,0:T(8,128)(2,1)} %get-tuple-element.11), calls=%async_computation | async-start | bytes 2097152 | tf_op jit(solution)/shard_map/all_to_all | solution.py:211
  36.9 15.1 %copy-start = (bf16[256,256]{1,0:T(8,128)(2,1)S(1)}, bf16[256,256]{1,0:T(8,128)(2,1)}, u32[]{:S(2)}) copy-start(bf16[256,256]{1,0:T(8,128)(2,1)} %constant.54.clone.plus_ref) | copy-start | bytes 393220
  36.9 15.1 %copy-start.2 = (bf16[2,128,128]{2,1,0:T(8,128)(2,1)S(1)}, bf16[2,128,128]{2,1,0:T(8,128)(2,1)}, u32[]{:S(2)}) copy-start(bf16[2,128,128]{2,1,0:T(8,128)(2,1)} %probe_ref.1) | copy-start | bytes 196612
  75.3 9.0 %collective-permute-start.4 = (bf16[2,128,256]{2,1,0:T(8,128)(2,1)S(1)}, bf16[2,128,256]{2,1,0:T(8,128)(2,1)S(1)}, u32[]{:S(2)}, u32[]{:S(2)}) collective-permute-start(bf16[2,128,256]{2,1,0:T(8,128)(2,1)S(1)} %get-tuple-element.14), channel_id=1, source_target_pairs={{63,0},{0,1},{1,2},{2,3},{3,4},{4,5},{5,6},{6,7},{7,8},{8,9},{9,10... | collective-permute-start | bytes 393224 | tf_op jit(solution)/shard_map/ppermute | solution.py:179
  77.2 8.6 %collective-permute-start.3 = (bf16[2,128,256]{2,1,0:T(8,128)(2,1)S(1)}, bf16[2,128,256]{2,1,0:T(8,128)(2,1)S(1)}, u32[]{:S(2)}, u32[]{:S(2)}) collective-permute-start(bf16[2,128,256]{2,1,0:T(8,128)(2,1)S(1)} %get-tuple-element.13), channel_id=1, source_target_pairs={{1,0},{2,1},{3,2},{4,3},{5,4},{6,5},{7,6},{8,7},{9,8},{10,9},{11,1... | collective-permute-start | bytes 393224 | tf_op jit(solution)/shard_map/ppermute | solution.py:179

commit v3 on v2

--- a/solution.py
+++ b/solution.py
@@ -46,13 +46,59 @@
     return jnp.where((row_index - col_index).astype(F32) == start, 1.0, 0.0).astype(BF16)
 
 
-def cut_kernel(rows, far_ref, above_ref, own_ref, below_ref, out_ref, start_ref):
+def pack_kernel(
+    strip_rows, total_rows, row_any, col_any, object_any, direction_any, block_ref, note_ref, row_ref, col_ref, sems
+):
+    half = object_any.shape[0]
+    columns = block_ref.shape[1]
+    corners = [
+        pltpu.make_async_copy(row_any, row_ref, sems.at[0]),
+        pltpu.make_async_copy(col_any, col_ref, sems.at[1]),
+    ]
+    bulk = [
+        pltpu.make_async_copy(object_any, block_ref.at[pl.ds(0, half), :], sems.at[2]),
+        pltpu.make_async_copy(direction_any, block_ref.at[pl.ds(half, half), :], sems.at[3]),
+    ]
+    for copy in corners + bulk:
+        copy.start()
+    for copy in corners:
+        copy.wait()
+    strip_index = lax.axis_index("strip")
+    near = row_ref.shape[0]
+    lane = lax.broadcasted_iota(jnp.int32, (NOTE_ROWS, columns), 1)
+    note = jnp.zeros((NOTE_ROWS, columns), F32)
+    for position in range(near):
+        inside = row_ref[position] - (strip_index - REACH) * strip_rows
+        inside = lax.rem(inside + 2 * total_rows, total_rows)
+        ahead = 2 * REACH - lax.div(inside, strip_rows) - REACH
+        to_owner = ahead - jnp.clip(ahead, 0, 1)
+        first_row = inside + (to_owner + 1 - REACH) * strip_rows
+        for place, value in enumerate((first_row, col_ref[position], to_owner)):
+            note = jnp.where(lane == place * near + position, value.astype(F32), note)
+    note = note.astype(BF16)
+    block_ref[2 * half :, :] = note
+    note_ref[...] = note
+    for copy in bulk:
+        copy.wait()
+
+
+def phase_kernel(note_ref, phase_ref, far_ref, cos_ref, sin_ref):
+    far_ref[...] = note_ref[...]
+    cos_ref[...] = jnp.cos(phase_ref[...])
+    sin_ref[...] = jnp.sin(phase_ref[...])
+
+
+def cut_kernel(rows, far_ref, note_ref, object_ref, direction_ref, second_ref, first_ref, out_ref, start_ref):
+    even = lax.rem(lax.axis_index("strip"), 2) == 0
+    first, second = first_ref[...], second_ref[...]
+    above, below = jnp.where(even, first, second), jnp.where(even, second, first)
+    own = jnp.concatenate([object_ref[...], direction_ref[...], note_ref[...]], axis=0)
     slots, parts, size, _ = out_ref.shape
-    columns = own_ref.shape[1]
+    columns = object_ref.shape[1]
     near = slots // 4
     hots = []
-    for owner, note_ref in enumerate((far_ref, above_ref, own_ref, below_ref)):
-        note = note_ref[note_ref.shape[0] - NOTE_ROWS :, :].astype(F32)[0:1]
+    for owner, block in enumerate((far_ref[...], above, own, below)):
+        note = block[block.shape[0] - NOTE_ROWS :, :].astype(F32)[0:1]
         for position in range(near):
             here = note[:, 2 * near + position : 2 * near + position + 1] == owner - REACH
             first_row = jnp.where(here, note[:, position : position + 1], 4.0 * rows)
@@ -63,7 +109,7 @@
             hots.append((row_hot(first_row, size, 3 * rows), col_hot(first_col, columns, size)))
     bands = [
         jnp.concatenate(
-            [ref[part * rows : (part + 1) * rows, :] for ref in (above_ref, own_ref, below_ref)], axis=0
+            [block[part * rows : (part + 1) * rows, :] for block in (above, own, below)], axis=0
         )
         for part in range(parts)
     ]
@@ -144,9 +190,10 @@
             adjoint = inverse(kernel_times(forward(columns), -1.0, hop_scale))
 
 
-def gather_kernel(start_ref, grad_ref, above_ref, own_ref, below_ref):
+def gather_kernel(start_ref, grad_ref, first_ref, own_ref, second_ref):
     slots, parts, size, _ = grad_ref.shape
     rows, columns = own_ref.shape[1:]
+    even = lax.rem(lax.axis_index("strip"), 2) == 0
     placed = [[] for _ in range(parts)]
     hots = []
     for slot in range(slots):
@@ -160,9 +207,10 @@
     pick_rows = jnp.concatenate(hots, axis=1)
     for part in range(parts):
         total = dot(pick_rows, jnp.concatenate(placed[part], axis=0))
-        above_ref[part] = total[:rows].astype(BF16)
+        above, below = total[:rows].astype(BF16), total[2 * rows :].astype(BF16)
         own_ref[part] = total[rows : 2 * rows]
-        below_ref[part] = total[2 * rows :].astype(BF16)
+        first_ref[part] = jnp.where(even, above, below)
+        second_ref[part] = jnp.where(even, below, above)
 
 
 def on_device(object_slices, direction, probe_wave, kernel_phase, corner_row, corner_col):
@@ -171,43 +219,62 @@
     patch_size = probe_wave.shape[1]
     strip_count = lax.axis_size("strip")
     cuts_count = lax.axis_size("cuts")
-    strip_index = lax.axis_index("strip")
     plus, minus, unit = transform_tables(patch_size)
 
-    def shifted(block, distance):
-        route = [((i - distance) % strip_count, i) for i in range(strip_count)]
-        return lax.ppermute(block, "strip", route)
+    def exchanged(block, offset):
+        route = [(i, ((i - offset) ^ 1) + offset) for i in range(strip_count)]
+        return lax.ppermute(block, "strip", [(i, j % strip_count) for i, j in route])
 
     vmem = pl.BlockSpec(memory_space=pltpu.VMEM)
     params = pltpu.CompilerParams(vmem_limit_bytes=32 * 1024 * 1024)
 
-    total_rows = strip_count * strip_rows
-    inside = (corner_row - (strip_index - REACH) * strip_rows) % total_rows - REACH * strip_rows
-    ahead = REACH - (inside + REACH * strip_rows) // strip_rows
-    to_owner = ahead - jnp.clip(ahead, 0, 1)
-    first_row = inside + (to_owner + 1) * strip_rows
-    note = jnp.concatenate([first_row, corner_col, to_owner]).astype(BF16)
-    note = jnp.pad(note[None], ((0, NOTE_ROWS - 1), (0, column_count - note.shape[0])))
-    block = jnp.concatenate(
-        [
-            object_slices.reshape(2 * strip_rows, column_count),
-            direction.reshape(2 * strip_rows, column_count),
-            note,
+    block_rows = 4 * strip_rows + NOTE_ROWS
+    hbm = pl.BlockSpec(memory_space=pl.ANY)
+    wide = pltpu.CompilerParams(vmem_limit_bytes=60 * 1024 * 1024)
+    objects = object_slices.reshape(-1, column_count)
+    directions = direction.reshape(-1, column_count)
+    block, note = pl.pallas_call(
+        functools.partial(pack_kernel, strip_rows, strip_count * strip_rows),
+        out_shape=(
+            jax.ShapeDtypeStruct((block_rows, column_count), BF16),
+            jax.ShapeDtypeStruct((NOTE_ROWS, column_count), BF16),
+        ),
+        in_specs=[hbm] * 4,
+        out_specs=(vmem, vmem),
+        scratch_shapes=[
+            pltpu.SMEM(corner_row.shape, jnp.int32),
+            pltpu.SMEM(corner_row.shape, jnp.int32),
+            pltpu.SemaphoreType.DMA((4,)),
         ],
-        axis=0,
-    )
-    above, below = shifted(block, 1), shifted(block, -1)
+        compiler_params=wide,
+        name="pack_block",
+    )(corner_row, corner_col, objects, directions)
+    far = lax.ppermute(note, "strip", [(i, (i + REACH) % strip_count) for i in range(strip_count)])
+    first, second = exchanged(block, -1), exchanged(block, 0)
+    far, kernel_cos, kernel_sin = pl.pallas_call(
+        phase_kernel,
+        out_shape=(
+            jax.ShapeDtypeStruct(note.shape, BF16),
+            jax.ShapeDtypeStruct(kernel_phase.shape, F32),
+            jax.ShapeDtypeStruct(kernel_phase.shape, F32),
+        ),
+        in_specs=[vmem] * 2,
+        out_specs=(vmem,) * 3,
+        compiler_params=params,
+        cost_estimate=pl.CostEstimate(flops=20_000_000_000, bytes_accessed=100_000_000, transcendentals=0),
+        name="phase_tables",
+    )(far, kernel_phase)
     windows, start = pl.pallas_call(
         functools.partial(cut_kernel, strip_rows),
         out_shape=(
             jax.ShapeDtypeStruct((cuts_count, 4, patch_size, patch_size), BF16),
             jax.ShapeDtypeStruct((2 * cuts_count, 128), F32),
         ),
-        in_specs=[vmem] * 4,
+        in_specs=[vmem] * 6,
         out_specs=(vmem, vmem),
         compiler_params=params,
         name="cut_windows",
-    )(shifted(note, REACH), above, block, below)
+    )(far, note, objects, directions, second, first)
     windows = lax.all_to_all(windows, "cuts", 0, 0, tiled=False)
     gradient = pl.pallas_call(
         functools.partial(chain_kernel, unit),
@@ -217,10 +284,10 @@
         scratch_shapes=[pltpu.VMEM((cuts_count, 2, patch_size, patch_size), F32)],
         compiler_params=params,
         name="wave_chain",
-    )(windows, probe_wave, jnp.cos(kernel_phase), jnp.sin(kernel_phase), jnp.asarray(plus), jnp.asarray(minus))
+    )(windows, probe_wave, kernel_cos, kernel_sin, jnp.asarray(plus), jnp.asarray(minus))
     gradient = lax.all_to_all(gradient, "cuts", 0, 0, tiled=False)
     strip_shape = (2, strip_rows, column_count)
-    to_above, own, to_below = pl.pallas_call(
+    first, own, second = pl.pallas_call(
         gather_kernel,
         out_shape=(
             jax.ShapeDtypeStruct(strip_shape, BF16),
@@ -232,9 +299,8 @@
         compiler_params=params,
         name="add_windows",
     )(start, gradient)
-    from_below = shifted(to_above, -1).astype(F32)
-    from_above = shifted(to_below, 1).astype(F32)
-    return (own + from_below + from_above)[None]
+    first, second = exchanged(first, -1), exchanged(second, 0)
+    return (own + first.astype(F32) + second.astype(F32))[None]
 
 
 def solution(mesh):

time: 87 us -> 84.5 us (0.971)
  blocking collectives: 12.6 us -> 34 us
  waiting for transfers between devices: 23.5 us -> 10.8 us
  starting transfers between devices: 33.4 us -> 23.6 us
  local copies, waits for them, and re-layouts: 1.56 us -> 0.04 us
  Pallas kernels: 13.6 us -> 14.8 us
  other arithmetic: 1.85 us -> 0.75 us
    all_to_all x0 -> x1, blocking collectives: none -> 21.2 us  [on_device(): windows = lax.all_to_all(windows, 'cuts', 0, 0, tiled=False)]
    all_to_all x1 -> x0, waiting for transfers between devices: 14.8 us -> none  [on_device(): windows = lax.all_to_all(windows, 'cuts', 0, 0, tiled=False)]
    all_to_all x1 -> x0, starting transfers between devices: 6.54 us -> none  [on_device(): windows = lax.all_to_all(windows, 'cuts', 0, 0, tiled=False)]
    ppermute x5, starting transfers between devices: 26.8 us -> 23.6 us  [the longest x4 17.9 us: exchanged(): lax.ppermute(block, 'strip', [(i, j % strip_count) for i, j in route])]
    ppermute x5, waiting for transfers between devices: 8.62 us -> 10.8 us  [the longest x4 10.8 us: exchanged(): lax.ppermute(block, 'strip', [(i, j % strip_count) for i, j in route])]
    pallas_call x0 -> x2, Pallas kernels: none -> 2.17 us  [the longest x1 1.74 us: on_device(): pl.pallas_call(functools.partial(pack_kernel, strip_rows, strip_count * s...]
    unnamed x12 -> x14, local copies, waits for them, and re-layouts: 1.32 us -> 0.04 us
    concatenate x4 -> x0, other arithmetic: 1.1 us -> none  [the longest x1 0.99 us: on_device(): jnp.concatenate([object_slices.reshape(2 * strip_rows, column_count), dir...]
  transfers between devices with their start and end apart: 6 -> 5, of which waited for: 4 -> 4; matrix products, arithmetic and copies ran while one was open for 0% -> 0% of each run, Pallas kernels for 0% -> 1%
where the time goes in v3:
time: 84.5 us; the launch traced here: 84.2 us
  blocking collectives  34 us (40%)
  starting transfers between devices  23.6 us (28%)
  Pallas kernels  14.8 us (18%)
  waiting for transfers between devices  10.8 us (13%)
    all_to_all x1, blocking collectives, on_device(): windows = lax.all_to_all(windows, 'cuts', 0, 0, tiled=False)  21.2 us
    ppermute x4, starting transfers between devices, exchanged(): lax.ppermute(block, 'strip', [(i, j % strip_count) for i, j in route])  17.9 us
    all_to_all x1, blocking collectives, on_device(): gradient = lax.all_to_all(gradient, 'cuts', 0, 0, tiled=False)  12.8 us
    ppermute x4, waiting for transfers between devices, exchanged(): lax.ppermute(block, 'strip', [(i, j % strip_count) for i, j in route])  10.8 us
    pallas_call x1, Pallas kernels, on_device(): pl.pallas_call(functools.partial(chain_kernel, unit), out_shape=jax.Shape...  9.84 us
    ppermute x1, starting transfers between devices, on_device(): lax.ppermute(note, 'strip', [(i, (i + REACH) % strip_count) for i in rang...  5.73 us
    pallas_call x1, Pallas kernels, on_device(): pl.pallas_call(functools.partial(cut_kernel, strip_rows), out_shape=(jax....  1.95 us
    pallas_call x1, Pallas kernels, on_device(): pl.pallas_call(functools.partial(pack_kernel, strip_rows, strip_count * s...  1.74 us
  transfers between devices with their start and end apart: 5, of which 4 were waited for; matrix products, arithmetic and copies ran while one was open for 0% of the time, Pallas kernels for 1%

profile of v3, /device:TPU:1, one launch (start us, length us, event | category | flops | bytes accessed | tf_op | source)
XLA Modules:
  0.0 84.2 jit_solution(9394349021741094273)
XLA Ops:
  0.0 0.0 copy-start.6
  0.0 1.7 %pack_block.1 = (bf16[528,256]{1,0:T(8,128)(2,1)}, bf16[16,256]{1,0:T(8,128)(2,1)}) custom-call(s32[2]{0:T(128)} %row_any.1, s32[2]{0:T(128)} %col_any.1, bf16[256,256]{1,0:T(8,128)(2,1)} %bitcast.4, bf16[256,256]{1,0:T(8,128)(2,1)} %bitcast.6), custom_call_target="tpu_custom_call" | custom-call | tf_op jit(solution)/shard_map/pack_block/pallas_call | solution.py:236
  1.7 5.7 %collective-permute-start = (bf16[16,256]{1,0:T(8,128)(2,1)}, bf16[16,256]{1,0:T(8,128)(2,1)S(1)}, u32[]{:S(2)}, u32[]{:S(2)}) collective-permute-start(bf16[16,256]{1,0:T(8,128)(2,1)} %get-tuple-element.15.note_ref), channel_id=1, source_target_pairs={{0,2},{1,3},{2,4},{3,5},{4,6},{5,7},{6,8},{7,9},{8,10},{9,11},{10,... | collective-permute-start | bytes 24584 | tf_op jit(solution)/shard_map/ppermute | solution.py:252
  7.5 0.0 copy-start
  7.5 0.0 copy-start.1
  7.5 0.0 copy-start.5
  7.5 10.7 %collective-permute-start.2 = (bf16[528,256]{1,0:T(8,128)(2,1)}, bf16[528,256]{1,0:T(8,128)(2,1)S(1)}, u32[]{:S(2)}, u32[]{:S(2)}) collective-permute-start(bf16[528,256]{1,0:T(8,128)(2,1)} %get-tuple-element.17), channel_id=1, source_target_pairs={{0,63},{1,2},{2,1},{3,4},{4,3},{5,6},{6,5},{7,8},{8,7},{9,10},{10,... | collective-permute-start | bytes 811016 | tf_op jit(solution)/shard_map/ppermute | solution.py:226
  18.3 1.9 %collective-permute-start.1 = (bf16[528,256]{1,0:T(8,128)(2,1)}, bf16[528,256]{1,0:T(8,128)(2,1)S(1)}, u32[]{:S(2)}, u32[]{:S(2)}) collective-permute-start(bf16[528,256]{1,0:T(8,128)(2,1)} %get-tuple-element.17), channel_id=1, source_target_pairs={{0,1},{1,0},{2,3},{3,2},{4,5},{5,4},{6,7},{7,6},{8,9},{9,8},{10,11... | collective-permute-start | bytes 811016 | tf_op jit(solution)/shard_map/ppermute | solution.py:226
  20.2 0.0 collective-permute-done.note_ref
  20.2 0.0 copy-done.6
  20.2 0.4 phase_tables.1
  20.6 4.0 %collective-permute-done.2.first_ref = bf16[528,256]{1,0:T(8,128)(2,1)S(1)} collective-permute-done((bf16[528,256]{1,0:T(8,128)(2,1)}, bf16[528,256]{1,0:T(8,128)(2,1)S(1)}, u32[]{:S(2)}, u32[]{:S(2)}) %collective-permute-start.2) | collective-permute-done | bytes 270368 | tf_op jit(solution)/shard_map/ppermute | solution.py:226
  24.7 2.7 %collective-permute-done.1.second_ref = bf16[528,256]{1,0:T(8,128)(2,1)S(1)} collective-permute-done((bf16[528,256]{1,0:T(8,128)(2,1)}, bf16[528,256]{1,0:T(8,128)(2,1)S(1)}, u32[]{:S(2)}, u32[]{:S(2)}) %collective-permute-start.1) | collective-permute-done | bytes 270368 | tf_op jit(solution)/shard_map/ppermute | solution.py:226
  27.4 0.0 copy-done
  27.4 0.0 copy-done.1
  27.4 0.0 copy-done.5
  27.4 1.9 %cut_windows.1 = (bf16[8,4,128,128]{3,2,1,0:T(8,128)(2,1)S(1)}, f32[16,128]{1,0:T(8,128)S(1)}) custom-call(bf16[16,256]{1,0:T(8,128)(2,1)S(1)} %get-tuple-element.16.far_ref, bf16[16,256]{1,0:T(8,128)(2,1)S(1)} %copy-done.5, bf16[256,256]{1,0:T(8,128)(2,1)S(1)} %bitcast.5, bf16[256,256]{1,0:T(8,128)(2,1)S(1)} %bitcast.7, ...), custom_call_target="tpu_custom_call" | custom-call | tf_op jit(solution)/shard_map/cut_windows/pallas_call | solution.py:267
  29.4 0.0 copy-start.2
  29.4 0.0 copy-start.3
  29.4 0.0 copy-start.4
  29.4 21.2 %all_to_all.10.window_ref = bf16[8,4,128,128]{3,2,1,0:T(8,128)(2,1)S(1)} all-to-all(bf16[8,4,128,128]{3,2,1,0:T(8,128)(2,1)S(1)} %get-tuple-element.19), channel_id=1, replica_groups=mesh['cuts'=8,'strip'=64] {'cuts'}, dimensions={0} | all-to-all | bytes 2097152 | tf_op jit(solution)/shard_map/all_to_all | solution.py:278
  50.5 0.0 copy-done.2
  50.5 0.0 copy-done.3
  50.6 0.0 copy-done.4
  50.6 9.8 %wave_chain.1 = bf16[8,2,128,128]{3,2,1,0:T(8,128)(2,1)S(1)} custom-call(bf16[8,4,128,128]{3,2,1,0:T(8,128)(2,1)S(1)} %all_to_all.10.window_ref, bf16[2,128,128]{2,1,0:T(8,128)(2,1)S(1)} %copy-done.4, f32[128,128]{1,0:T(8,128)S(1)} %get-tuple-element.20.cos_ref, f32[128,128]{1,0:T(8,128)S(1)} %get-tuple-element.21.sin_ref, bf16[256,256]{1,0:T(8,128)(2,1)S(1)} %copy-done.3, ...), custom_call_target="tpu_custom_call" | custom-call | tf_op jit(solution)/shard_map/wave_chain/pallas_call | solution.py:279
  60.4 12.8 %all_to_all.11.grad_ref = bf16[8,2,128,128]{3,2,1,0:T(8,128)(2,1)S(1)} all-to-all(bf16[8,2,128,128]{3,2,1,0:T(8,128)(2,1)S(1)} %wave_chain.1), channel_id=1, replica_groups=mesh['cuts'=8,'strip'=64] {'cuts'}, dimensions={0} | all-to-all | bytes 1048576 | tf_op jit(solution)/shard_map/all_to_all | solution.py:288
  73.2 0.9 %add_windows.1 = (bf16[2,128,256]{2,1,0:T(8,128)(2,1)S(1)}, f32[2,128,256]{2,1,0:T(8,128)S(1)}, bf16[2,128,256]{2,1,0:T(8,128)(2,1)S(1)}) custom-call(f32[16,128]{1,0:T(8,128)S(1)} %get-tuple-element.18.start_ref, bf16[8,2,128,128]{3,2,1,0:T(8,128)(2,1)S(1)} %all_to_all.11.grad_ref), custom_call_target="tpu_custom_call" | custom-call | tf_op jit(solution)/shard_map/add_windows/pallas_call | solution.py:290
  74.1 3.3 %collective-permute-start.3 = (bf16[2,128,256]{2,1,0:T(8,128)(2,1)S(1)}, bf16[2,128,256]{2,1,0:T(8,128)(2,1)S(1)}, u32[]{:S(2)}, u32[]{:S(2)}) collective-permute-start(bf16[2,128,256]{2,1,0:T(8,128)(2,1)S(1)} %get-tuple-element.23), channel_id=1, source_target_pairs={{0,63},{1,2},{2,1},{3,4},{4,3},{5,6},{6,5},{7,8},{8,7},{9,10},{10,... | collective-permute-start | bytes 393224 | tf_op jit(solution)/shard_map/ppermute | solution.py:226
  77.4 1.9 %collective-permute-start.4 = (bf16[2,128,256]{2,1,0:T(8,128)(2,1)S(1)}, bf16[2,128,256]{2,1,0:T(8,128)(2,1)S(1)}, u32[]{:S(2)}, u32[]{:S(2)}) collective-permute-start(bf16[2,128,256]{2,1,0:T(8,128)(2,1)S(1)} %get-tuple-element.24), channel_id=1, source_target_pairs={{0,1},{1,0},{2,3},{3,2},{4,5},{5,4},{6,7},{7,6},{8,9},{9,8},{10,11... | collective-permute-start | bytes 393224 | tf_op jit(solution)/shard_map/ppermute | solution.py:226
  79.3 3.8 %collective-permute-done.3 = bf16[2,128,256]{2,1,0:T(8,128)(2,1)S(1)} collective-permute-done((bf16[2,128,256]{2,1,0:T(8,128)(2,1)S(1)}, bf16[2,128,256]{2,1,0:T(8,128)(2,1)S(1)}, u32[]{:S(2)}, u32[]{:S(2)}) %collective-permute-start.3) | collective-permute-done | bytes 131104 | tf_op jit(solution)/shard_map/ppermute | solution.py:226
  83.1 0.3 collective-permute-done.4
  83.4 0.7 add_bitcast_fusion
Async XLA Ops:
  0.0 20.2 %copy-start.6 = (f32[128,128]{1,0:T(8,128)S(1)}, f32[128,128]{1,0:T(8,128)}, u32[]{:S(2)}) copy-start(f32[128,128]{1,0:T(8,128)} %phase_ref.1) | copy-start | bytes 196612
  1.7 18.4 %collective-permute-start = (bf16[16,256]{1,0:T(8,128)(2,1)}, bf16[16,256]{1,0:T(8,128)(2,1)S(1)}, u32[]{:S(2)}, u32[]{:S(2)}) collective-permute-start(bf16[16,256]{1,0:T(8,128)(2,1)} %get-tuple-element.15.note_ref), channel_id=1, source_target_pairs={{0,2},{1,3},{2,4},{3,5},{4,6},{5,7},{6,8},{7,9},{8,10},{9,11},{10,... | collective-permute-start | bytes 24584 | tf_op jit(solution)/shard_map/ppermute | solution.py:252
  7.5 19.9 %copy-start = (bf16[1,2,128,256]{3,2,1,0:T(8,128)(2,1)S(1)}, bf16[1,2,128,256]{3,2,1,0:T(8,128)(2,1)}, u32[]{:S(2)}) copy-start(bf16[1,2,128,256]{3,2,1,0:T(8,128)(2,1)} %param.8) | copy-start | bytes 393220
  7.5 19.9 %copy-start.1 = (bf16[1,2,128,256]{3,2,1,0:T(8,128)(2,1)S(1)}, bf16[1,2,128,256]{3,2,1,0:T(8,128)(2,1)}, u32[]{:S(2)}) copy-start(bf16[1,2,128,256]{3,2,1,0:T(8,128)(2,1)} %param.9) | copy-start | bytes 393220
  7.5 19.9 %copy-start.5 = (bf16[16,256]{1,0:T(8,128)(2,1)S(1)}, bf16[16,256]{1,0:T(8,128)(2,1)}, u32[]{:S(2)}) copy-start(bf16[16,256]{1,0:T(8,128)(2,1)} %get-tuple-element.15.note_ref) | copy-start | bytes 24580
  7.5 17.1 %collective-permute-start.2 = (bf16[528,256]{1,0:T(8,128)(2,1)}, bf16[528,256]{1,0:T(8,128)(2,1)S(1)}, u32[]{:S(2)}, u32[]{:S(2)}) collective-permute-start(bf16[528,256]{1,0:T(8,128)(2,1)} %get-tuple-element.17), channel_id=1, source_target_pairs={{0,63},{1,2},{2,1},{3,4},{4,3},{5,6},{6,5},{7,8},{8,7},{9,10},{10,... | collective-permute-start | bytes 811016 | tf_op jit(solution)/shard_map/ppermute | solution.py:226
  18.3 9.1 %collective-permute-start.1 = (bf16[528,256]{1,0:T(8,128)(2,1)}, bf16[528,256]{1,0:T(8,128)(2,1)S(1)}, u32[]{:S(2)}, u32[]{:S(2)}) collective-permute-start(bf16[528,256]{1,0:T(8,128)(2,1)} %get-tuple-element.17), channel_id=1, source_target_pairs={{0,1},{1,0},{2,3},{3,2},{4,5},{5,4},{6,7},{7,6},{8,9},{9,8},{10,11... | collective-permute-start | bytes 811016 | tf_op jit(solution)/shard_map/ppermute | solution.py:226
  29.4 21.2 %copy-start.2 = (bf16[256,256]{1,0:T(8,128)(2,1)S(1)}, bf16[256,256]{1,0:T(8,128)(2,1)}, u32[]{:S(2)}) copy-start(bf16[256,256]{1,0:T(8,128)(2,1)} %constant.5.clone.minus_ref) | copy-start | bytes 393220
  29.4 21.2 %copy-start.3 = (bf16[256,256]{1,0:T(8,128)(2,1)S(1)}, bf16[256,256]{1,0:T(8,128)(2,1)}, u32[]{:S(2)}) copy-start(bf16[256,256]{1,0:T(8,128)(2,1)} %constant.4.clone.plus_ref) | copy-start | bytes 393220
  29.4 21.2 %copy-start.4 = (bf16[2,128,128]{2,1,0:T(8,128)(2,1)S(1)}, bf16[2,128,128]{2,1,0:T(8,128)(2,1)}, u32[]{:S(2)}) copy-start(bf16[2,128,128]{2,1,0:T(8,128)(2,1)} %probe_ref.1) | copy-start | bytes 196612
  74.1 9.0 %collective-permute-start.3 = (bf16[2,128,256]{2,1,0:T(8,128)(2,1)S(1)}, bf16[2,128,256]{2,1,0:T(8,128)(2,1)S(1)}, u32[]{:S(2)}, u32[]{:S(2)}) collective-permute-start(bf16[2,128,256]{2,1,0:T(8,128)(2,1)S(1)} %get-tuple-element.23), channel_id=1, source_target_pairs={{0,63},{1,2},{2,1},{3,4},{4,3},{5,6},{6,5},{7,8},{8,7},{9,10},{10,... | collective-permute-start | bytes 393224 | tf_op jit(solution)/shard_map/ppermute | solution.py:226
  77.4 6.0 %collective-permute-start.4 = (bf16[2,128,256]{2,1,0:T(8,128)(2,1)S(1)}, bf16[2,128,256]{2,1,0:T(8,128)(2,1)S(1)}, u32[]{:S(2)}, u32[]{:S(2)}) collective-permute-start(bf16[2,128,256]{2,1,0:T(8,128)(2,1)S(1)} %get-tuple-element.24), channel_id=1, source_target_pairs={{0,1},{1,0},{2,3},{3,2},{4,5},{5,4},{6,7},{7,6},{8,9},{9,8},{10,11... | collective-permute-start | bytes 393224 | tf_op jit(solution)/shard_map/ppermute | solution.py:226

commit v4 on v3

--- a/solution.py
+++ b/solution.py
@@ -12,6 +12,7 @@
 
 REACH = 2
 NOTE_ROWS = 16
+OWNERS = (-REACH, 0, 1)
 STRETCH = 1.6236604965019064
 BF16 = jnp.bfloat16
 F32 = jnp.float32
@@ -71,7 +72,7 @@
         inside = row_ref[position] - (strip_index - REACH) * strip_rows
         inside = lax.rem(inside + 2 * total_rows, total_rows)
         ahead = 2 * REACH - lax.div(inside, strip_rows) - REACH
-        to_owner = ahead - jnp.clip(ahead, 0, 1)
+        to_owner = jnp.where(ahead < 0, -REACH, jnp.where(ahead == REACH, 1, 0))
         first_row = inside + (to_owner + 1 - REACH) * strip_rows
         for place, value in enumerate((first_row, col_ref[position], to_owner)):
             note = jnp.where(lane == place * near + position, value.astype(F32), note)
@@ -88,25 +89,58 @@
     sin_ref[...] = jnp.sin(phase_ref[...])
 
 
-def cut_kernel(rows, far_ref, note_ref, object_ref, direction_ref, second_ref, first_ref, out_ref, start_ref):
+def strips_around(first_ref, own, second_ref):
     even = lax.rem(lax.axis_index("strip"), 2) == 0
     first, second = first_ref[...], second_ref[...]
-    above, below = jnp.where(even, first, second), jnp.where(even, second, first)
+    return jnp.where(even, first, second), own, jnp.where(even, second, first)
+
+
+def corners_here(rows, far, own, below, near):
+    found = []
+    for note, owner in zip((far, own, below), OWNERS):
+        note = note[note.shape[0] - NOTE_ROWS :, :].astype(F32)[0:1]
+        for position in range(near):
+            here = note[:, 2 * near + position : 2 * near + position + 1] == owner
+            first_row = note[:, position : position + 1]
+            first_col = note[:, near + position : near + position + 1]
+            found.append((jnp.where(here, 1.0, 0.0), first_row, first_col))
+    return found
+
+
+def count_kernel(rows, near, far_ref, note_ref, second_ref, first_ref, out_ref):
+    even = lax.rem(lax.axis_index("strip"), 2) == 0
+    below = jnp.where(even, second_ref[...], first_ref[...])
+    found = corners_here(rows, far_ref[...], note_ref[...], below, near)
+    out_ref[0] = jnp.sum(sum(here for here, _, _ in found)).astype(jnp.int32)
+
+
+def cut_kernel(
+    rows, near, packed, far_ref, note_ref, object_ref, direction_ref, second_ref, first_ref, out_ref, start_ref
+):
+    targets, parts, size, wide = out_ref.shape
+    columns = object_ref.shape[1]
     own = jnp.concatenate([object_ref[...], direction_ref[...], note_ref[...]], axis=0)
-    slots, parts, size, _ = out_ref.shape
-    columns = object_ref.shape[1]
-    near = slots // 4
+    above, own, below = strips_around(first_ref, own, second_ref)
+    found = corners_here(rows, far_ref[...], own, below, near)
+    nowhere = 4.0 * rows
+    if packed:
+        slots = targets // 2
+        starts = [[nowhere, 0.0] for _ in range(slots)]
+        rank = jnp.zeros((1, 1), F32)
+        for here, first_row, first_col in found:
+            for slot in range(slots):
+                taken = here * jnp.where(rank == slot, 1.0, 0.0) > 0.0
+                starts[slot][0] = jnp.where(taken, first_row, starts[slot][0])
+                starts[slot][1] = jnp.where(taken, first_col, starts[slot][1])
+            rank += here
+    else:
+        slots = len(found)
+        starts = [[jnp.where(here > 0.0, row, nowhere), col] for here, row, col in found]
     hots = []
-    for owner, block in enumerate((far_ref[...], above, own, below)):
-        note = block[block.shape[0] - NOTE_ROWS :, :].astype(F32)[0:1]
-        for position in range(near):
-            here = note[:, 2 * near + position : 2 * near + position + 1] == owner - REACH
-            first_row = jnp.where(here, note[:, position : position + 1], 4.0 * rows)
-            first_col = note[:, near + position : near + position + 1]
-            slot = owner * near + position
-            start_ref[2 * slot : 2 * slot + 1, :] = jnp.broadcast_to(first_row, (1, 128))
-            start_ref[2 * slot + 1 : 2 * slot + 2, :] = jnp.broadcast_to(first_col, (1, 128))
-            hots.append((row_hot(first_row, size, 3 * rows), col_hot(first_col, columns, size)))
+    for slot, (first_row, first_col) in enumerate(starts):
+        start_ref[2 * slot : 2 * slot + 1, :] = jnp.broadcast_to(first_row, (1, 128))
+        start_ref[2 * slot + 1 : 2 * slot + 2, :] = jnp.broadcast_to(first_col, (1, 128))
+        hots.append((row_hot(first_row, wide, 3 * rows), col_hot(first_col, columns, wide)))
     bands = [
         jnp.concatenate(
             [block[part * rows : (part + 1) * rows, :] for block in (above, own, below)], axis=0
@@ -116,15 +150,33 @@
     pick_rows = jnp.concatenate([hot for hot, _ in hots], axis=0)
     picked = [dot(pick_rows, band).astype(BF16) for band in bands]
     for slot in range(slots):
-        lines = [part[slot * size : (slot + 1) * size] for part in picked]
-        window = dot(jnp.concatenate(lines, axis=0), hots[slot][1]).astype(BF16)
-        out_ref[slot] = window.reshape(parts, size, size)
-
-
-def chain_kernel(unit, window_ref, probe_ref, cos_ref, sin_ref, plus_ref, minus_ref, out_ref, wave_ref):
-    slices = window_ref.shape[0]
-    size = window_ref.shape[2]
+        lines = [part[slot * wide : (slot + 1) * wide] for part in picked]
+        window = dot(jnp.concatenate(lines, axis=0), hots[slot][1]).astype(BF16).reshape(parts, wide, wide)
+        if packed:
+            out_ref[2 * slot] = window[:, :size]
+            out_ref[2 * slot + 1] = window[:, size:]
+        else:
+            out_ref[slot] = window
+    if not packed:
+        out_ref[slots:] = jnp.zeros((targets - slots, parts, size, wide), BF16)
+
+
+def chain_kernel(unit, window_ref, other_ref, probe_ref, cos_ref, sin_ref, plus_ref, minus_ref, out_ref, wave_ref):
+    slices, _, rows_out, size = out_ref.shape
+    packed = rows_out < size
     plus, minus = plus_ref[...], minus_ref[...]
+
+    even = lax.rem(lax.axis_index("cuts"), 2) == 0
+
+    def window(layer, part):
+        mine = window_ref[layer, part].astype(F32)
+        if not packed:
+            return mine
+        other = other_ref[layer, part].astype(F32)
+        return jnp.concatenate([jnp.where(even, mine, other), jnp.where(even, other, mine)], axis=0)
+
+    def kept(values):
+        return jnp.where(even, values[:rows_out], values[rows_out:]) if packed else values
 
     def swap(values, waves):
         blocks = [[values[i * size : (i + 1) * size, j * size : (j + 1) * size]
@@ -155,8 +207,8 @@
     hop_scale = 1.0 / unit**4
     for layer in range(slices):
         wave_ref[layer, 0], wave_ref[layer, 1] = psi_re, psi_im
-        obj_re, obj_im = window_ref[layer, 0].astype(F32), window_ref[layer, 1].astype(F32)
-        dir_re, dir_im = window_ref[layer, 2].astype(F32), window_ref[layer, 3].astype(F32)
+        obj_re, obj_im = window(layer, 0), window(layer, 1)
+        dir_re, dir_im = window(layer, 2), window(layer, 3)
         exit_re = obj_re * psi_re - obj_im * psi_im
         exit_im = obj_re * psi_im + obj_im * psi_re
         delta_re = dir_re * psi_re - dir_im * psi_im
@@ -181,17 +233,21 @@
     for layer in range(slices - 1, -1, -1):
         adj_re, adj_im = adjoint[:size], adjoint[size:]
         psi_re, psi_im = wave_ref[layer, 0], wave_ref[layer, 1]
-        out_ref[layer, 0] = (psi_re * adj_re + psi_im * adj_im).astype(BF16)
-        out_ref[layer, 1] = (psi_re * adj_im - psi_im * adj_re).astype(BF16)
+        psi_re, psi_im = kept(psi_re), kept(psi_im)
+        out_re, out_im = kept(adj_re), kept(adj_im)
+        out_ref[layer, 0] = (psi_re * out_re + psi_im * out_im).astype(BF16)
+        out_ref[layer, 1] = (psi_re * out_im - psi_im * out_re).astype(BF16)
         if layer > 0:
-            obj_re, obj_im = window_ref[layer, 0].astype(F32), window_ref[layer, 1].astype(F32)
+            obj_re, obj_im = window(layer, 0), window(layer, 1)
             columns = jnp.concatenate(
                 [obj_re * adj_re + obj_im * adj_im, obj_re * adj_im - obj_im * adj_re], axis=0)
             adjoint = inverse(kernel_times(forward(columns), -1.0, hop_scale))
 
 
-def gather_kernel(start_ref, grad_ref, first_ref, own_ref, second_ref):
-    slots, parts, size, _ = grad_ref.shape
+def gather_kernel(slots, start_ref, grad_ref, first_ref, own_ref, second_ref):
+    senders, parts, rows_in, size = grad_ref.shape
+    packed = rows_in < size
+    slots = senders // 2 if packed else slots
     rows, columns = own_ref.shape[1:]
     even = lax.rem(lax.axis_index("strip"), 2) == 0
     placed = [[] for _ in range(parts)]
@@ -200,7 +256,11 @@
         first_row = start_ref[2 * slot : 2 * slot + 1, 0:1]
         first_col = start_ref[2 * slot + 1 : 2 * slot + 2, 0:1]
         hots.append(col_hot(first_row, 3 * rows, size))
-        values = grad_ref[slot].reshape(parts * size, size)
+        if packed:
+            halves = [grad_ref[2 * slot + core, part] for part in range(parts) for core in range(2)]
+            values = jnp.concatenate(halves, axis=0)
+        else:
+            values = grad_ref[slot].reshape(parts * size, size)
         spread = dot(values, row_hot(first_col, size, columns)).astype(BF16)
         for part in range(parts):
             placed[part].append(spread[part * size : (part + 1) * size])
@@ -264,41 +324,63 @@
         cost_estimate=pl.CostEstimate(flops=20_000_000_000, bytes_accessed=100_000_000, transcendentals=0),
         name="phase_tables",
     )(far, kernel_phase)
-    windows, start = pl.pallas_call(
-        functools.partial(cut_kernel, strip_rows),
-        out_shape=(
-            jax.ShapeDtypeStruct((cuts_count, 4, patch_size, patch_size), BF16),
-            jax.ShapeDtypeStruct((2 * cuts_count, 128), F32),
-        ),
-        in_specs=[vmem] * 6,
-        out_specs=(vmem, vmem),
+    near = corner_row.shape[0]
+    strip_shape = (2, strip_rows, column_count)
+
+    def work(packed, far, note, objects, directions, first, second, probe_wave, kernel_cos, kernel_sin, plus, minus):
+        rows_sent = patch_size // 2 if packed else patch_size
+        windows, start = pl.pallas_call(
+            functools.partial(cut_kernel, strip_rows, near, packed),
+            out_shape=(
+                jax.ShapeDtypeStruct((cuts_count, 4, rows_sent, patch_size), BF16),
+                jax.ShapeDtypeStruct((2 * cuts_count, 128), F32),
+            ),
+            in_specs=[vmem] * 6,
+            out_specs=(vmem, vmem),
+            compiler_params=params,
+            name="cut_windows",
+        )(far, note, objects, directions, second, first)
+        other = windows = lax.all_to_all(windows, "cuts", 0, 0, tiled=False)
+        if packed:
+            other = lax.ppermute(windows, "cuts", [(i, i ^ 1) for i in range(cuts_count)])
+        gradient = pl.pallas_call(
+            functools.partial(chain_kernel, unit),
+            out_shape=jax.ShapeDtypeStruct((cuts_count, 2, rows_sent, patch_size), BF16),
+            in_specs=[vmem] * 7,
+            out_specs=vmem,
+            scratch_shapes=[pltpu.VMEM((cuts_count, 2, patch_size, patch_size), F32)],
+            compiler_params=params,
+            name="wave_chain",
+        )(windows, other, probe_wave, kernel_cos, kernel_sin, plus, minus)
+        gradient = lax.all_to_all(gradient, "cuts", 0, 0, tiled=False)
+        return pl.pallas_call(
+            functools.partial(gather_kernel, len(OWNERS) * near),
+            out_shape=(
+                jax.ShapeDtypeStruct(strip_shape, BF16),
+                jax.ShapeDtypeStruct(strip_shape, F32),
+                jax.ShapeDtypeStruct(strip_shape, BF16),
+            ),
+            in_specs=[vmem, vmem],
+            out_specs=(vmem, vmem, vmem),
+            compiler_params=params,
+            name="add_windows",
+        )(start, gradient)
+
+    count = pl.pallas_call(
+        functools.partial(count_kernel, strip_rows, near),
+        out_shape=jax.ShapeDtypeStruct((1,), jnp.int32),
+        in_specs=[vmem] * 4,
+        out_specs=pl.BlockSpec(memory_space=pltpu.SMEM),
         compiler_params=params,
-        name="cut_windows",
-    )(far, note, objects, directions, second, first)
-    windows = lax.all_to_all(windows, "cuts", 0, 0, tiled=False)
-    gradient = pl.pallas_call(
-        functools.partial(chain_kernel, unit),
-        out_shape=jax.ShapeDtypeStruct((cuts_count, 2, patch_size, patch_size), BF16),
-        in_specs=[vmem] * 6,
-        out_specs=vmem,
-        scratch_shapes=[pltpu.VMEM((cuts_count, 2, patch_size, patch_size), F32)],
-        compiler_params=params,
-        name="wave_chain",
-    )(windows, probe_wave, kernel_cos, kernel_sin, jnp.asarray(plus), jnp.asarray(minus))
-    gradient = lax.all_to_all(gradient, "cuts", 0, 0, tiled=False)
-    strip_shape = (2, strip_rows, column_count)
-    first, own, second = pl.pallas_call(
-        gather_kernel,
-        out_shape=(
-            jax.ShapeDtypeStruct(strip_shape, BF16),
-            jax.ShapeDtypeStruct(strip_shape, F32),
-            jax.ShapeDtypeStruct(strip_shape, BF16),
-        ),
-        in_specs=[vmem, vmem],
-        out_specs=(vmem, vmem, vmem),
-        compiler_params=params,
-        name="add_windows",
-    )(start, gradient)
+        name="count_positions",
+    )(far, note, second, first)
+    first, own, second = lax.cond(
+        count[0] > cuts_count // 2,
+        functools.partial(work, False),
+        functools.partial(work, True),
+        far, note, objects, directions, first, second,
+        probe_wave, kernel_cos, kernel_sin, jnp.asarray(plus), jnp.asarray(minus),
+    )
     first, second = exchanged(first, -1), exchanged(second, 0)
     return (own + first.astype(F32) + second.astype(F32))[None]
 

time: 84.5 us -> 85 us (level)
  blocking collectives: 34 us -> 24.6 us
  starting transfers between devices: 23.6 us -> 31.2 us
  waiting for transfers between devices: 10.8 us -> 12 us
    all_to_all x2, blocking collectives: 34 us -> 24.6 us  [the longest x1 15.3 us: work(): other = windows = lax.all_to_all(windows, 'cuts', 0, 0, tiled=False)]
    ppermute x4, starting transfers between devices: 17.9 us -> 22.6 us  [exchanged(): lax.ppermute(block, 'strip', [(i, j % strip_count) for i, j in route])]
    ppermute x0 -> x1, starting transfers between devices: none -> 2.94 us  [work(): lax.ppermute(windows, 'cuts', [(i, i ^ 1) for i in range(cuts_count)])]
    ppermute x0 -> x1, waiting for transfers between devices: none -> 1.51 us  [work(): lax.ppermute(windows, 'cuts', [(i, i ^ 1) for i in range(cuts_count)])]
    pallas_call x3 -> x4, Pallas kernels: 12.7 us -> 12.8 us  [the longest x1 9.9 us: work(): pl.pallas_call(functools.partial(chain_kernel, unit), out_shape=jax.Shape...]
  transfers between devices with their start and end apart: 5 -> 6, of which waited for: 4 -> 5; matrix products, arithmetic and copies ran while one was open for 0% -> 0% of each run, Pallas kernels for 1% -> 1%
where the time goes in v4:
time: 85 us; the launch traced here: 84.6 us
  starting transfers between devices  31.2 us (37%)
  blocking collectives  24.6 us (29%)
  Pallas kernels  14.9 us (18%)
  waiting for transfers between devices  12 us (14%)
    ppermute x4, starting transfers between devices, exchanged(): lax.ppermute(block, 'strip', [(i, j % strip_count) for i, j in route])  22.6 us
    all_to_all x1, blocking collectives, work(): other = windows = lax.all_to_all(windows, 'cuts', 0, 0, tiled=False)  15.3 us
    ppermute x4, waiting for transfers between devices, exchanged(): lax.ppermute(block, 'strip', [(i, j % strip_count) for i, j in route])  10.5 us
    pallas_call x1, Pallas kernels, work(): pl.pallas_call(functools.partial(chain_kernel, unit), out_shape=jax.Shape...  9.9 us
    all_to_all x1, blocking collectives, work(): gradient = lax.all_to_all(gradient, 'cuts', 0, 0, tiled=False)  9.28 us
    ppermute x1, starting transfers between devices, on_device(): lax.ppermute(note, 'strip', [(i, (i + REACH) % strip_count) for i in rang...  5.73 us
    ppermute x1, starting transfers between devices, work(): lax.ppermute(windows, 'cuts', [(i, i ^ 1) for i in range(cuts_count)])  2.94 us
    pallas_call x1, Pallas kernels, on_device(): pl.pallas_call(functools.partial(pack_kernel, strip_rows, strip_count * s...  1.74 us
  transfers between devices with their start and end apart: 6, of which 5 were waited for; matrix products, arithmetic and copies ran while one was open for 0% of the time, Pallas kernels for 1%

profile of v4, /device:TPU:1, one launch (start us, length us, event | category | flops | bytes accessed | tf_op | source)
XLA Modules:
  0.0 84.6 jit_solution(10193192261641296009)
XLA Ops:
  0.0 0.0 copy-start
  0.0 1.7 %pack_block.1 = (bf16[528,256]{1,0:T(8,128)(2,1)}, bf16[16,256]{1,0:T(8,128)(2,1)S(1)}) custom-call(s32[2]{0:T(128)} %row_any.1, s32[2]{0:T(128)} %col_any.1, bf16[256,256]{1,0:T(8,128)(2,1)} %bitcast.5, bf16[256,256]{1,0:T(8,128)(2,1)} %bitcast.8), custom_call_target="tpu_custom_call" | custom-call | tf_op jit(solution)/shard_map/pack_block/pallas_call | solution.py:296
  1.7 5.7 %collective-permute-start.1 = (bf16[16,256]{1,0:T(8,128)(2,1)S(1)}, bf16[16,256]{1,0:T(8,128)(2,1)S(1)}, u32[]{:S(2)}, u32[]{:S(2)}) collective-permute-start(bf16[16,256]{1,0:T(8,128)(2,1)S(1)} %get-tuple-element.83.note_ref), channel_id=1, source_target_pairs={{0,2},{1,3},{2,4},{3,5},{4,6},{5,7},{6,8},{7,9},{8,10},{9,11},{10,... | collective-permute-start | bytes 24584 | tf_op jit(solution)/shard_map/ppermute | solution.py:312
  7.5 10.6 %collective-permute-start.3 = (bf16[528,256]{1,0:T(8,128)(2,1)}, bf16[528,256]{1,0:T(8,128)(2,1)S(1)}, u32[]{:S(2)}, u32[]{:S(2)}) collective-permute-start(bf16[528,256]{1,0:T(8,128)(2,1)} %get-tuple-element.85), channel_id=1, source_target_pairs={{0,63},{1,2},{2,1},{3,4},{4,3},{5,6},{6,5},{7,8},{8,7},{9,10},{10,... | collective-permute-start | bytes 811016 | tf_op jit(solution)/shard_map/ppermute | solution.py:286
  18.1 1.9 %collective-permute-start.2 = (bf16[528,256]{1,0:T(8,128)(2,1)}, bf16[528,256]{1,0:T(8,128)(2,1)S(1)}, u32[]{:S(2)}, u32[]{:S(2)}) collective-permute-start(bf16[528,256]{1,0:T(8,128)(2,1)} %get-tuple-element.85), channel_id=1, source_target_pairs={{0,1},{1,0},{2,3},{3,2},{4,5},{5,4},{6,7},{7,6},{8,9},{9,8},{10,11... | collective-permute-start | bytes 811016 | tf_op jit(solution)/shard_map/ppermute | solution.py:286
  20.0 0.0 collective-permute-done.1.note_ref
  20.0 0.0 copy-done
  20.0 0.0 copy-start.5
  20.0 0.4 phase_tables.1
  20.5 4.0 %collective-permute-done.3.first_ref = bf16[528,256]{1,0:T(8,128)(2,1)S(1)} collective-permute-done((bf16[528,256]{1,0:T(8,128)(2,1)}, bf16[528,256]{1,0:T(8,128)(2,1)S(1)}, u32[]{:S(2)}, u32[]{:S(2)}) %collective-permute-start.3) | collective-permute-done | bytes 270368 | tf_op jit(solution)/shard_map/ppermute | solution.py:286
  24.5 2.7 %collective-permute-done.2.second_ref = bf16[528,256]{1,0:T(8,128)(2,1)S(1)} collective-permute-done((bf16[528,256]{1,0:T(8,128)(2,1)}, bf16[528,256]{1,0:T(8,128)(2,1)S(1)}, u32[]{:S(2)}, u32[]{:S(2)}) %collective-permute-start.2) | collective-permute-done | bytes 270368 | tf_op jit(solution)/shard_map/ppermute | solution.py:286
  27.2 0.0 copy-start.1
  27.2 0.0 copy-start.2
  27.2 0.7 count_positions.1
  28.6 0.0 copy-done.5
  28.6 0.0 copy-done.1
  28.6 0.0 copy-done.2
  28.6 0.0 copy-done.3
  28.6 0.0 copy-done.4
  28.6 41.4 %conditional.1 = ((bf16[2,128,256]{2,1,0:T(8,128)(2,1)S(1)}, f32[2,128,256]{2,1,0:T(8,128)S(1)}, bf16[2,128,256]{2,1,0:T(8,128)(2,1)S(1)})) conditional(s32[]{:T(128)} %bitcast.2, (bf16[16,256]{1,0:T(8,128)(2,1)S(1)}, bf16[16,256]{1,0:T(8,128)(2,1)S(1)}, bf16[256,256]{1,0:T(8,128)(2,1)S(1)}, bf16[256,256]{1,0:T(8,128)(2,1)S(1)}, ...), branch_computations={%region_0.0_spmd, %region_1.0_spmd} | conditional | bytes 3670064 | solution.py:377
  28.7 1.6 %cut_windows.2 = (bf16[8,4,64,128]{3,2,1,0:T(8,128)(2,1)S(1)}, f32[16,128]{1,0:T(8,128)S(1)}) custom-call(bf16[16,256]{1,0:T(8,128)(2,1)S(1)} %get-tuple-element.49.far_ref, bf16[16,256]{1,0:T(8,128)(2,1)S(1)} %get-tuple-element.50.note_ref, bf16[256,256]{1,0:T(8,128)(2,1)S(1)} %get-tuple-element.51.object_ref, ...), custom_call_target="tpu_custom_call" | custom-call | tf_op jit(solution)/shard_map/cond/branch_0_fun/cut_windows/pallas_call | solution.py:332
  30.2 15.3 %all_to_all.16.window_ref = bf16[8,4,64,128]{3,2,1,0:T(8,128)(2,1)S(1)} all-to-all(bf16[8,4,64,128]{3,2,1,0:T(8,128)(2,1)S(1)} %get-tuple-element.56), channel_id=1, replica_groups=mesh['cuts'=8,'strip'=64] {'cuts'}, dimensions={0} | all-to-all | bytes 1048576 | tf_op jit(solution)/shard_map/cond/branch_0_fun/all_to_all | solution.py:343
  45.5 2.9 %collective-permute-start = (bf16[8,4,64,128]{3,2,1,0:T(8,128)(2,1)S(1)}, bf16[8,4,64,128]{3,2,1,0:T(8,128)(2,1)S(1)}, u32[]{:S(2)}, u32[]{:S(2)}) collective-permute-start(bf16[8,4,64,128]{3,2,1,0:T(8,128)(2,1)S(1)} %all_to_all.16.window_ref), channel_id=1, source_target_pairs={{0,64},{64,0},{128,192},{192,128},{256,320},{320,256},{384,448},{4... | collective-permute-start | bytes 1572872 | tf_op jit(solution)/shard_map/cond/branch_0_fun/ppermute | solution.py:345
  48.5 1.5 %collective-permute-done.other_ref = bf16[8,4,64,128]{3,2,1,0:T(8,128)(2,1)S(1)} collective-permute-done((bf16[8,4,64,128]{3,2,1,0:T(8,128)(2,1)S(1)}, bf16[8,4,64,128]{3,2,1,0:T(8,128)(2,1)S(1)}, u32[]{:S(2)}, u32[]{:S(2)}) %collective-permute-start) | collective-permute-done | bytes 524320 | tf_op jit(solution)/shard_map/cond/branch_0_fun/ppermute | solution.py:345
  50.0 9.9 %wave_chain.2 = bf16[8,2,64,128]{3,2,1,0:T(8,128)(2,1)S(1)} custom-call(bf16[8,4,64,128]{3,2,1,0:T(8,128)(2,1)S(1)} %all_to_all.16.window_ref, bf16[8,4,64,128]{3,2,1,0:T(8,128)(2,1)S(1)} %collective-permute-done.other_ref, bf16[2,128,128]{2,1,0:T(8,128)(2,1)S(1)} %get-tuple-element.57.probe_ref, f32[128,128]{1,0:T(8,128)S(1)} %get-tuple-element.58.cos_ref, ...), custom_call_target="tpu_custom_call" | custom-call | tf_op jit(solution)/shard_map/cond/branch_0_fun/wave_chain/pallas_call | solution.py:346
  59.9 9.3 %all_to_all.17.grad_ref = bf16[8,2,64,128]{3,2,1,0:T(8,128)(2,1)S(1)} all-to-all(bf16[8,2,64,128]{3,2,1,0:T(8,128)(2,1)S(1)} %wave_chain.2), channel_id=1, replica_groups=mesh['cuts'=8,'strip'=64] {'cuts'}, dimensions={0} | all-to-all | bytes 524288 | tf_op jit(solution)/shard_map/cond/branch_0_fun/all_to_all | solution.py:355
  69.2 0.6 add_windows.2
  70.0 8.1 %collective-permute-start.4 = (bf16[2,128,256]{2,1,0:T(8,128)(2,1)S(1)}, bf16[2,128,256]{2,1,0:T(8,128)(2,1)S(1)}, u32[]{:S(2)}, u32[]{:S(2)}) collective-permute-start(bf16[2,128,256]{2,1,0:T(8,128)(2,1)S(1)} %get-tuple-element.89), channel_id=1, source_target_pairs={{0,63},{1,2},{2,1},{3,4},{4,3},{5,6},{6,5},{7,8},{8,7},{9,10},{10,... | collective-permute-start | bytes 393224 | tf_op jit(solution)/shard_map/ppermute | solution.py:286
  78.2 1.9 %collective-permute-start.5 = (bf16[2,128,256]{2,1,0:T(8,128)(2,1)S(1)}, bf16[2,128,256]{2,1,0:T(8,128)(2,1)S(1)}, u32[]{:S(2)}, u32[]{:S(2)}) collective-permute-start(bf16[2,128,256]{2,1,0:T(8,128)(2,1)S(1)} %get-tuple-element.90), channel_id=1, source_target_pairs={{0,1},{1,0},{2,3},{3,2},{4,5},{5,4},{6,7},{7,6},{8,9},{9,8},{10,11... | collective-permute-start | bytes 393224 | tf_op jit(solution)/shard_map/ppermute | solution.py:286
  80.1 0.9 %collective-permute-done.4 = bf16[2,128,256]{2,1,0:T(8,128)(2,1)S(1)} collective-permute-done((bf16[2,128,256]{2,1,0:T(8,128)(2,1)S(1)}, bf16[2,128,256]{2,1,0:T(8,128)(2,1)S(1)}, u32[]{:S(2)}, u32[]{:S(2)}) %collective-permute-start.4) | collective-permute-done | bytes 131104 | tf_op jit(solution)/shard_map/ppermute | solution.py:286
  81.0 2.9 %collective-permute-done.5 = bf16[2,128,256]{2,1,0:T(8,128)(2,1)S(1)} collective-permute-done((bf16[2,128,256]{2,1,0:T(8,128)(2,1)S(1)}, bf16[2,128,256]{2,1,0:T(8,128)(2,1)S(1)}, u32[]{:S(2)}, u32[]{:S(2)}) %collective-permute-start.5) | collective-permute-done | bytes 131104 | tf_op jit(solution)/shard_map/ppermute | solution.py:286
  83.9 0.7 add_bitcast_fusion
  (2 shorter events, 0.0 us)
Async XLA Ops:
  0.0 20.0 %copy-start = (f32[128,128]{1,0:T(8,128)S(1)}, f32[128,128]{1,0:T(8,128)}, u32[]{:S(2)}) copy-start(f32[128,128]{1,0:T(8,128)} %phase_ref.1) | copy-start | bytes 196612
  1.7 18.3 %collective-permute-start.1 = (bf16[16,256]{1,0:T(8,128)(2,1)S(1)}, bf16[16,256]{1,0:T(8,128)(2,1)S(1)}, u32[]{:S(2)}, u32[]{:S(2)}) collective-permute-start(bf16[16,256]{1,0:T(8,128)(2,1)S(1)} %get-tuple-element.83.note_ref), channel_id=1, source_target_pairs={{0,2},{1,3},{2,4},{3,5},{4,6},{5,7},{6,8},{7,9},{8,10},{9,11},{10,... | collective-permute-start | bytes 24584 | tf_op jit(solution)/shard_map/ppermute | solution.py:312
  7.5 17.0 %collective-permute-start.3 = (bf16[528,256]{1,0:T(8,128)(2,1)}, bf16[528,256]{1,0:T(8,128)(2,1)S(1)}, u32[]{:S(2)}, u32[]{:S(2)}) collective-permute-start(bf16[528,256]{1,0:T(8,128)(2,1)} %get-tuple-element.85), channel_id=1, source_target_pairs={{0,63},{1,2},{2,1},{3,4},{4,3},{5,6},{6,5},{7,8},{8,7},{9,10},{10,... | collective-permute-start | bytes 811016 | tf_op jit(solution)/shard_map/ppermute | solution.py:286
  18.1 9.1 %collective-permute-start.2 = (bf16[528,256]{1,0:T(8,128)(2,1)}, bf16[528,256]{1,0:T(8,128)(2,1)S(1)}, u32[]{:S(2)}, u32[]{:S(2)}) collective-permute-start(bf16[528,256]{1,0:T(8,128)(2,1)} %get-tuple-element.85), channel_id=1, source_target_pairs={{0,1},{1,0},{2,3},{3,2},{4,5},{5,4},{6,7},{7,6},{8,9},{9,8},{10,11... | collective-permute-start | bytes 811016 | tf_op jit(solution)/shard_map/ppermute | solution.py:286
  20.0 8.6 %copy-start.5 = (bf16[2,128,128]{2,1,0:T(8,128)(2,1)S(1)}, bf16[2,128,128]{2,1,0:T(8,128)(2,1)}, u32[]{:S(2)}) copy-start(bf16[2,128,128]{2,1,0:T(8,128)(2,1)} %param.12) | copy-start | bytes 196612
  27.2 1.4 %copy-start.1 = (bf16[1,2,128,256]{3,2,1,0:T(8,128)(2,1)S(1)}, bf16[1,2,128,256]{3,2,1,0:T(8,128)(2,1)}, u32[]{:S(2)}) copy-start(bf16[1,2,128,256]{3,2,1,0:T(8,128)(2,1)} %param.10) | copy-start | bytes 393220
  27.2 1.4 %copy-start.2 = (bf16[1,2,128,256]{3,2,1,0:T(8,128)(2,1)S(1)}, bf16[1,2,128,256]{3,2,1,0:T(8,128)(2,1)}, u32[]{:S(2)}) copy-start(bf16[1,2,128,256]{3,2,1,0:T(8,128)(2,1)} %param.11) | copy-start | bytes 393220
  27.2 1.4 %copy-start.3 = (bf16[256,256]{1,0:T(8,128)(2,1)S(1)}, bf16[256,256]{1,0:T(8,128)(2,1)}, u32[]{:S(2)}) copy-start(bf16[256,256]{1,0:T(8,128)(2,1)} %constant.8.clone) | copy-start | bytes 393220
  27.2 1.4 %copy-start.4 = (bf16[256,256]{1,0:T(8,128)(2,1)S(1)}, bf16[256,256]{1,0:T(8,128)(2,1)}, u32[]{:S(2)}) copy-start(bf16[256,256]{1,0:T(8,128)(2,1)} %constant.7.clone) | copy-start | bytes 393220
  45.5 4.5 %collective-permute-start = (bf16[8,4,64,128]{3,2,1,0:T(8,128)(2,1)S(1)}, bf16[8,4,64,128]{3,2,1,0:T(8,128)(2,1)S(1)}, u32[]{:S(2)}, u32[]{:S(2)}) collective-permute-start(bf16[8,4,64,128]{3,2,1,0:T(8,128)(2,1)S(1)} %all_to_all.16.window_ref), channel_id=1, source_target_pairs={{0,64},{64,0},{128,192},{192,128},{256,320},{320,256},{384,448},{4... | collective-permute-start | bytes 1572872 | tf_op jit(solution)/shard_map/cond/branch_0_fun/ppermute | solution.py:345
  70.0 10.9 %collective-permute-start.4 = (bf16[2,128,256]{2,1,0:T(8,128)(2,1)S(1)}, bf16[2,128,256]{2,1,0:T(8,128)(2,1)S(1)}, u32[]{:S(2)}, u32[]{:S(2)}) collective-permute-start(bf16[2,128,256]{2,1,0:T(8,128)(2,1)S(1)} %get-tuple-element.89), channel_id=1, source_target_pairs={{0,63},{1,2},{2,1},{3,4},{4,3},{5,6},{6,5},{7,8},{8,7},{9,10},{10,... | collective-permute-start | bytes 393224 | tf_op jit(solution)/shard_map/ppermute | solution.py:286
  78.2 5.7 %collective-permute-start.5 = (bf16[2,128,256]{2,1,0:T(8,128)(2,1)S(1)}, bf16[2,128,256]{2,1,0:T(8,128)(2,1)S(1)}, u32[]{:S(2)}, u32[]{:S(2)}) collective-permute-start(bf16[2,128,256]{2,1,0:T(8,128)(2,1)S(1)} %get-tuple-element.90), channel_id=1, source_target_pairs={{0,1},{1,0},{2,3},{3,2},{4,5},{5,4},{6,7},{7,6},{8,9},{9,8},{10,11... | collective-permute-start | bytes 393224 | tf_op jit(solution)/shard_map/ppermute | solution.py:286

commit v5 on v4

--- a/solution.py
+++ b/solution.py
@@ -12,7 +12,14 @@
 
 REACH = 2
 NOTE_ROWS = 16
-OWNERS = (-REACH, 0, 1)
+OWNERS = (-REACH, -1, 0, 1)
+PLACES = (
+    ((2, 2), (2, 1), (2, 1), (2, -1), (2, -1)),
+    ((1, 2), (1, 2), (2, 1), (2, -1), (2, -1)),
+    ((1, 2), (1, 2), (0, 1), (1, -1), (1, -1)),
+    ((-1, 2), (-1, 2), (-1, 1), (-1, 0), (0, -1)),
+    ((-1, 2), (-1, 2), (-1, 1), (-1, 0), (-1, -1)),
+)
 STRETCH = 1.6236604965019064
 BF16 = jnp.bfloat16
 F32 = jnp.float32
@@ -66,14 +73,21 @@
         copy.wait()
     strip_index = lax.axis_index("strip")
     near = row_ref.shape[0]
+    insides, aheads = [], []
+    for position in range(near):
+        inside = row_ref[position] - (strip_index - REACH) * strip_rows
+        inside = lax.rem(inside + 2 * total_rows, total_rows)
+        insides.append(inside)
+        aheads.append(REACH - lax.div(inside, strip_rows))
     lane = lax.broadcasted_iota(jnp.int32, (NOTE_ROWS, columns), 1)
     note = jnp.zeros((NOTE_ROWS, columns), F32)
     for position in range(near):
-        inside = row_ref[position] - (strip_index - REACH) * strip_rows
-        inside = lax.rem(inside + 2 * total_rows, total_rows)
-        ahead = 2 * REACH - lax.div(inside, strip_rows) - REACH
-        to_owner = jnp.where(ahead < 0, -REACH, jnp.where(ahead == REACH, 1, 0))
-        first_row = inside + (to_owner + 1 - REACH) * strip_rows
+        to_owner = jnp.int32(0)
+        for row, places in enumerate(PLACES):
+            for column, place in enumerate(places):
+                chosen = (aheads[0] == row - REACH) & (aheads[1] == column - REACH)
+                to_owner = jnp.where(chosen, -place[position], to_owner)
+        first_row = insides[position] + (to_owner + 1 - REACH) * strip_rows
         for place, value in enumerate((first_row, col_ref[position], to_owner)):
             note = jnp.where(lane == place * near + position, value.astype(F32), note)
     note = note.astype(BF16)
@@ -95,9 +109,9 @@
     return jnp.where(even, first, second), own, jnp.where(even, second, first)
 
 
-def corners_here(rows, far, own, below, near):
+def corners_here(far, above, own, below, near):
     found = []
-    for note, owner in zip((far, own, below), OWNERS):
+    for note, owner in zip((far, above, own, below), OWNERS):
         note = note[note.shape[0] - NOTE_ROWS :, :].astype(F32)[0:1]
         for position in range(near):
             here = note[:, 2 * near + position : 2 * near + position + 1] == owner
@@ -107,24 +121,18 @@
     return found
 
 
-def count_kernel(rows, near, far_ref, note_ref, second_ref, first_ref, out_ref):
-    even = lax.rem(lax.axis_index("strip"), 2) == 0
-    below = jnp.where(even, second_ref[...], first_ref[...])
-    found = corners_here(rows, far_ref[...], note_ref[...], below, near)
-    out_ref[0] = jnp.sum(sum(here for here, _, _ in found)).astype(jnp.int32)
-
-
 def cut_kernel(
-    rows, near, packed, far_ref, note_ref, object_ref, direction_ref, second_ref, first_ref, out_ref, start_ref
+    rows, near, far_ref, note_ref, object_ref, direction_ref, second_ref, first_ref, out_ref, start_ref, *count_ref
 ):
-    targets, parts, size, wide = out_ref.shape
+    targets, parts, size, _ = out_ref.shape
     columns = object_ref.shape[1]
     own = jnp.concatenate([object_ref[...], direction_ref[...], note_ref[...]], axis=0)
     above, own, below = strips_around(first_ref, own, second_ref)
-    found = corners_here(rows, far_ref[...], own, below, near)
+    found = corners_here(far_ref[...], above, own, below, near)
     nowhere = 4.0 * rows
-    if packed:
-        slots = targets // 2
+    if count_ref:
+        slots = targets
+        count_ref[0][0] = jnp.sum(sum(here for here, _, _ in found)).astype(jnp.int32)
         starts = [[nowhere, 0.0] for _ in range(slots)]
         rank = jnp.zeros((1, 1), F32)
         for here, first_row, first_col in found:
@@ -140,7 +148,7 @@
     for slot, (first_row, first_col) in enumerate(starts):
         start_ref[2 * slot : 2 * slot + 1, :] = jnp.broadcast_to(first_row, (1, 128))
         start_ref[2 * slot + 1 : 2 * slot + 2, :] = jnp.broadcast_to(first_col, (1, 128))
-        hots.append((row_hot(first_row, wide, 3 * rows), col_hot(first_col, columns, wide)))
+        hots.append((row_hot(first_row, size, 3 * rows), col_hot(first_col, columns, size)))
     bands = [
         jnp.concatenate(
             [block[part * rows : (part + 1) * rows, :] for block in (above, own, below)], axis=0
@@ -150,33 +158,24 @@
     pick_rows = jnp.concatenate([hot for hot, _ in hots], axis=0)
     picked = [dot(pick_rows, band).astype(BF16) for band in bands]
     for slot in range(slots):
-        lines = [part[slot * wide : (slot + 1) * wide] for part in picked]
-        window = dot(jnp.concatenate(lines, axis=0), hots[slot][1]).astype(BF16).reshape(parts, wide, wide)
-        if packed:
-            out_ref[2 * slot] = window[:, :size]
-            out_ref[2 * slot + 1] = window[:, size:]
-        else:
-            out_ref[slot] = window
-    if not packed:
-        out_ref[slots:] = jnp.zeros((targets - slots, parts, size, wide), BF16)
+        lines = [part[slot * size : (slot + 1) * size] for part in picked]
+        window = dot(jnp.concatenate(lines, axis=0), hots[slot][1]).astype(BF16)
+        out_ref[slot] = window.reshape(parts, size, size)
+    if slots < targets:
+        out_ref[slots:] = jnp.zeros((targets - slots, parts, size, size), BF16)
 
 
 def chain_kernel(unit, window_ref, other_ref, probe_ref, cos_ref, sin_ref, plus_ref, minus_ref, out_ref, wave_ref):
-    slices, _, rows_out, size = out_ref.shape
-    packed = rows_out < size
+    slices, _, size, _ = wave_ref.shape
+    packed = window_ref.shape[0] < slices
     plus, minus = plus_ref[...], minus_ref[...]
-
     even = lax.rem(lax.axis_index("cuts"), 2) == 0
 
     def window(layer, part):
-        mine = window_ref[layer, part].astype(F32)
         if not packed:
-            return mine
-        other = other_ref[layer, part].astype(F32)
-        return jnp.concatenate([jnp.where(even, mine, other), jnp.where(even, other, mine)], axis=0)
-
-    def kept(values):
-        return jnp.where(even, values[:rows_out], values[rows_out:]) if packed else values
+            return window_ref[layer, part].astype(F32)
+        mine, other = window_ref[layer // 2, part], other_ref[layer // 2, part]
+        return (jnp.where(even, mine, other) if layer % 2 == 0 else jnp.where(even, other, mine)).astype(F32)
 
     def swap(values, waves):
         blocks = [[values[i * size : (i + 1) * size, j * size : (j + 1) * size]
@@ -233,10 +232,13 @@
     for layer in range(slices - 1, -1, -1):
         adj_re, adj_im = adjoint[:size], adjoint[size:]
         psi_re, psi_im = wave_ref[layer, 0], wave_ref[layer, 1]
-        psi_re, psi_im = kept(psi_re), kept(psi_im)
-        out_re, out_im = kept(adj_re), kept(adj_im)
-        out_ref[layer, 0] = (psi_re * out_re + psi_im * out_im).astype(BF16)
-        out_ref[layer, 1] = (psi_re * out_im - psi_im * out_re).astype(BF16)
+        later = grad if layer < slices - 1 else None
+        grad = [(psi_re * adj_re + psi_im * adj_im).astype(BF16), (psi_re * adj_im - psi_im * adj_re).astype(BF16)]
+        for part in range(2):
+            if not packed:
+                out_ref[layer, part] = grad[part]
+            elif layer % 2 == 0:
+                out_ref[layer // 2, part] = jnp.where(even, grad[part], later[part])
         if layer > 0:
             obj_re, obj_im = window(layer, 0), window(layer, 1)
             columns = jnp.concatenate(
@@ -244,10 +246,9 @@
             adjoint = inverse(kernel_times(forward(columns), -1.0, hop_scale))
 
 
-def gather_kernel(slots, start_ref, grad_ref, first_ref, own_ref, second_ref):
-    senders, parts, rows_in, size = grad_ref.shape
-    packed = rows_in < size
-    slots = senders // 2 if packed else slots
+def gather_kernel(most, start_ref, grad_ref, first_ref, own_ref, second_ref):
+    slots, parts, size, _ = grad_ref.shape
+    slots = min(slots, most)
     rows, columns = own_ref.shape[1:]
     even = lax.rem(lax.axis_index("strip"), 2) == 0
     placed = [[] for _ in range(parts)]
@@ -256,11 +257,7 @@
         first_row = start_ref[2 * slot : 2 * slot + 1, 0:1]
         first_col = start_ref[2 * slot + 1 : 2 * slot + 2, 0:1]
         hots.append(col_hot(first_row, 3 * rows, size))
-        if packed:
-            halves = [grad_ref[2 * slot + core, part] for part in range(parts) for core in range(2)]
-            values = jnp.concatenate(halves, axis=0)
-        else:
-            values = grad_ref[slot].reshape(parts * size, size)
+        values = grad_ref[slot].reshape(parts * size, size)
         spread = dot(values, row_hot(first_col, size, columns)).astype(BF16)
         for part in range(parts):
             placed[part].append(spread[part * size : (part + 1) * size])
@@ -327,32 +324,37 @@
     near = corner_row.shape[0]
     strip_shape = (2, strip_rows, column_count)
 
-    def work(packed, far, note, objects, directions, first, second, probe_wave, kernel_cos, kernel_sin, plus, minus):
-        rows_sent = patch_size // 2 if packed else patch_size
-        windows, start = pl.pallas_call(
-            functools.partial(cut_kernel, strip_rows, near, packed),
-            out_shape=(
-                jax.ShapeDtypeStruct((cuts_count, 4, rows_sent, patch_size), BF16),
-                jax.ShapeDtypeStruct((2 * cuts_count, 128), F32),
-            ),
+    chips = cuts_count // 2
+    same_core = [[core + 2 * chip for chip in range(chips)] for core in range(2)]
+
+    def cut(targets, counted, *operands):
+        windows_shape = (targets, 4, patch_size, patch_size)
+        out_shape = (jax.ShapeDtypeStruct(windows_shape, BF16), jax.ShapeDtypeStruct((2 * targets, 128), F32))
+        out_specs = (vmem, vmem)
+        if counted:
+            out_shape += (jax.ShapeDtypeStruct((1,), jnp.int32),)
+            out_specs += (pl.BlockSpec(memory_space=pltpu.SMEM),)
+        return pl.pallas_call(
+            functools.partial(cut_kernel, strip_rows, near),
+            out_shape=out_shape,
             in_specs=[vmem] * 6,
-            out_specs=(vmem, vmem),
+            out_specs=out_specs,
             compiler_params=params,
             name="cut_windows",
-        )(far, note, objects, directions, second, first)
-        other = windows = lax.all_to_all(windows, "cuts", 0, 0, tiled=False)
-        if packed:
-            other = lax.ppermute(windows, "cuts", [(i, i ^ 1) for i in range(cuts_count)])
-        gradient = pl.pallas_call(
+        )(*operands)
+
+    def chain(windows, other, probe_wave, *tables):
+        return pl.pallas_call(
             functools.partial(chain_kernel, unit),
-            out_shape=jax.ShapeDtypeStruct((cuts_count, 2, rows_sent, patch_size), BF16),
+            out_shape=jax.ShapeDtypeStruct((windows.shape[0], 2, patch_size, patch_size), BF16),
             in_specs=[vmem] * 7,
             out_specs=vmem,
             scratch_shapes=[pltpu.VMEM((cuts_count, 2, patch_size, patch_size), F32)],
             compiler_params=params,
             name="wave_chain",
-        )(windows, other, probe_wave, kernel_cos, kernel_sin, plus, minus)
-        gradient = lax.all_to_all(gradient, "cuts", 0, 0, tiled=False)
+        )(windows, other, probe_wave, *tables)
+
+    def gather(start, gradient):
         return pl.pallas_call(
             functools.partial(gather_kernel, len(OWNERS) * near),
             out_shape=(
@@ -366,20 +368,27 @@
             name="add_windows",
         )(start, gradient)
 
-    count = pl.pallas_call(
-        functools.partial(count_kernel, strip_rows, near),
-        out_shape=jax.ShapeDtypeStruct((1,), jnp.int32),
-        in_specs=[vmem] * 4,
-        out_specs=pl.BlockSpec(memory_space=pltpu.SMEM),
-        compiler_params=params,
-        name="count_positions",
-    )(far, note, second, first)
+    def one_per_chip(windows, start, around, constants):
+        del around
+        windows = lax.all_to_all(windows, "cuts", 0, 0, axis_index_groups=same_core, tiled=False)
+        other = lax.ppermute(windows, "cuts", [(i, i ^ 1) for i in range(cuts_count)])
+        gradient = chain(windows, other, *constants)
+        gradient = lax.all_to_all(gradient, "cuts", 0, 0, axis_index_groups=same_core, tiled=False)
+        return gather(start, gradient)
+
+    def one_per_device(windows, start, around, constants):
+        del windows, start
+        windows, start = cut(cuts_count, False, *around)
+        windows = lax.all_to_all(windows, "cuts", 0, 0, tiled=False)
+        gradient = chain(windows, windows, *constants)
+        gradient = lax.all_to_all(gradient, "cuts", 0, 0, tiled=False)
+        return gather(start, gradient)
+
+    around = (far, note, objects, directions, second, first)
+    windows, start, count = cut(chips, True, *around)
+    constants = (probe_wave, kernel_cos, kernel_sin, jnp.asarray(plus), jnp.asarray(minus))
     first, own, second = lax.cond(
-        count[0] > cuts_count // 2,
-        functools.partial(work, False),
-        functools.partial(work, True),
-        far, note, objects, directions, first, second,
-        probe_wave, kernel_cos, kernel_sin, jnp.asarray(plus), jnp.asarray(minus),
+        count[0] > chips, one_per_device, one_per_chip, windows, start, around, constants
     )
     first, second = exchanged(first, -1), exchanged(second, 0)
     return (own + first.astype(F32) + second.astype(F32))[None]

time: 85 us -> 77.8 us (0.915)
  blocking collectives: 24.6 us -> 19.7 us
  starting transfers between devices: 31.2 us -> 29.2 us
    all_to_all x2, blocking collectives: 24.6 us -> 19.7 us  [the longest x1 10.9 us: one_per_chip(): lax.all_to_all(windows, 'cuts', 0, 0, axis_index_groups=same_core, tiled=...]
    ppermute x4, starting transfers between devices: 22.6 us -> 18.2 us  [exchanged(): lax.ppermute(block, 'strip', [(i, j % strip_count) for i, j in route])]
    ppermute x1, starting transfers between devices: 2.94 us -> 5.26 us  [one_per_chip(): lax.ppermute(windows, 'cuts', [(i, i ^ 1) for i in range(cuts_count)])]
    pallas_call x4 -> x3, Pallas kernels: 12.8 us -> 12.2 us  [the longest x1 9.87 us: chain(): pl.pallas_call(functools.partial(chain_kernel, unit), out_shape=jax.Shape...]
where the time goes in v5:
time: 77.8 us; the launch traced here: 77.4 us
  starting transfers between devices  29.2 us (38%)
  blocking collectives  19.7 us (25%)
  Pallas kernels  14.4 us (19%)
  waiting for transfers between devices  12.3 us (16%)
  between operations  0.79 us (1%)
    ppermute x4, starting transfers between devices, exchanged(): lax.ppermute(block, 'strip', [(i, j % strip_count) for i, j in route])  18.2 us
    all_to_all x1, blocking collectives, one_per_chip(): lax.all_to_all(windows, 'cuts', 0, 0, axis_index_groups=same_core, tiled=...  10.9 us
    ppermute x4, waiting for transfers between devices, exchanged(): lax.ppermute(block, 'strip', [(i, j % strip_count) for i, j in route])  10.8 us
    pallas_call x1, Pallas kernels, chain(): pl.pallas_call(functools.partial(chain_kernel, unit), out_shape=jax.Shape...  9.87 us
    all_to_all x1, blocking collectives, one_per_chip(): lax.all_to_all(gradient, 'cuts', 0, 0, axis_index_groups=same_core, tiled...  8.81 us
    ppermute x1, starting transfers between devices, on_device(): lax.ppermute(note, 'strip', [(i, (i + REACH) % strip_count) for i in rang...  5.73 us
    ppermute x1, starting transfers between devices, one_per_chip(): lax.ppermute(windows, 'cuts', [(i, i ^ 1) for i in range(cuts_count)])  5.26 us
    pallas_call x1, Pallas kernels, on_device(): pl.pallas_call(functools.partial(pack_kernel, strip_rows, strip_count * s...  1.74 us
  transfers between devices with their start and end apart: 6, of which 5 were waited for; matrix products, arithmetic and copies ran while one was open for 0% of the time, Pallas kernels for 1%

profile of v5, /device:TPU:1, one launch (start us, length us, event | category | flops | bytes accessed | tf_op | source)
XLA Modules:
  0.0 77.4 jit_solution(1358568181845079187)
XLA Ops:
  0.0 0.0 copy-start
  0.0 1.7 %pack_block.1 = (bf16[528,256]{1,0:T(8,128)(2,1)}, bf16[16,256]{1,0:T(8,128)(2,1)S(1)}) custom-call(s32[2]{0:T(128)} %row_any.1, s32[2]{0:T(128)} %col_any.1, bf16[256,256]{1,0:T(8,128)(2,1)} %bitcast.5, bf16[256,256]{1,0:T(8,128)(2,1)} %bitcast.8), custom_call_target="tpu_custom_call" | custom-call | tf_op jit(solution)/shard_map/pack_block/pallas_call | solution.py:293
  1.7 5.7 %collective-permute-start.1 = (bf16[16,256]{1,0:T(8,128)(2,1)S(1)}, bf16[16,256]{1,0:T(8,128)(2,1)S(1)}, u32[]{:S(2)}, u32[]{:S(2)}) collective-permute-start(bf16[16,256]{1,0:T(8,128)(2,1)S(1)} %get-tuple-element.72.note_ref), channel_id=1, source_target_pairs={{0,2},{1,3},{2,4},{3,5},{4,6},{5,7},{6,8},{7,9},{8,10},{9,11},{10,... | collective-permute-start | bytes 24584 | tf_op jit(solution)/shard_map/ppermute | solution.py:309
  7.5 0.0 copy-start.1
  7.5 0.0 copy-start.2
  7.5 10.7 %collective-permute-start.3 = (bf16[528,256]{1,0:T(8,128)(2,1)}, bf16[528,256]{1,0:T(8,128)(2,1)S(1)}, u32[]{:S(2)}, u32[]{:S(2)}) collective-permute-start(bf16[528,256]{1,0:T(8,128)(2,1)} %get-tuple-element.74), channel_id=1, source_target_pairs={{0,63},{1,2},{2,1},{3,4},{4,3},{5,6},{6,5},{7,8},{8,7},{9,10},{10,... | collective-permute-start | bytes 811016 | tf_op jit(solution)/shard_map/ppermute | solution.py:283
  18.2 1.9 %collective-permute-start.2 = (bf16[528,256]{1,0:T(8,128)(2,1)}, bf16[528,256]{1,0:T(8,128)(2,1)S(1)}, u32[]{:S(2)}, u32[]{:S(2)}) collective-permute-start(bf16[528,256]{1,0:T(8,128)(2,1)} %get-tuple-element.74), channel_id=1, source_target_pairs={{0,1},{1,0},{2,3},{3,2},{4,5},{5,4},{6,7},{7,6},{8,9},{9,8},{10,11... | collective-permute-start | bytes 811016 | tf_op jit(solution)/shard_map/ppermute | solution.py:283
  20.2 0.0 collective-permute-done.1.note_ref
  20.2 0.0 copy-done
  20.2 0.4 phase_tables.1
  20.6 4.0 %collective-permute-done.3.first_ref = bf16[528,256]{1,0:T(8,128)(2,1)S(1)} collective-permute-done((bf16[528,256]{1,0:T(8,128)(2,1)}, bf16[528,256]{1,0:T(8,128)(2,1)S(1)}, u32[]{:S(2)}, u32[]{:S(2)}) %collective-permute-start.3) | collective-permute-done | bytes 270368 | tf_op jit(solution)/shard_map/ppermute | solution.py:283
  24.6 2.7 %collective-permute-done.2.second_ref = bf16[528,256]{1,0:T(8,128)(2,1)S(1)} collective-permute-done((bf16[528,256]{1,0:T(8,128)(2,1)}, bf16[528,256]{1,0:T(8,128)(2,1)S(1)}, u32[]{:S(2)}, u32[]{:S(2)}) %collective-permute-start.2) | collective-permute-done | bytes 270368 | tf_op jit(solution)/shard_map/ppermute | solution.py:283
  27.4 0.0 copy-done.1
  27.4 0.0 copy-done.2
  27.4 0.0 copy-start.3
  27.4 0.0 copy-start.5
  27.4 1.7 %cut_windows.3 = (bf16[4,4,128,128]{3,2,1,0:T(8,128)(2,1)S(1)}, f32[8,128]{1,0:T(8,128)S(1)}, s32[1]{0:T(128)}) custom-call(bf16[16,256]{1,0:T(8,128)(2,1)S(1)} %get-tuple-element.73.far_ref, bf16[16,256]{1,0:T(8,128)(2,1)S(1)} %get-tuple-element.72.note_ref, bf16[256,256]{1,0:T(8,128)(2,1)S(1)} %bitcast.6, bf16[256,256]{1,0:T(8,128)(2,1)S(1)} %bitcast.9, ...), custom_call_target="tpu_custom_call" | custom-call | tf_op jit(solution)/shard_map/cut_windows/pallas_call | solution.py:337
  29.8 0.0 copy-done.3
  29.8 0.0 copy-done.4
  29.8 0.0 copy-done.5
  29.8 37.2 %conditional.1 = ((bf16[2,128,256]{2,1,0:T(8,128)(2,1)S(1)}, f32[2,128,256]{2,1,0:T(8,128)S(1)}, bf16[2,128,256]{2,1,0:T(8,128)(2,1)S(1)})) conditional(s32[]{:T(128)} %bitcast.2, (bf16[4,4,128,128]{3,2,1,0:T(8,128)(2,1)S(1)}, bf16[2,128,128]{2,1,0:T(8,128)(2,1)S(1)}, f32[128,128]{1,0:T(8,128)S(1)}, f32[128,128]{1,0:T(8,128)S(1)}, ...), branch_computations={%region_0.0_spmd, %region_1.0_spmd} | conditional | bytes 3670064 | solution.py:390
  29.8 10.9 %all_to_all.16.window_ref = bf16[4,4,128,128]{3,2,1,0:T(8,128)(2,1)S(1)} all-to-all(bf16[4,4,128,128]{3,2,1,0:T(8,128)(2,1)S(1)} %get-tuple-element.42), channel_id=1, replica_groups={{0,128,256,384},{64,192,320,448},{1,129,257,385},{65,193,321,449},{2,13..., dimensions={0} | all-to-all | bytes 1048576 | tf_op jit(solution)/shard_map/cond/branch_0_fun/all_to_all | solution.py:373
  40.7 5.3 %collective-permute-start = (bf16[4,4,128,128]{3,2,1,0:T(8,128)(2,1)S(1)}, bf16[4,4,128,128]{3,2,1,0:T(8,128)(2,1)S(1)}, u32[]{:S(2)}, u32[]{:S(2)}) collective-permute-start(bf16[4,4,128,128]{3,2,1,0:T(8,128)(2,1)S(1)} %all_to_all.16.window_ref), channel_id=1, source_target_pairs={{0,64},{64,0},{128,192},{192,128},{256,320},{320,256},{384,448},{4... | collective-permute-start | bytes 1572872 | tf_op jit(solution)/shard_map/cond/branch_0_fun/ppermute | solution.py:374
  46.0 1.5 %collective-permute-done.other_ref = bf16[4,4,128,128]{3,2,1,0:T(8,128)(2,1)S(1)} collective-permute-done((bf16[4,4,128,128]{3,2,1,0:T(8,128)(2,1)S(1)}, bf16[4,4,128,128]{3,2,1,0:T(8,128)(2,1)S(1)}, u32[]{:S(2)}, u32[]{:S(2)}) %collective-permute-start) | collective-permute-done | bytes 524320 | tf_op jit(solution)/shard_map/cond/branch_0_fun/ppermute | solution.py:374
  47.5 9.9 %wave_chain.2 = bf16[4,2,128,128]{3,2,1,0:T(8,128)(2,1)S(1)} custom-call(bf16[4,4,128,128]{3,2,1,0:T(8,128)(2,1)S(1)} %all_to_all.16.window_ref, bf16[4,4,128,128]{3,2,1,0:T(8,128)(2,1)S(1)} %collective-permute-done.other_ref, bf16[2,128,128]{2,1,0:T(8,128)(2,1)S(1)} %get-tuple-element.43.probe_ref, f32[128,128]{1,0:T(8,128)S(1)} %get-tuple-element.44.cos_ref, ...), custom_call_target="tpu_custom_call" | custom-call | tf_op jit(solution)/shard_map/cond/branch_0_fun/wave_chain/pallas_call | solution.py:347
  57.4 8.8 %all_to_all.17.grad_ref = bf16[4,2,128,128]{3,2,1,0:T(8,128)(2,1)S(1)} all-to-all(bf16[4,2,128,128]{3,2,1,0:T(8,128)(2,1)S(1)} %wave_chain.2), channel_id=1, replica_groups={{0,128,256,384},{64,192,320,448},{1,129,257,385},{65,193,321,449},{2,13..., dimensions={0} | all-to-all | bytes 524288 | tf_op jit(solution)/shard_map/cond/branch_0_fun/all_to_all | solution.py:376
  66.2 0.6 add_windows.2
  67.0 3.7 %collective-permute-start.4 = (bf16[2,128,256]{2,1,0:T(8,128)(2,1)S(1)}, bf16[2,128,256]{2,1,0:T(8,128)(2,1)S(1)}, u32[]{:S(2)}, u32[]{:S(2)}) collective-permute-start(bf16[2,128,256]{2,1,0:T(8,128)(2,1)S(1)} %get-tuple-element.81), channel_id=1, source_target_pairs={{0,63},{1,2},{2,1},{3,4},{4,3},{5,6},{6,5},{7,8},{8,7},{9,10},{10,... | collective-permute-start | bytes 393224 | tf_op jit(solution)/shard_map/ppermute | solution.py:283
  70.7 1.9 %collective-permute-start.5 = (bf16[2,128,256]{2,1,0:T(8,128)(2,1)S(1)}, bf16[2,128,256]{2,1,0:T(8,128)(2,1)S(1)}, u32[]{:S(2)}, u32[]{:S(2)}) collective-permute-start(bf16[2,128,256]{2,1,0:T(8,128)(2,1)S(1)} %get-tuple-element.82), channel_id=1, source_target_pairs={{0,1},{1,0},{2,3},{3,2},{4,5},{5,4},{6,7},{7,6},{8,9},{9,8},{10,11... | collective-permute-start | bytes 393224 | tf_op jit(solution)/shard_map/ppermute | solution.py:283
  72.6 3.4 %collective-permute-done.4 = bf16[2,128,256]{2,1,0:T(8,128)(2,1)S(1)} collective-permute-done((bf16[2,128,256]{2,1,0:T(8,128)(2,1)S(1)}, bf16[2,128,256]{2,1,0:T(8,128)(2,1)S(1)}, u32[]{:S(2)}, u32[]{:S(2)}) %collective-permute-start.4) | collective-permute-done | bytes 131104 | tf_op jit(solution)/shard_map/ppermute | solution.py:283
  76.1 0.6 collective-permute-done.5
  76.7 0.7 add_bitcast_fusion
  (1 shorter events, 0.0 us)
Async XLA Ops:
  0.0 20.2 %copy-start = (f32[128,128]{1,0:T(8,128)S(1)}, f32[128,128]{1,0:T(8,128)}, u32[]{:S(2)}) copy-start(f32[128,128]{1,0:T(8,128)} %phase_ref.1) | copy-start | bytes 196612
  1.7 18.4 %collective-permute-start.1 = (bf16[16,256]{1,0:T(8,128)(2,1)S(1)}, bf16[16,256]{1,0:T(8,128)(2,1)S(1)}, u32[]{:S(2)}, u32[]{:S(2)}) collective-permute-start(bf16[16,256]{1,0:T(8,128)(2,1)S(1)} %get-tuple-element.72.note_ref), channel_id=1, source_target_pairs={{0,2},{1,3},{2,4},{3,5},{4,6},{5,7},{6,8},{7,9},{8,10},{9,11},{10,... | collective-permute-start | bytes 24584 | tf_op jit(solution)/shard_map/ppermute | solution.py:309
  7.5 19.9 %copy-start.1 = (bf16[1,2,128,256]{3,2,1,0:T(8,128)(2,1)S(1)}, bf16[1,2,128,256]{3,2,1,0:T(8,128)(2,1)}, u32[]{:S(2)}) copy-start(bf16[1,2,128,256]{3,2,1,0:T(8,128)(2,1)} %param.10) | copy-start | bytes 393220
  7.5 19.9 %copy-start.2 = (bf16[1,2,128,256]{3,2,1,0:T(8,128)(2,1)S(1)}, bf16[1,2,128,256]{3,2,1,0:T(8,128)(2,1)}, u32[]{:S(2)}) copy-start(bf16[1,2,128,256]{3,2,1,0:T(8,128)(2,1)} %param.11) | copy-start | bytes 393220
  7.5 17.1 %collective-permute-start.3 = (bf16[528,256]{1,0:T(8,128)(2,1)}, bf16[528,256]{1,0:T(8,128)(2,1)S(1)}, u32[]{:S(2)}, u32[]{:S(2)}) collective-permute-start(bf16[528,256]{1,0:T(8,128)(2,1)} %get-tuple-element.74), channel_id=1, source_target_pairs={{0,63},{1,2},{2,1},{3,4},{4,3},{5,6},{6,5},{7,8},{8,7},{9,10},{10,... | collective-permute-start | bytes 811016 | tf_op jit(solution)/shard_map/ppermute | solution.py:283
  18.2 9.1 %collective-permute-start.2 = (bf16[528,256]{1,0:T(8,128)(2,1)}, bf16[528,256]{1,0:T(8,128)(2,1)S(1)}, u32[]{:S(2)}, u32[]{:S(2)}) collective-permute-start(bf16[528,256]{1,0:T(8,128)(2,1)} %get-tuple-element.74), channel_id=1, source_target_pairs={{0,1},{1,0},{2,3},{3,2},{4,5},{5,4},{6,7},{7,6},{8,9},{9,8},{10,11... | collective-permute-start | bytes 811016 | tf_op jit(solution)/shard_map/ppermute | solution.py:283
  27.4 2.4 %copy-start.3 = (bf16[256,256]{1,0:T(8,128)(2,1)S(1)}, bf16[256,256]{1,0:T(8,128)(2,1)}, u32[]{:S(2)}) copy-start(bf16[256,256]{1,0:T(8,128)(2,1)} %constant.8.clone) | copy-start | bytes 393220
  27.4 2.4 %copy-start.4 = (bf16[256,256]{1,0:T(8,128)(2,1)S(1)}, bf16[256,256]{1,0:T(8,128)(2,1)}, u32[]{:S(2)}) copy-start(bf16[256,256]{1,0:T(8,128)(2,1)} %constant.7.clone) | copy-start | bytes 393220
  27.4 2.4 %copy-start.5 = (bf16[2,128,128]{2,1,0:T(8,128)(2,1)S(1)}, bf16[2,128,128]{2,1,0:T(8,128)(2,1)}, u32[]{:S(2)}) copy-start(bf16[2,128,128]{2,1,0:T(8,128)(2,1)} %param.12) | copy-start | bytes 196612
  40.7 6.8 %collective-permute-start = (bf16[4,4,128,128]{3,2,1,0:T(8,128)(2,1)S(1)}, bf16[4,4,128,128]{3,2,1,0:T(8,128)(2,1)S(1)}, u32[]{:S(2)}, u32[]{:S(2)}) collective-permute-start(bf16[4,4,128,128]{3,2,1,0:T(8,128)(2,1)S(1)} %all_to_all.16.window_ref), channel_id=1, source_target_pairs={{0,64},{64,0},{128,192},{192,128},{256,320},{320,256},{384,448},{4... | collective-permute-start | bytes 1572872 | tf_op jit(solution)/shard_map/cond/branch_0_fun/ppermute | solution.py:374
  67.0 9.0 %collective-permute-start.4 = (bf16[2,128,256]{2,1,0:T(8,128)(2,1)S(1)}, bf16[2,128,256]{2,1,0:T(8,128)(2,1)S(1)}, u32[]{:S(2)}, u32[]{:S(2)}) collective-permute-start(bf16[2,128,256]{2,1,0:T(8,128)(2,1)S(1)} %get-tuple-element.81), channel_id=1, source_target_pairs={{0,63},{1,2},{2,1},{3,4},{4,3},{5,6},{6,5},{7,8},{8,7},{9,10},{10,... | collective-permute-start | bytes 393224 | tf_op jit(solution)/shard_map/ppermute | solution.py:283
  70.7 6.0 %collective-permute-start.5 = (bf16[2,128,256]{2,1,0:T(8,128)(2,1)S(1)}, bf16[2,128,256]{2,1,0:T(8,128)(2,1)S(1)}, u32[]{:S(2)}, u32[]{:S(2)}) collective-permute-start(bf16[2,128,256]{2,1,0:T(8,128)(2,1)S(1)} %get-tuple-element.82), channel_id=1, source_target_pairs={{0,1},{1,0},{2,3},{3,2},{4,5},{5,4},{6,7},{7,6},{8,9},{9,8},{10,11... | collective-permute-start | bytes 393224 | tf_op jit(solution)/shard_map/ppermute | solution.py:283

commit v6 on v5

--- a/solution.py
+++ b/solution.py
@@ -97,8 +97,7 @@
         copy.wait()
 
 
-def phase_kernel(note_ref, phase_ref, far_ref, cos_ref, sin_ref):
-    far_ref[...] = note_ref[...]
+def phase_kernel(phase_ref, cos_ref, sin_ref):
     cos_ref[...] = jnp.cos(phase_ref[...])
     sin_ref[...] = jnp.sin(phase_ref[...])
 
@@ -177,19 +176,22 @@
         mine, other = window_ref[layer // 2, part], other_ref[layer // 2, part]
         return (jnp.where(even, mine, other) if layer % 2 == 0 else jnp.where(even, other, mine)).astype(F32)
 
-    def swap(values, waves):
+    def swap(values):
         blocks = [[values[i * size : (i + 1) * size, j * size : (j + 1) * size]
                    for j in range(values.shape[1] // size)] for i in range(values.shape[0] // size)]
         turned = [jnp.concatenate([row[j] for row in blocks], axis=1) for j in range(len(blocks[0]))]
         return jnp.concatenate(turned, axis=0) if len(turned) > 1 else turned[0]
 
+    def from_left(table, columns):
+        return jnp.concatenate([dot(table[:size], columns), dot(table[size:], columns)], axis=0)
+
     def forward(columns):
-        half = dot(plus, columns.astype(BF16)).astype(BF16)
-        return dot(swap(half, None), minus)
+        half = from_left(plus, columns.astype(BF16)).astype(BF16)
+        return dot(swap(half), minus)
 
     def inverse(rows):
         half = dot(rows.astype(BF16), plus).astype(BF16)
-        return dot(minus, swap(half, None))
+        return from_left(minus, swap(half))
 
     def kernel_times(rows, sign, scale):
         kernel_cos, kernel_sin = cos_ref[...] * scale, sin_ref[...] * (sign * scale)
@@ -308,19 +310,14 @@
     )(corner_row, corner_col, objects, directions)
     far = lax.ppermute(note, "strip", [(i, (i + REACH) % strip_count) for i in range(strip_count)])
     first, second = exchanged(block, -1), exchanged(block, 0)
-    far, kernel_cos, kernel_sin = pl.pallas_call(
+    kernel_cos, kernel_sin = pl.pallas_call(
         phase_kernel,
-        out_shape=(
-            jax.ShapeDtypeStruct(note.shape, BF16),
-            jax.ShapeDtypeStruct(kernel_phase.shape, F32),
-            jax.ShapeDtypeStruct(kernel_phase.shape, F32),
-        ),
-        in_specs=[vmem] * 2,
-        out_specs=(vmem,) * 3,
+        out_shape=(jax.ShapeDtypeStruct(kernel_phase.shape, F32),) * 2,
+        in_specs=[vmem],
+        out_specs=(vmem,) * 2,
         compiler_params=params,
-        cost_estimate=pl.CostEstimate(flops=20_000_000_000, bytes_accessed=100_000_000, transcendentals=0),
         name="phase_tables",
-    )(far, kernel_phase)
+    )(kernel_phase)
     near = corner_row.shape[0]
     strip_shape = (2, strip_rows, column_count)
 

time: 77.8 us -> 75.4 us (0.969)
  waiting for transfers between devices: 12.3 us -> 11.2 us
  Pallas kernels: 14.4 us -> 13.5 us
    ppermute x4, waiting for transfers between devices: 10.8 us -> 3.47 us  [exchanged(): lax.ppermute(block, 'strip', [(i, j % strip_count) for i, j in route])]
    ppermute x1, waiting for transfers between devices: 0.01 us -> 6.2 us  [on_device(): lax.ppermute(note, 'strip', [(i, (i + REACH) % strip_count) for i in rang...]
    ppermute x1, starting transfers between devices: 5.73 us -> 1.92 us  [on_device(): lax.ppermute(note, 'strip', [(i, (i + REACH) % strip_count) for i in rang...]
    ppermute x4, starting transfers between devices: 18.2 us -> 21.9 us  [exchanged(): lax.ppermute(block, 'strip', [(i, j % strip_count) for i, j in route])]
    pallas_call x1, Pallas kernels: 9.87 us -> 9 us  [chain(): pl.pallas_call(functools.partial(chain_kernel, unit), out_shape=jax.Shape...]
  transfers between devices with their start and end apart: 6 -> 6, of which waited for: 5 -> 3; matrix products, arithmetic and copies ran while one was open for 0% -> 0% of each run, Pallas kernels for 1% -> 1%
where the time goes in v6:
time: 75.4 us; the launch traced here: 75.1 us
  starting transfers between devices  29.2 us (39%)
  blocking collectives  19.6 us (26%)
  Pallas kernels  13.5 us (18%)
  waiting for transfers between devices  11.2 us (15%)
  between operations  0.79 us (1%)
    ppermute x4, starting transfers between devices, exchanged(): lax.ppermute(block, 'strip', [(i, j % strip_count) for i, j in route])  21.9 us
    all_to_all x1, blocking collectives, one_per_chip(): lax.all_to_all(windows, 'cuts', 0, 0, axis_index_groups=same_core, tiled=...  10.8 us
    pallas_call x1, Pallas kernels, chain(): pl.pallas_call(functools.partial(chain_kernel, unit), out_shape=jax.Shape...  9 us
    all_to_all x1, blocking collectives, one_per_chip(): lax.all_to_all(gradient, 'cuts', 0, 0, axis_index_groups=same_core, tiled...  8.79 us
    ppermute x1, waiting for transfers between devices, on_device(): lax.ppermute(note, 'strip', [(i, (i + REACH) % strip_count) for i in rang...  6.2 us
    ppermute x1, starting transfers between devices, one_per_chip(): lax.ppermute(windows, 'cuts', [(i, i ^ 1) for i in range(cuts_count)])  5.4 us
    ppermute x4, waiting for transfers between devices, exchanged(): lax.ppermute(block, 'strip', [(i, j % strip_count) for i, j in route])  3.47 us
    ppermute x1, starting transfers between devices, on_device(): lax.ppermute(note, 'strip', [(i, (i + REACH) % strip_count) for i in rang...  1.92 us
  transfers between devices with their start and end apart: 6, of which 3 were waited for; matrix products, arithmetic and copies ran while one was open for 0% of the time, Pallas kernels for 1%

profile of v6, /device:TPU:1, one launch (start us, length us, event | category | flops | bytes accessed | tf_op | source)
XLA Modules:
  0.0 75.1 jit_solution(4245299677564783644)
XLA Ops:
  0.0 0.0 copy-start
  0.0 0.0 copy-start.1
  0.0 1.8 %pack_block.1 = (bf16[528,256]{1,0:T(8,128)(2,1)}, bf16[16,256]{1,0:T(8,128)(2,1)S(1)}) custom-call(s32[2]{0:T(128)} %row_any.1, s32[2]{0:T(128)} %col_any.1, bf16[256,256]{1,0:T(8,128)(2,1)} %bitcast.5, bf16[256,256]{1,0:T(8,128)(2,1)} %bitcast.8), custom_call_target="tpu_custom_call" | custom-call | tf_op jit(solution)/shard_map/pack_block/pallas_call | solution.py:295
  1.8 14.4 %collective-permute-start.3 = (bf16[528,256]{1,0:T(8,128)(2,1)}, bf16[528,256]{1,0:T(8,128)(2,1)S(1)}, u32[]{:S(2)}, u32[]{:S(2)}) collective-permute-start(bf16[528,256]{1,0:T(8,128)(2,1)} %get-tuple-element.72), channel_id=1, source_target_pairs={{0,63},{1,2},{2,1},{3,4},{4,3},{5,6},{6,5},{7,8},{8,7},{9,10},{10,... | collective-permute-start | bytes 811016 | tf_op jit(solution)/shard_map/ppermute | solution.py:285
  16.2 1.9 %collective-permute-start.2 = (bf16[528,256]{1,0:T(8,128)(2,1)}, bf16[528,256]{1,0:T(8,128)(2,1)S(1)}, u32[]{:S(2)}, u32[]{:S(2)}) collective-permute-start(bf16[528,256]{1,0:T(8,128)(2,1)} %get-tuple-element.72), channel_id=1, source_target_pairs={{0,1},{1,0},{2,3},{3,2},{4,5},{5,4},{6,7},{7,6},{8,9},{9,8},{10,11... | collective-permute-start | bytes 811016 | tf_op jit(solution)/shard_map/ppermute | solution.py:285
  18.1 1.9 %collective-permute-start.1 = (bf16[16,256]{1,0:T(8,128)(2,1)S(1)}, bf16[16,256]{1,0:T(8,128)(2,1)S(1)}, u32[]{:S(2)}, u32[]{:S(2)}) collective-permute-start(bf16[16,256]{1,0:T(8,128)(2,1)S(1)} %get-tuple-element.71.note_ref), channel_id=1, source_target_pairs={{0,2},{1,3},{2,4},{3,5},{4,6},{5,7},{6,8},{7,9},{8,10},{9,11},{10,... | collective-permute-start | bytes 24584 | tf_op jit(solution)/shard_map/ppermute | solution.py:311
  20.0 0.0 copy-done
  20.0 0.4 phase_tables.1
  20.5 0.0 copy-start.3
  20.5 0.0 copy-start.4
  20.5 0.0 copy-start.5
  20.5 6.2 %collective-permute-done.1.far_ref = bf16[16,256]{1,0:T(8,128)(2,1)S(1)} collective-permute-done((bf16[16,256]{1,0:T(8,128)(2,1)S(1)}, bf16[16,256]{1,0:T(8,128)(2,1)S(1)}, u32[]{:S(2)}, u32[]{:S(2)}) %collective-permute-start.1) | collective-permute-done | bytes 8224 | tf_op jit(solution)/shard_map/ppermute | solution.py:311
  26.7 0.0 collective-permute-done.3.first_ref
  26.7 0.0 collective-permute-done.2.second_ref
  26.7 0.0 copy-done.1
  26.7 0.0 copy-done.2
  26.7 1.7 %cut_windows.3 = (bf16[4,4,128,128]{3,2,1,0:T(8,128)(2,1)S(1)}, f32[8,128]{1,0:T(8,128)S(1)}, s32[1]{0:T(128)}) custom-call(bf16[16,256]{1,0:T(8,128)(2,1)S(1)} %collective-permute-done.1.far_ref, bf16[16,256]{1,0:T(8,128)(2,1)S(1)} %get-tuple-element.71.note_ref, bf16[256,256]{1,0:T(8,128)(2,1)S(1)} %bitcast.6, bf16[256,256]{1,0:T(8,128)(2,1)S(1)} %bitcast.9, ...), custom_call_target="tpu_custom_call" | custom-call | tf_op jit(solution)/shard_map/cut_windows/pallas_call | solution.py:334
  29.1 0.0 copy-done.3
  29.1 0.0 copy-done.4
  29.2 0.0 copy-done.5
  29.2 36.1 %conditional.1 = ((bf16[2,128,256]{2,1,0:T(8,128)(2,1)S(1)}, f32[2,128,256]{2,1,0:T(8,128)S(1)}, bf16[2,128,256]{2,1,0:T(8,128)(2,1)S(1)})) conditional(s32[]{:T(128)} %bitcast.2, (bf16[4,4,128,128]{3,2,1,0:T(8,128)(2,1)S(1)}, bf16[2,128,128]{2,1,0:T(8,128)(2,1)S(1)}, f32[128,128]{1,0:T(8,128)S(1)}, f32[128,128]{1,0:T(8,128)S(1)}, ...), branch_computations={%region_0.0_spmd, %region_1.0_spmd} | conditional | bytes 3670064 | solution.py:387
  29.2 10.8 %all_to_all.16.window_ref = bf16[4,4,128,128]{3,2,1,0:T(8,128)(2,1)S(1)} all-to-all(bf16[4,4,128,128]{3,2,1,0:T(8,128)(2,1)S(1)} %get-tuple-element.42), channel_id=1, replica_groups={{0,128,256,384},{64,192,320,448},{1,129,257,385},{65,193,321,449},{2,13..., dimensions={0} | all-to-all | bytes 1048576 | tf_op jit(solution)/shard_map/cond/branch_0_fun/all_to_all | solution.py:370
  40.0 5.4 %collective-permute-start = (bf16[4,4,128,128]{3,2,1,0:T(8,128)(2,1)S(1)}, bf16[4,4,128,128]{3,2,1,0:T(8,128)(2,1)S(1)}, u32[]{:S(2)}, u32[]{:S(2)}) collective-permute-start(bf16[4,4,128,128]{3,2,1,0:T(8,128)(2,1)S(1)} %all_to_all.16.window_ref), channel_id=1, source_target_pairs={{0,64},{64,0},{128,192},{192,128},{256,320},{320,256},{384,448},{4... | collective-permute-start | bytes 1572872 | tf_op jit(solution)/shard_map/cond/branch_0_fun/ppermute | solution.py:371
  45.4 1.5 %collective-permute-done.other_ref = bf16[4,4,128,128]{3,2,1,0:T(8,128)(2,1)S(1)} collective-permute-done((bf16[4,4,128,128]{3,2,1,0:T(8,128)(2,1)S(1)}, bf16[4,4,128,128]{3,2,1,0:T(8,128)(2,1)S(1)}, u32[]{:S(2)}, u32[]{:S(2)}) %collective-permute-start) | collective-permute-done | bytes 524320 | tf_op jit(solution)/shard_map/cond/branch_0_fun/ppermute | solution.py:371
  46.9 9.0 %wave_chain.2 = bf16[4,2,128,128]{3,2,1,0:T(8,128)(2,1)S(1)} custom-call(bf16[4,4,128,128]{3,2,1,0:T(8,128)(2,1)S(1)} %all_to_all.16.window_ref, bf16[4,4,128,128]{3,2,1,0:T(8,128)(2,1)S(1)} %collective-permute-done.other_ref, bf16[2,128,128]{2,1,0:T(8,128)(2,1)S(1)} %get-tuple-element.43.probe_ref, f32[128,128]{1,0:T(8,128)S(1)} %get-tuple-element.44.cos_ref, ...), custom_call_target="tpu_custom_call" | custom-call | tf_op jit(solution)/shard_map/cond/branch_0_fun/wave_chain/pallas_call | solution.py:344
  55.9 8.8 %all_to_all.17.grad_ref = bf16[4,2,128,128]{3,2,1,0:T(8,128)(2,1)S(1)} all-to-all(bf16[4,2,128,128]{3,2,1,0:T(8,128)(2,1)S(1)} %wave_chain.2), channel_id=1, replica_groups={{0,128,256,384},{64,192,320,448},{1,129,257,385},{65,193,321,449},{2,13..., dimensions={0} | all-to-all | bytes 524288 | tf_op jit(solution)/shard_map/cond/branch_0_fun/all_to_all | solution.py:373
  64.7 0.6 add_windows.2
  65.3 2.2 %collective-permute-start.4 = (bf16[2,128,256]{2,1,0:T(8,128)(2,1)S(1)}, bf16[2,128,256]{2,1,0:T(8,128)(2,1)S(1)}, u32[]{:S(2)}, u32[]{:S(2)}) collective-permute-start(bf16[2,128,256]{2,1,0:T(8,128)(2,1)S(1)} %get-tuple-element.79), channel_id=1, source_target_pairs={{0,63},{1,2},{2,1},{3,4},{4,3},{5,6},{6,5},{7,8},{8,7},{9,10},{10,... | collective-permute-start | bytes 393224 | tf_op jit(solution)/shard_map/ppermute | solution.py:285
  67.5 3.4 %collective-permute-start.5 = (bf16[2,128,256]{2,1,0:T(8,128)(2,1)S(1)}, bf16[2,128,256]{2,1,0:T(8,128)(2,1)S(1)}, u32[]{:S(2)}, u32[]{:S(2)}) collective-permute-start(bf16[2,128,256]{2,1,0:T(8,128)(2,1)S(1)} %get-tuple-element.80), channel_id=1, source_target_pairs={{0,1},{1,0},{2,3},{3,2},{4,5},{5,4},{6,7},{7,6},{8,9},{9,8},{10,11... | collective-permute-start | bytes 393224 | tf_op jit(solution)/shard_map/ppermute | solution.py:285
  70.9 3.5 %collective-permute-done.4 = bf16[2,128,256]{2,1,0:T(8,128)(2,1)S(1)} collective-permute-done((bf16[2,128,256]{2,1,0:T(8,128)(2,1)S(1)}, bf16[2,128,256]{2,1,0:T(8,128)(2,1)S(1)}, u32[]{:S(2)}, u32[]{:S(2)}) %collective-permute-start.4) | collective-permute-done | bytes 131104 | tf_op jit(solution)/shard_map/ppermute | solution.py:285
  74.3 0.0 collective-permute-done.5
  74.3 0.7 add_bitcast_fusion
  (1 shorter events, 0.0 us)
Async XLA Ops:
  0.0 20.0 %copy-start = (f32[128,128]{1,0:T(8,128)S(1)}, f32[128,128]{1,0:T(8,128)}, u32[]{:S(2)}) copy-start(f32[128,128]{1,0:T(8,128)} %phase_ref.1) | copy-start | bytes 196612
  0.0 26.7 %copy-start.1 = (bf16[1,2,128,256]{3,2,1,0:T(8,128)(2,1)S(1)}, bf16[1,2,128,256]{3,2,1,0:T(8,128)(2,1)}, u32[]{:S(2)}) copy-start(bf16[1,2,128,256]{3,2,1,0:T(8,128)(2,1)} %param.10) | copy-start | bytes 393220
  0.0 26.7 %copy-start.2 = (bf16[1,2,128,256]{3,2,1,0:T(8,128)(2,1)S(1)}, bf16[1,2,128,256]{3,2,1,0:T(8,128)(2,1)}, u32[]{:S(2)}) copy-start(bf16[1,2,128,256]{3,2,1,0:T(8,128)(2,1)} %param.11) | copy-start | bytes 393220
  1.8 25.0 %collective-permute-start.3 = (bf16[528,256]{1,0:T(8,128)(2,1)}, bf16[528,256]{1,0:T(8,128)(2,1)S(1)}, u32[]{:S(2)}, u32[]{:S(2)}) collective-permute-start(bf16[528,256]{1,0:T(8,128)(2,1)} %get-tuple-element.72), channel_id=1, source_target_pairs={{0,63},{1,2},{2,1},{3,4},{4,3},{5,6},{6,5},{7,8},{8,7},{9,10},{10,... | collective-permute-start | bytes 811016 | tf_op jit(solution)/shard_map/ppermute | solution.py:285
  16.2 10.5 %collective-permute-start.2 = (bf16[528,256]{1,0:T(8,128)(2,1)}, bf16[528,256]{1,0:T(8,128)(2,1)S(1)}, u32[]{:S(2)}, u32[]{:S(2)}) collective-permute-start(bf16[528,256]{1,0:T(8,128)(2,1)} %get-tuple-element.72), channel_id=1, source_target_pairs={{0,1},{1,0},{2,3},{3,2},{4,5},{5,4},{6,7},{7,6},{8,9},{9,8},{10,11... | collective-permute-start | bytes 811016 | tf_op jit(solution)/shard_map/ppermute | solution.py:285
  18.1 8.6 %collective-permute-start.1 = (bf16[16,256]{1,0:T(8,128)(2,1)S(1)}, bf16[16,256]{1,0:T(8,128)(2,1)S(1)}, u32[]{:S(2)}, u32[]{:S(2)}) collective-permute-start(bf16[16,256]{1,0:T(8,128)(2,1)S(1)} %get-tuple-element.71.note_ref), channel_id=1, source_target_pairs={{0,2},{1,3},{2,4},{3,5},{4,6},{5,7},{6,8},{7,9},{8,10},{9,11},{10,... | collective-permute-start | bytes 24584 | tf_op jit(solution)/shard_map/ppermute | solution.py:311
  20.5 8.7 %copy-start.3 = (bf16[256,256]{1,0:T(8,128)(2,1)S(1)}, bf16[256,256]{1,0:T(8,128)(2,1)}, u32[]{:S(2)}) copy-start(bf16[256,256]{1,0:T(8,128)(2,1)} %constant.8.clone) | copy-start | bytes 393220
  20.5 8.6 %copy-start.4 = (bf16[256,256]{1,0:T(8,128)(2,1)S(1)}, bf16[256,256]{1,0:T(8,128)(2,1)}, u32[]{:S(2)}) copy-start(bf16[256,256]{1,0:T(8,128)(2,1)} %constant.7.clone) | copy-start | bytes 393220
  20.5 8.6 %copy-start.5 = (bf16[2,128,128]{2,1,0:T(8,128)(2,1)S(1)}, bf16[2,128,128]{2,1,0:T(8,128)(2,1)}, u32[]{:S(2)}) copy-start(bf16[2,128,128]{2,1,0:T(8,128)(2,1)} %param.12) | copy-start | bytes 196612
  40.0 6.9 %collective-permute-start = (bf16[4,4,128,128]{3,2,1,0:T(8,128)(2,1)S(1)}, bf16[4,4,128,128]{3,2,1,0:T(8,128)(2,1)S(1)}, u32[]{:S(2)}, u32[]{:S(2)}) collective-permute-start(bf16[4,4,128,128]{3,2,1,0:T(8,128)(2,1)S(1)} %all_to_all.16.window_ref), channel_id=1, source_target_pairs={{0,64},{64,0},{128,192},{192,128},{256,320},{320,256},{384,448},{4... | collective-permute-start | bytes 1572872 | tf_op jit(solution)/shard_map/cond/branch_0_fun/ppermute | solution.py:371
  65.3 9.0 %collective-permute-start.4 = (bf16[2,128,256]{2,1,0:T(8,128)(2,1)S(1)}, bf16[2,128,256]{2,1,0:T(8,128)(2,1)S(1)}, u32[]{:S(2)}, u32[]{:S(2)}) collective-permute-start(bf16[2,128,256]{2,1,0:T(8,128)(2,1)S(1)} %get-tuple-element.79), channel_id=1, source_target_pairs={{0,63},{1,2},{2,1},{3,4},{4,3},{5,6},{6,5},{7,8},{8,7},{9,10},{10,... | collective-permute-start | bytes 393224 | tf_op jit(solution)/shard_map/ppermute | solution.py:285
  67.5 6.8 %collective-permute-start.5 = (bf16[2,128,256]{2,1,0:T(8,128)(2,1)S(1)}, bf16[2,128,256]{2,1,0:T(8,128)(2,1)S(1)}, u32[]{:S(2)}, u32[]{:S(2)}) collective-permute-start(bf16[2,128,256]{2,1,0:T(8,128)(2,1)S(1)} %get-tuple-element.80), channel_id=1, source_target_pairs={{0,1},{1,0},{2,3},{3,2},{4,5},{5,4},{6,7},{7,6},{8,9},{9,8},{10,11... | collective-permute-start | bytes 393224 | tf_op jit(solution)/shard_map/ppermute | solution.py:285

commit v7 on v6

--- a/solution.py
+++ b/solution.py
@@ -183,14 +183,19 @@
         return jnp.concatenate(turned, axis=0) if len(turned) > 1 else turned[0]
 
     def from_left(table, columns):
-        return jnp.concatenate([dot(table[:size], columns), dot(table[size:], columns)], axis=0)
+        step = 2 * size // 2
+        return jnp.concatenate([dot(table[i * step : (i + 1) * step], columns) for i in range(2)], axis=0)
+
+    def from_right(rows, table):
+        step = rows.shape[0] // 2
+        return jnp.concatenate([dot(rows[i * step : (i + 1) * step], table) for i in range(2)], axis=0)
 
     def forward(columns):
         half = from_left(plus, columns.astype(BF16)).astype(BF16)
-        return dot(swap(half), minus)
+        return from_right(swap(half), minus)
 
     def inverse(rows):
-        half = dot(rows.astype(BF16), plus).astype(BF16)
+        half = from_right(rows.astype(BF16), plus).astype(BF16)
         return from_left(minus, swap(half))
 
     def kernel_times(rows, sign, scale):

time: 75.4 us -> 75.3 us (level)
  no operation moved by 1% of the time
where the time goes in v7:
time: 75.3 us; the launch traced here: 74.9 us
  starting transfers between devices  29.2 us (39%)
  blocking collectives  19.6 us (26%)
  Pallas kernels  13.4 us (18%)
  waiting for transfers between devices  11.2 us (15%)
  between operations  0.79 us (1%)
    ppermute x4, starting transfers between devices, exchanged(): lax.ppermute(block, 'strip', [(i, j % strip_count) for i, j in route])  21.9 us
    all_to_all x1, blocking collectives, one_per_chip(): lax.all_to_all(windows, 'cuts', 0, 0, axis_index_groups=same_core, tiled=...  10.8 us
    pallas_call x1, Pallas kernels, chain(): pl.pallas_call(functools.partial(chain_kernel, unit), out_shape=jax.Shape...  8.85 us
    all_to_all x1, blocking collectives, one_per_chip(): lax.all_to_all(gradient, 'cuts', 0, 0, axis_index_groups=same_core, tiled...  8.8 us
    ppermute x1, waiting for transfers between devices, on_device(): lax.ppermute(note, 'strip', [(i, (i + REACH) % strip_count) for i in rang...  6.2 us
    ppermute x1, starting transfers between devices, one_per_chip(): lax.ppermute(windows, 'cuts', [(i, i ^ 1) for i in range(cuts_count)])  5.4 us
    ppermute x4, waiting for transfers between devices, exchanged(): lax.ppermute(block, 'strip', [(i, j % strip_count) for i, j in route])  3.47 us
    ppermute x1, starting transfers between devices, on_device(): lax.ppermute(note, 'strip', [(i, (i + REACH) % strip_count) for i in rang...  1.92 us
  transfers between devices with their start and end apart: 6, of which 3 were waited for; matrix products, arithmetic and copies ran while one was open for 0% of the time, Pallas kernels for 1%

profile of v7, /device:TPU:1, one launch (start us, length us, event | category | flops | bytes accessed | tf_op | source)
XLA Modules:
  0.0 74.9 jit_solution(14738832459709082001)
XLA Ops:
  0.0 0.0 copy-start
  0.0 0.0 copy-start.1
  0.0 1.8 %pack_block.1 = (bf16[528,256]{1,0:T(8,128)(2,1)}, bf16[16,256]{1,0:T(8,128)(2,1)S(1)}) custom-call(s32[2]{0:T(128)} %row_any.1, s32[2]{0:T(128)} %col_any.1, bf16[256,256]{1,0:T(8,128)(2,1)} %bitcast.5, bf16[256,256]{1,0:T(8,128)(2,1)} %bitcast.8), custom_call_target="tpu_custom_call" | custom-call | tf_op jit(solution)/shard_map/pack_block/pallas_call | solution.py:300
  1.8 14.4 %collective-permute-start.3 = (bf16[528,256]{1,0:T(8,128)(2,1)}, bf16[528,256]{1,0:T(8,128)(2,1)S(1)}, u32[]{:S(2)}, u32[]{:S(2)}) collective-permute-start(bf16[528,256]{1,0:T(8,128)(2,1)} %get-tuple-element.72), channel_id=1, source_target_pairs={{0,63},{1,2},{2,1},{3,4},{4,3},{5,6},{6,5},{7,8},{8,7},{9,10},{10,... | collective-permute-start | bytes 811016 | tf_op jit(solution)/shard_map/ppermute | solution.py:290
  16.2 1.9 %collective-permute-start.2 = (bf16[528,256]{1,0:T(8,128)(2,1)}, bf16[528,256]{1,0:T(8,128)(2,1)S(1)}, u32[]{:S(2)}, u32[]{:S(2)}) collective-permute-start(bf16[528,256]{1,0:T(8,128)(2,1)} %get-tuple-element.72), channel_id=1, source_target_pairs={{0,1},{1,0},{2,3},{3,2},{4,5},{5,4},{6,7},{7,6},{8,9},{9,8},{10,11... | collective-permute-start | bytes 811016 | tf_op jit(solution)/shard_map/ppermute | solution.py:290
  18.1 1.9 %collective-permute-start.1 = (bf16[16,256]{1,0:T(8,128)(2,1)S(1)}, bf16[16,256]{1,0:T(8,128)(2,1)S(1)}, u32[]{:S(2)}, u32[]{:S(2)}) collective-permute-start(bf16[16,256]{1,0:T(8,128)(2,1)S(1)} %get-tuple-element.71.note_ref), channel_id=1, source_target_pairs={{0,2},{1,3},{2,4},{3,5},{4,6},{5,7},{6,8},{7,9},{8,10},{9,11},{10,... | collective-permute-start | bytes 24584 | tf_op jit(solution)/shard_map/ppermute | solution.py:316
  20.0 0.0 copy-done
  20.0 0.4 phase_tables.1
  20.5 0.0 copy-start.3
  20.5 0.0 copy-start.4
  20.5 0.0 copy-start.5
  20.5 6.2 %collective-permute-done.1.far_ref = bf16[16,256]{1,0:T(8,128)(2,1)S(1)} collective-permute-done((bf16[16,256]{1,0:T(8,128)(2,1)S(1)}, bf16[16,256]{1,0:T(8,128)(2,1)S(1)}, u32[]{:S(2)}, u32[]{:S(2)}) %collective-permute-start.1) | collective-permute-done | bytes 8224 | tf_op jit(solution)/shard_map/ppermute | solution.py:316
  26.7 0.0 collective-permute-done.3.first_ref
  26.7 0.0 collective-permute-done.2.second_ref
  26.7 0.0 copy-done.1
  26.7 0.0 copy-done.2
  26.7 1.7 %cut_windows.3 = (bf16[4,4,128,128]{3,2,1,0:T(8,128)(2,1)S(1)}, f32[8,128]{1,0:T(8,128)S(1)}, s32[1]{0:T(128)}) custom-call(bf16[16,256]{1,0:T(8,128)(2,1)S(1)} %collective-permute-done.1.far_ref, bf16[16,256]{1,0:T(8,128)(2,1)S(1)} %get-tuple-element.71.note_ref, bf16[256,256]{1,0:T(8,128)(2,1)S(1)} %bitcast.6, bf16[256,256]{1,0:T(8,128)(2,1)S(1)} %bitcast.9, ...), custom_call_target="tpu_custom_call" | custom-call | tf_op jit(solution)/shard_map/cut_windows/pallas_call | solution.py:339
  29.1 0.0 copy-done.3
  29.1 0.0 copy-done.4
  29.2 0.0 copy-done.5
  29.2 36.0 %conditional.1 = ((bf16[2,128,256]{2,1,0:T(8,128)(2,1)S(1)}, f32[2,128,256]{2,1,0:T(8,128)S(1)}, bf16[2,128,256]{2,1,0:T(8,128)(2,1)S(1)})) conditional(s32[]{:T(128)} %bitcast.2, (bf16[4,4,128,128]{3,2,1,0:T(8,128)(2,1)S(1)}, bf16[2,128,128]{2,1,0:T(8,128)(2,1)S(1)}, f32[128,128]{1,0:T(8,128)S(1)}, f32[128,128]{1,0:T(8,128)S(1)}, ...), branch_computations={%region_0.0_spmd, %region_1.0_spmd} | conditional | bytes 3670064 | solution.py:392
  29.2 10.8 %all_to_all.16.window_ref = bf16[4,4,128,128]{3,2,1,0:T(8,128)(2,1)S(1)} all-to-all(bf16[4,4,128,128]{3,2,1,0:T(8,128)(2,1)S(1)} %get-tuple-element.42), channel_id=1, replica_groups={{0,128,256,384},{64,192,320,448},{1,129,257,385},{65,193,321,449},{2,13..., dimensions={0} | all-to-all | bytes 1048576 | tf_op jit(solution)/shard_map/cond/branch_0_fun/all_to_all | solution.py:375
  40.0 5.4 %collective-permute-start = (bf16[4,4,128,128]{3,2,1,0:T(8,128)(2,1)S(1)}, bf16[4,4,128,128]{3,2,1,0:T(8,128)(2,1)S(1)}, u32[]{:S(2)}, u32[]{:S(2)}) collective-permute-start(bf16[4,4,128,128]{3,2,1,0:T(8,128)(2,1)S(1)} %all_to_all.16.window_ref), channel_id=1, source_target_pairs={{0,64},{64,0},{128,192},{192,128},{256,320},{320,256},{384,448},{4... | collective-permute-start | bytes 1572872 | tf_op jit(solution)/shard_map/cond/branch_0_fun/ppermute | solution.py:376
  45.4 1.5 %collective-permute-done.other_ref = bf16[4,4,128,128]{3,2,1,0:T(8,128)(2,1)S(1)} collective-permute-done((bf16[4,4,128,128]{3,2,1,0:T(8,128)(2,1)S(1)}, bf16[4,4,128,128]{3,2,1,0:T(8,128)(2,1)S(1)}, u32[]{:S(2)}, u32[]{:S(2)}) %collective-permute-start) | collective-permute-done | bytes 524320 | tf_op jit(solution)/shard_map/cond/branch_0_fun/ppermute | solution.py:376
  46.9 8.9 %wave_chain.2 = bf16[4,2,128,128]{3,2,1,0:T(8,128)(2,1)S(1)} custom-call(bf16[4,4,128,128]{3,2,1,0:T(8,128)(2,1)S(1)} %all_to_all.16.window_ref, bf16[4,4,128,128]{3,2,1,0:T(8,128)(2,1)S(1)} %collective-permute-done.other_ref, bf16[2,128,128]{2,1,0:T(8,128)(2,1)S(1)} %get-tuple-element.43.probe_ref, f32[128,128]{1,0:T(8,128)S(1)} %get-tuple-element.44.cos_ref, ...), custom_call_target="tpu_custom_call" | custom-call | tf_op jit(solution)/shard_map/cond/branch_0_fun/wave_chain/pallas_call | solution.py:349
  55.7 8.8 %all_to_all.17.grad_ref = bf16[4,2,128,128]{3,2,1,0:T(8,128)(2,1)S(1)} all-to-all(bf16[4,2,128,128]{3,2,1,0:T(8,128)(2,1)S(1)} %wave_chain.2), channel_id=1, replica_groups={{0,128,256,384},{64,192,320,448},{1,129,257,385},{65,193,321,449},{2,13..., dimensions={0} | all-to-all | bytes 524288 | tf_op jit(solution)/shard_map/cond/branch_0_fun/all_to_all | solution.py:378
  64.5 0.6 add_windows.2
  65.2 2.2 %collective-permute-start.4 = (bf16[2,128,256]{2,1,0:T(8,128)(2,1)S(1)}, bf16[2,128,256]{2,1,0:T(8,128)(2,1)S(1)}, u32[]{:S(2)}, u32[]{:S(2)}) collective-permute-start(bf16[2,128,256]{2,1,0:T(8,128)(2,1)S(1)} %get-tuple-element.79), channel_id=1, source_target_pairs={{0,63},{1,2},{2,1},{3,4},{4,3},{5,6},{6,5},{7,8},{8,7},{9,10},{10,... | collective-permute-start | bytes 393224 | tf_op jit(solution)/shard_map/ppermute | solution.py:290
  67.4 3.4 %collective-permute-start.5 = (bf16[2,128,256]{2,1,0:T(8,128)(2,1)S(1)}, bf16[2,128,256]{2,1,0:T(8,128)(2,1)S(1)}, u32[]{:S(2)}, u32[]{:S(2)}) collective-permute-start(bf16[2,128,256]{2,1,0:T(8,128)(2,1)S(1)} %get-tuple-element.80), channel_id=1, source_target_pairs={{0,1},{1,0},{2,3},{3,2},{4,5},{5,4},{6,7},{7,6},{8,9},{9,8},{10,11... | collective-permute-start | bytes 393224 | tf_op jit(solution)/shard_map/ppermute | solution.py:290
  70.7 3.5 %collective-permute-done.4 = bf16[2,128,256]{2,1,0:T(8,128)(2,1)S(1)} collective-permute-done((bf16[2,128,256]{2,1,0:T(8,128)(2,1)S(1)}, bf16[2,128,256]{2,1,0:T(8,128)(2,1)S(1)}, u32[]{:S(2)}, u32[]{:S(2)}) %collective-permute-start.4) | collective-permute-done | bytes 131104 | tf_op jit(solution)/shard_map/ppermute | solution.py:290
  74.2 0.0 collective-permute-done.5
  74.2 0.7 add_bitcast_fusion
  (1 shorter events, 0.0 us)
Async XLA Ops:
  0.0 20.0 %copy-start = (f32[128,128]{1,0:T(8,128)S(1)}, f32[128,128]{1,0:T(8,128)}, u32[]{:S(2)}) copy-start(f32[128,128]{1,0:T(8,128)} %phase_ref.1) | copy-start | bytes 196612
  0.0 26.7 %copy-start.1 = (bf16[1,2,128,256]{3,2,1,0:T(8,128)(2,1)S(1)}, bf16[1,2,128,256]{3,2,1,0:T(8,128)(2,1)}, u32[]{:S(2)}) copy-start(bf16[1,2,128,256]{3,2,1,0:T(8,128)(2,1)} %param.10) | copy-start | bytes 393220
  0.0 26.7 %copy-start.2 = (bf16[1,2,128,256]{3,2,1,0:T(8,128)(2,1)S(1)}, bf16[1,2,128,256]{3,2,1,0:T(8,128)(2,1)}, u32[]{:S(2)}) copy-start(bf16[1,2,128,256]{3,2,1,0:T(8,128)(2,1)} %param.11) | copy-start | bytes 393220
  1.8 25.0 %collective-permute-start.3 = (bf16[528,256]{1,0:T(8,128)(2,1)}, bf16[528,256]{1,0:T(8,128)(2,1)S(1)}, u32[]{:S(2)}, u32[]{:S(2)}) collective-permute-start(bf16[528,256]{1,0:T(8,128)(2,1)} %get-tuple-element.72), channel_id=1, source_target_pairs={{0,63},{1,2},{2,1},{3,4},{4,3},{5,6},{6,5},{7,8},{8,7},{9,10},{10,... | collective-permute-start | bytes 811016 | tf_op jit(solution)/shard_map/ppermute | solution.py:290
  16.2 10.5 %collective-permute-start.2 = (bf16[528,256]{1,0:T(8,128)(2,1)}, bf16[528,256]{1,0:T(8,128)(2,1)S(1)}, u32[]{:S(2)}, u32[]{:S(2)}) collective-permute-start(bf16[528,256]{1,0:T(8,128)(2,1)} %get-tuple-element.72), channel_id=1, source_target_pairs={{0,1},{1,0},{2,3},{3,2},{4,5},{5,4},{6,7},{7,6},{8,9},{9,8},{10,11... | collective-permute-start | bytes 811016 | tf_op jit(solution)/shard_map/ppermute | solution.py:290
  18.1 8.6 %collective-permute-start.1 = (bf16[16,256]{1,0:T(8,128)(2,1)S(1)}, bf16[16,256]{1,0:T(8,128)(2,1)S(1)}, u32[]{:S(2)}, u32[]{:S(2)}) collective-permute-start(bf16[16,256]{1,0:T(8,128)(2,1)S(1)} %get-tuple-element.71.note_ref), channel_id=1, source_target_pairs={{0,2},{1,3},{2,4},{3,5},{4,6},{5,7},{6,8},{7,9},{8,10},{9,11},{10,... | collective-permute-start | bytes 24584 | tf_op jit(solution)/shard_map/ppermute | solution.py:316
  20.5 8.7 %copy-start.3 = (bf16[256,256]{1,0:T(8,128)(2,1)S(1)}, bf16[256,256]{1,0:T(8,128)(2,1)}, u32[]{:S(2)}) copy-start(bf16[256,256]{1,0:T(8,128)(2,1)} %constant.8.clone) | copy-start | bytes 393220
  20.5 8.6 %copy-start.4 = (bf16[256,256]{1,0:T(8,128)(2,1)S(1)}, bf16[256,256]{1,0:T(8,128)(2,1)}, u32[]{:S(2)}) copy-start(bf16[256,256]{1,0:T(8,128)(2,1)} %constant.7.clone) | copy-start | bytes 393220
  20.5 8.6 %copy-start.5 = (bf16[2,128,128]{2,1,0:T(8,128)(2,1)S(1)}, bf16[2,128,128]{2,1,0:T(8,128)(2,1)}, u32[]{:S(2)}) copy-start(bf16[2,128,128]{2,1,0:T(8,128)(2,1)} %param.12) | copy-start | bytes 196612
  40.0 6.9 %collective-permute-start = (bf16[4,4,128,128]{3,2,1,0:T(8,128)(2,1)S(1)}, bf16[4,4,128,128]{3,2,1,0:T(8,128)(2,1)S(1)}, u32[]{:S(2)}, u32[]{:S(2)}) collective-permute-start(bf16[4,4,128,128]{3,2,1,0:T(8,128)(2,1)S(1)} %all_to_all.16.window_ref), channel_id=1, source_target_pairs={{0,64},{64,0},{128,192},{192,128},{256,320},{320,256},{384,448},{4... | collective-permute-start | bytes 1572872 | tf_op jit(solution)/shard_map/cond/branch_0_fun/ppermute | solution.py:376
  65.2 9.0 %collective-permute-start.4 = (bf16[2,128,256]{2,1,0:T(8,128)(2,1)S(1)}, bf16[2,128,256]{2,1,0:T(8,128)(2,1)S(1)}, u32[]{:S(2)}, u32[]{:S(2)}) collective-permute-start(bf16[2,128,256]{2,1,0:T(8,128)(2,1)S(1)} %get-tuple-element.79), channel_id=1, source_target_pairs={{0,63},{1,2},{2,1},{3,4},{4,3},{5,6},{6,5},{7,8},{8,7},{9,10},{10,... | collective-permute-start | bytes 393224 | tf_op jit(solution)/shard_map/ppermute | solution.py:290
  67.4 6.8 %collective-permute-start.5 = (bf16[2,128,256]{2,1,0:T(8,128)(2,1)S(1)}, bf16[2,128,256]{2,1,0:T(8,128)(2,1)S(1)}, u32[]{:S(2)}, u32[]{:S(2)}) collective-permute-start(bf16[2,128,256]{2,1,0:T(8,128)(2,1)S(1)} %get-tuple-element.80), channel_id=1, source_target_pairs={{0,1},{1,0},{2,3},{3,2},{4,5},{5,4},{6,7},{7,6},{8,9},{9,8},{10,11... | collective-permute-start | bytes 393224 | tf_op jit(solution)/shard_map/ppermute | solution.py:290

commit v8 on v7

--- a/solution.py
+++ b/solution.py
@@ -20,7 +20,7 @@
     ((-1, 2), (-1, 2), (-1, 1), (-1, 0), (0, -1)),
     ((-1, 2), (-1, 2), (-1, 1), (-1, 0), (-1, -1)),
 )
-STRETCH = 1.6236604965019064
+STRETCH = 1.6236604965019064 / 16
 BF16 = jnp.bfloat16
 F32 = jnp.float32
 

time: 75.3 us -> 75.3 us (level)
  no operation moved by 1% of the time
where the time goes in v8:
time: 75.3 us; the launch traced here: 74.9 us
  starting transfers between devices  29.2 us (39%)
  blocking collectives  19.6 us (26%)
  Pallas kernels  13.4 us (18%)
  waiting for transfers between devices  11.2 us (15%)
  between operations  0.79 us (1%)
    ppermute x4, starting transfers between devices, exchanged(): lax.ppermute(block, 'strip', [(i, j % strip_count) for i, j in route])  21.9 us
    all_to_all x1, blocking collectives, one_per_chip(): lax.all_to_all(windows, 'cuts', 0, 0, axis_index_groups=same_core, tiled=...  10.8 us
    pallas_call x1, Pallas kernels, chain(): pl.pallas_call(functools.partial(chain_kernel, unit), out_shape=jax.Shape...  8.85 us
    all_to_all x1, blocking collectives, one_per_chip(): lax.all_to_all(gradient, 'cuts', 0, 0, axis_index_groups=same_core, tiled...  8.8 us
    ppermute x1, waiting for transfers between devices, on_device(): lax.ppermute(note, 'strip', [(i, (i + REACH) % strip_count) for i in rang...  6.2 us
    ppermute x1, starting transfers between devices, one_per_chip(): lax.ppermute(windows, 'cuts', [(i, i ^ 1) for i in range(cuts_count)])  5.4 us
    ppermute x4, waiting for transfers between devices, exchanged(): lax.ppermute(block, 'strip', [(i, j % strip_count) for i, j in route])  3.47 us
    ppermute x1, starting transfers between devices, on_device(): lax.ppermute(note, 'strip', [(i, (i + REACH) % strip_count) for i in rang...  1.92 us
  transfers between devices with their start and end apart: 6, of which 3 were waited for; matrix products, arithmetic and copies ran while one was open for 0% of the time, Pallas kernels for 1%

profile of v8, /device:TPU:1, one launch (start us, length us, event | category | flops | bytes accessed | tf_op | source)
XLA Modules:
  0.0 74.9 jit_solution(5379738819603666353)
XLA Ops:
  0.0 0.0 copy-start
  0.0 0.0 copy-start.1
  0.0 1.8 %pack_block.1 = (bf16[528,256]{1,0:T(8,128)(2,1)}, bf16[16,256]{1,0:T(8,128)(2,1)S(1)}) custom-call(s32[2]{0:T(128)} %row_any.1, s32[2]{0:T(128)} %col_any.1, bf16[256,256]{1,0:T(8,128)(2,1)} %bitcast.5, bf16[256,256]{1,0:T(8,128)(2,1)} %bitcast.8), custom_call_target="tpu_custom_call" | custom-call | tf_op jit(solution)/shard_map/pack_block/pallas_call | solution.py:300
  1.8 14.4 %collective-permute-start.3 = (bf16[528,256]{1,0:T(8,128)(2,1)}, bf16[528,256]{1,0:T(8,128)(2,1)S(1)}, u32[]{:S(2)}, u32[]{:S(2)}) collective-permute-start(bf16[528,256]{1,0:T(8,128)(2,1)} %get-tuple-element.72), channel_id=1, source_target_pairs={{0,63},{1,2},{2,1},{3,4},{4,3},{5,6},{6,5},{7,8},{8,7},{9,10},{10,... | collective-permute-start | bytes 811016 | tf_op jit(solution)/shard_map/ppermute | solution.py:290
  16.2 1.9 %collective-permute-start.2 = (bf16[528,256]{1,0:T(8,128)(2,1)}, bf16[528,256]{1,0:T(8,128)(2,1)S(1)}, u32[]{:S(2)}, u32[]{:S(2)}) collective-permute-start(bf16[528,256]{1,0:T(8,128)(2,1)} %get-tuple-element.72), channel_id=1, source_target_pairs={{0,1},{1,0},{2,3},{3,2},{4,5},{5,4},{6,7},{7,6},{8,9},{9,8},{10,11... | collective-permute-start | bytes 811016 | tf_op jit(solution)/shard_map/ppermute | solution.py:290
  18.1 1.9 %collective-permute-start.1 = (bf16[16,256]{1,0:T(8,128)(2,1)S(1)}, bf16[16,256]{1,0:T(8,128)(2,1)S(1)}, u32[]{:S(2)}, u32[]{:S(2)}) collective-permute-start(bf16[16,256]{1,0:T(8,128)(2,1)S(1)} %get-tuple-element.71.note_ref), channel_id=1, source_target_pairs={{0,2},{1,3},{2,4},{3,5},{4,6},{5,7},{6,8},{7,9},{8,10},{9,11},{10,... | collective-permute-start | bytes 24584 | tf_op jit(solution)/shard_map/ppermute | solution.py:316
  20.0 0.0 copy-done
  20.0 0.4 phase_tables.1
  20.5 0.0 copy-start.3
  20.5 0.0 copy-start.4
  20.5 0.0 copy-start.5
  20.5 6.2 %collective-permute-done.1.far_ref = bf16[16,256]{1,0:T(8,128)(2,1)S(1)} collective-permute-done((bf16[16,256]{1,0:T(8,128)(2,1)S(1)}, bf16[16,256]{1,0:T(8,128)(2,1)S(1)}, u32[]{:S(2)}, u32[]{:S(2)}) %collective-permute-start.1) | collective-permute-done | bytes 8224 | tf_op jit(solution)/shard_map/ppermute | solution.py:316
  26.7 0.0 collective-permute-done.3.first_ref
  26.7 0.0 collective-permute-done.2.second_ref
  26.7 0.0 copy-done.1
  26.7 0.0 copy-done.2
  26.7 1.7 %cut_windows.3 = (bf16[4,4,128,128]{3,2,1,0:T(8,128)(2,1)S(1)}, f32[8,128]{1,0:T(8,128)S(1)}, s32[1]{0:T(128)}) custom-call(bf16[16,256]{1,0:T(8,128)(2,1)S(1)} %collective-permute-done.1.far_ref, bf16[16,256]{1,0:T(8,128)(2,1)S(1)} %get-tuple-element.71.note_ref, bf16[256,256]{1,0:T(8,128)(2,1)S(1)} %bitcast.6, bf16[256,256]{1,0:T(8,128)(2,1)S(1)} %bitcast.9, ...), custom_call_target="tpu_custom_call" | custom-call | tf_op jit(solution)/shard_map/cut_windows/pallas_call | solution.py:339
  29.1 0.0 copy-done.3
  29.1 0.0 copy-done.4
  29.2 0.0 copy-done.5
  29.2 36.0 %conditional.1 = ((bf16[2,128,256]{2,1,0:T(8,128)(2,1)S(1)}, f32[2,128,256]{2,1,0:T(8,128)S(1)}, bf16[2,128,256]{2,1,0:T(8,128)(2,1)S(1)})) conditional(s32[]{:T(128)} %bitcast.2, (bf16[4,4,128,128]{3,2,1,0:T(8,128)(2,1)S(1)}, bf16[2,128,128]{2,1,0:T(8,128)(2,1)S(1)}, f32[128,128]{1,0:T(8,128)S(1)}, f32[128,128]{1,0:T(8,128)S(1)}, ...), branch_computations={%region_0.0_spmd, %region_1.0_spmd} | conditional | bytes 3670064 | solution.py:392
  29.2 10.8 %all_to_all.16.window_ref = bf16[4,4,128,128]{3,2,1,0:T(8,128)(2,1)S(1)} all-to-all(bf16[4,4,128,128]{3,2,1,0:T(8,128)(2,1)S(1)} %get-tuple-element.42), channel_id=1, replica_groups={{0,128,256,384},{64,192,320,448},{1,129,257,385},{65,193,321,449},{2,13..., dimensions={0} | all-to-all | bytes 1048576 | tf_op jit(solution)/shard_map/cond/branch_0_fun/all_to_all | solution.py:375
  40.0 5.4 %collective-permute-start = (bf16[4,4,128,128]{3,2,1,0:T(8,128)(2,1)S(1)}, bf16[4,4,128,128]{3,2,1,0:T(8,128)(2,1)S(1)}, u32[]{:S(2)}, u32[]{:S(2)}) collective-permute-start(bf16[4,4,128,128]{3,2,1,0:T(8,128)(2,1)S(1)} %all_to_all.16.window_ref), channel_id=1, source_target_pairs={{0,64},{64,0},{128,192},{192,128},{256,320},{320,256},{384,448},{4... | collective-permute-start | bytes 1572872 | tf_op jit(solution)/shard_map/cond/branch_0_fun/ppermute | solution.py:376
  45.4 1.5 %collective-permute-done.other_ref = bf16[4,4,128,128]{3,2,1,0:T(8,128)(2,1)S(1)} collective-permute-done((bf16[4,4,128,128]{3,2,1,0:T(8,128)(2,1)S(1)}, bf16[4,4,128,128]{3,2,1,0:T(8,128)(2,1)S(1)}, u32[]{:S(2)}, u32[]{:S(2)}) %collective-permute-start) | collective-permute-done | bytes 524320 | tf_op jit(solution)/shard_map/cond/branch_0_fun/ppermute | solution.py:376
  46.9 8.9 %wave_chain.2 = bf16[4,2,128,128]{3,2,1,0:T(8,128)(2,1)S(1)} custom-call(bf16[4,4,128,128]{3,2,1,0:T(8,128)(2,1)S(1)} %all_to_all.16.window_ref, bf16[4,4,128,128]{3,2,1,0:T(8,128)(2,1)S(1)} %collective-permute-done.other_ref, bf16[2,128,128]{2,1,0:T(8,128)(2,1)S(1)} %get-tuple-element.43.probe_ref, f32[128,128]{1,0:T(8,128)S(1)} %get-tuple-element.44.cos_ref, ...), custom_call_target="tpu_custom_call" | custom-call | tf_op jit(solution)/shard_map/cond/branch_0_fun/wave_chain/pallas_call | solution.py:349
  55.7 8.8 %all_to_all.17.grad_ref = bf16[4,2,128,128]{3,2,1,0:T(8,128)(2,1)S(1)} all-to-all(bf16[4,2,128,128]{3,2,1,0:T(8,128)(2,1)S(1)} %wave_chain.2), channel_id=1, replica_groups={{0,128,256,384},{64,192,320,448},{1,129,257,385},{65,193,321,449},{2,13..., dimensions={0} | all-to-all | bytes 524288 | tf_op jit(solution)/shard_map/cond/branch_0_fun/all_to_all | solution.py:378
  64.5 0.6 add_windows.2
  65.2 2.2 %collective-permute-start.4 = (bf16[2,128,256]{2,1,0:T(8,128)(2,1)S(1)}, bf16[2,128,256]{2,1,0:T(8,128)(2,1)S(1)}, u32[]{:S(2)}, u32[]{:S(2)}) collective-permute-start(bf16[2,128,256]{2,1,0:T(8,128)(2,1)S(1)} %get-tuple-element.79), channel_id=1, source_target_pairs={{0,63},{1,2},{2,1},{3,4},{4,3},{5,6},{6,5},{7,8},{8,7},{9,10},{10,... | collective-permute-start | bytes 393224 | tf_op jit(solution)/shard_map/ppermute | solution.py:290
  67.4 3.4 %collective-permute-start.5 = (bf16[2,128,256]{2,1,0:T(8,128)(2,1)S(1)}, bf16[2,128,256]{2,1,0:T(8,128)(2,1)S(1)}, u32[]{:S(2)}, u32[]{:S(2)}) collective-permute-start(bf16[2,128,256]{2,1,0:T(8,128)(2,1)S(1)} %get-tuple-element.80), channel_id=1, source_target_pairs={{0,1},{1,0},{2,3},{3,2},{4,5},{5,4},{6,7},{7,6},{8,9},{9,8},{10,11... | collective-permute-start | bytes 393224 | tf_op jit(solution)/shard_map/ppermute | solution.py:290
  70.7 3.5 %collective-permute-done.4 = bf16[2,128,256]{2,1,0:T(8,128)(2,1)S(1)} collective-permute-done((bf16[2,128,256]{2,1,0:T(8,128)(2,1)S(1)}, bf16[2,128,256]{2,1,0:T(8,128)(2,1)S(1)}, u32[]{:S(2)}, u32[]{:S(2)}) %collective-permute-start.4) | collective-permute-done | bytes 131104 | tf_op jit(solution)/shard_map/ppermute | solution.py:290
  74.2 0.0 collective-permute-done.5
  74.2 0.7 add_bitcast_fusion
  (1 shorter events, 0.0 us)
Async XLA Ops:
  0.0 20.0 %copy-start = (f32[128,128]{1,0:T(8,128)S(1)}, f32[128,128]{1,0:T(8,128)}, u32[]{:S(2)}) copy-start(f32[128,128]{1,0:T(8,128)} %phase_ref.1) | copy-start | bytes 196612
  0.0 26.7 %copy-start.1 = (bf16[1,2,128,256]{3,2,1,0:T(8,128)(2,1)S(1)}, bf16[1,2,128,256]{3,2,1,0:T(8,128)(2,1)}, u32[]{:S(2)}) copy-start(bf16[1,2,128,256]{3,2,1,0:T(8,128)(2,1)} %param.10) | copy-start | bytes 393220
  0.0 26.7 %copy-start.2 = (bf16[1,2,128,256]{3,2,1,0:T(8,128)(2,1)S(1)}, bf16[1,2,128,256]{3,2,1,0:T(8,128)(2,1)}, u32[]{:S(2)}) copy-start(bf16[1,2,128,256]{3,2,1,0:T(8,128)(2,1)} %param.11) | copy-start | bytes 393220
  1.8 25.0 %collective-permute-start.3 = (bf16[528,256]{1,0:T(8,128)(2,1)}, bf16[528,256]{1,0:T(8,128)(2,1)S(1)}, u32[]{:S(2)}, u32[]{:S(2)}) collective-permute-start(bf16[528,256]{1,0:T(8,128)(2,1)} %get-tuple-element.72), channel_id=1, source_target_pairs={{0,63},{1,2},{2,1},{3,4},{4,3},{5,6},{6,5},{7,8},{8,7},{9,10},{10,... | collective-permute-start | bytes 811016 | tf_op jit(solution)/shard_map/ppermute | solution.py:290
  16.2 10.5 %collective-permute-start.2 = (bf16[528,256]{1,0:T(8,128)(2,1)}, bf16[528,256]{1,0:T(8,128)(2,1)S(1)}, u32[]{:S(2)}, u32[]{:S(2)}) collective-permute-start(bf16[528,256]{1,0:T(8,128)(2,1)} %get-tuple-element.72), channel_id=1, source_target_pairs={{0,1},{1,0},{2,3},{3,2},{4,5},{5,4},{6,7},{7,6},{8,9},{9,8},{10,11... | collective-permute-start | bytes 811016 | tf_op jit(solution)/shard_map/ppermute | solution.py:290
  18.1 8.6 %collective-permute-start.1 = (bf16[16,256]{1,0:T(8,128)(2,1)S(1)}, bf16[16,256]{1,0:T(8,128)(2,1)S(1)}, u32[]{:S(2)}, u32[]{:S(2)}) collective-permute-start(bf16[16,256]{1,0:T(8,128)(2,1)S(1)} %get-tuple-element.71.note_ref), channel_id=1, source_target_pairs={{0,2},{1,3},{2,4},{3,5},{4,6},{5,7},{6,8},{7,9},{8,10},{9,11},{10,... | collective-permute-start | bytes 24584 | tf_op jit(solution)/shard_map/ppermute | solution.py:316
  20.5 8.7 %copy-start.3 = (bf16[256,256]{1,0:T(8,128)(2,1)S(1)}, bf16[256,256]{1,0:T(8,128)(2,1)}, u32[]{:S(2)}) copy-start(bf16[256,256]{1,0:T(8,128)(2,1)} %constant.8.clone) | copy-start | bytes 393220
  20.5 8.6 %copy-start.4 = (bf16[256,256]{1,0:T(8,128)(2,1)S(1)}, bf16[256,256]{1,0:T(8,128)(2,1)}, u32[]{:S(2)}) copy-start(bf16[256,256]{1,0:T(8,128)(2,1)} %constant.7.clone) | copy-start | bytes 393220
  20.5 8.6 %copy-start.5 = (bf16[2,128,128]{2,1,0:T(8,128)(2,1)S(1)}, bf16[2,128,128]{2,1,0:T(8,128)(2,1)}, u32[]{:S(2)}) copy-start(bf16[2,128,128]{2,1,0:T(8,128)(2,1)} %param.12) | copy-start | bytes 196612
  40.0 6.9 %collective-permute-start = (bf16[4,4,128,128]{3,2,1,0:T(8,128)(2,1)S(1)}, bf16[4,4,128,128]{3,2,1,0:T(8,128)(2,1)S(1)}, u32[]{:S(2)}, u32[]{:S(2)}) collective-permute-start(bf16[4,4,128,128]{3,2,1,0:T(8,128)(2,1)S(1)} %all_to_all.16.window_ref), channel_id=1, source_target_pairs={{0,64},{64,0},{128,192},{192,128},{256,320},{320,256},{384,448},{4... | collective-permute-start | bytes 1572872 | tf_op jit(solution)/shard_map/cond/branch_0_fun/ppermute | solution.py:376
  65.2 9.0 %collective-permute-start.4 = (bf16[2,128,256]{2,1,0:T(8,128)(2,1)S(1)}, bf16[2,128,256]{2,1,0:T(8,128)(2,1)S(1)}, u32[]{:S(2)}, u32[]{:S(2)}) collective-permute-start(bf16[2,128,256]{2,1,0:T(8,128)(2,1)S(1)} %get-tuple-element.79), channel_id=1, source_target_pairs={{0,63},{1,2},{2,1},{3,4},{4,3},{5,6},{6,5},{7,8},{8,7},{9,10},{10,... | collective-permute-start | bytes 393224 | tf_op jit(solution)/shard_map/ppermute | solution.py:290
  67.4 6.8 %collective-permute-start.5 = (bf16[2,128,256]{2,1,0:T(8,128)(2,1)S(1)}, bf16[2,128,256]{2,1,0:T(8,128)(2,1)S(1)}, u32[]{:S(2)}, u32[]{:S(2)}) collective-permute-start(bf16[2,128,256]{2,1,0:T(8,128)(2,1)S(1)} %get-tuple-element.80), channel_id=1, source_target_pairs={{0,1},{1,0},{2,3},{3,2},{4,5},{5,4},{6,7},{7,6},{8,9},{9,8},{10,11... | collective-permute-start | bytes 393224 | tf_op jit(solution)/shard_map/ppermute | solution.py:290

commit v9 on v8

--- a/solution.py
+++ b/solution.py
@@ -20,7 +20,7 @@
     ((-1, 2), (-1, 2), (-1, 1), (-1, 0), (0, -1)),
     ((-1, 2), (-1, 2), (-1, 1), (-1, 0), (-1, -1)),
 )
-STRETCH = 1.6236604965019064 / 16
+STRETCHES = (1.666129 / 16, 1.625068 / 16, 1.885787 / 16, 1.99216 / 16)
 BF16 = jnp.bfloat16
 F32 = jnp.float32
 
@@ -29,13 +29,16 @@
     index_line = np.arange(size)
     angle = (index_line[:, None] * index_line[None, :] % size) * (2.0 * math.pi / size)
     cosine, sine = np.cos(angle), np.sin(angle)
-    kept_cos = (STRETCH * cosine).astype(ml_dtypes.bfloat16).astype(np.float64)
-    kept_sin = (STRETCH * sine).astype(ml_dtypes.bfloat16).astype(np.float64)
-    unit = np.sum(kept_cos * cosine + kept_sin * sine) / np.sum(cosine**2 + sine**2)
-    unit = unit * math.sqrt(size)
-    plus = np.block([[kept_cos, kept_sin], [-kept_sin, kept_cos]])
-    minus = np.block([[kept_cos, -kept_sin], [kept_sin, kept_cos]])
-    return plus.astype(ml_dtypes.bfloat16), minus.astype(ml_dtypes.bfloat16), unit
+    tables, units = [], []
+    for stretch in STRETCHES:
+        kept_cos = (stretch * cosine).astype(ml_dtypes.bfloat16).astype(np.float64)
+        kept_sin = (stretch * sine).astype(ml_dtypes.bfloat16).astype(np.float64)
+        unit = np.sum(kept_cos * cosine + kept_sin * sine) / np.sum(cosine**2 + sine**2)
+        units.append(float(unit * math.sqrt(size)))
+        plus = np.block([[kept_cos, kept_sin], [-kept_sin, kept_cos]])
+        minus = np.block([[kept_cos, -kept_sin], [kept_sin, kept_cos]])
+        tables.append(np.stack([plus, minus]))
+    return np.stack(tables).astype(ml_dtypes.bfloat16), units
 
 
 def dot(left, right):
@@ -164,10 +167,9 @@
         out_ref[slots:] = jnp.zeros((targets - slots, parts, size, size), BF16)
 
 
-def chain_kernel(unit, window_ref, other_ref, probe_ref, cos_ref, sin_ref, plus_ref, minus_ref, out_ref, wave_ref):
+def chain_kernel(units, window_ref, other_ref, probe_ref, cos_ref, sin_ref, table_ref, out_ref, wave_ref):
     slices, _, size, _ = wave_ref.shape
     packed = window_ref.shape[0] < slices
-    plus, minus = plus_ref[...], minus_ref[...]
     even = lax.rem(lax.axis_index("cuts"), 2) == 0
 
     def window(layer, part):
@@ -190,13 +192,13 @@
         step = rows.shape[0] // 2
         return jnp.concatenate([dot(rows[i * step : (i + 1) * step], table) for i in range(2)], axis=0)
 
-    def forward(columns):
-        half = from_left(plus, columns.astype(BF16)).astype(BF16)
-        return from_right(swap(half), minus)
-
-    def inverse(rows):
-        half = from_right(rows.astype(BF16), plus).astype(BF16)
-        return from_left(minus, swap(half))
+    def forward(columns, table):
+        half = from_left(table_ref[table, 0], columns.astype(BF16)).astype(BF16)
+        return from_right(swap(half), table_ref[table, 1])
+
+    def inverse(rows, table):
+        half = from_right(rows.astype(BF16), table_ref[table, 0]).astype(BF16)
+        return from_left(table_ref[table, 1], swap(half))
 
     def kernel_times(rows, sign, scale):
         kernel_cos, kernel_sin = cos_ref[...] * scale, sin_ref[...] * (sign * scale)
@@ -209,8 +211,7 @@
 
     psi_re, psi_im = probe_ref[0].astype(F32), probe_ref[1].astype(F32)
     tan_re, tan_im = None, None
-    far_scale = 1.0 / unit**2
-    hop_scale = 1.0 / unit**4
+    scales = [1.0 / unit**2 for unit in units]
     for layer in range(slices):
         wave_ref[layer, 0], wave_ref[layer, 1] = psi_re, psi_im
         obj_re, obj_im = window(layer, 0), window(layer, 1)
@@ -225,17 +226,18 @@
         columns = jnp.concatenate([
             jnp.concatenate([exit_re, delta_re], axis=1),
             jnp.concatenate([exit_im, delta_im], axis=1)], axis=0)
-        spectrum = forward(columns)
+        there, back = 2 * (layer % 2), 2 * (layer % 2) + 1
+        spectrum = forward(columns, there)
         if layer < slices - 1:
-            waves = inverse(kernel_times(spectrum, 1.0, hop_scale))
+            waves = inverse(kernel_times(spectrum, 1.0, scales[there] * scales[back]), back)
             psi_re, tan_re = waves[:size, :size], waves[:size, size:]
             psi_im, tan_im = waves[size:, :size], waves[size:, size:]
         else:
-            far = kernel_times(spectrum, 1.0, far_scale)
+            far = kernel_times(spectrum, 1.0, scales[there])
     far_re, far_im = far[:size, :size], far[:size, size:]
     weight = (4.0 / slices) * (far_re * far[size:, :size] + far_im * far[size:, size:])
-    back = jnp.concatenate([weight * far_re, weight * far_im], axis=1)
-    adjoint = inverse(kernel_times(back, -1.0, far_scale))
+    weighted = jnp.concatenate([weight * far_re, weight * far_im], axis=1)
+    adjoint = inverse(kernel_times(weighted, -1.0, scales[back]), back)
     for layer in range(slices - 1, -1, -1):
         adj_re, adj_im = adjoint[:size], adjoint[size:]
         psi_re, psi_im = wave_ref[layer, 0], wave_ref[layer, 1]
@@ -250,7 +252,8 @@
             obj_re, obj_im = window(layer, 0), window(layer, 1)
             columns = jnp.concatenate(
                 [obj_re * adj_re + obj_im * adj_im, obj_re * adj_im - obj_im * adj_re], axis=0)
-            adjoint = inverse(kernel_times(forward(columns), -1.0, hop_scale))
+            there, back = 2 * (layer % 2), 2 * (layer % 2) + 1
+            adjoint = inverse(kernel_times(forward(columns, there), -1.0, scales[there] * scales[back]), back)
 
 
 def gather_kernel(most, start_ref, grad_ref, first_ref, own_ref, second_ref):
@@ -283,7 +286,7 @@
     patch_size = probe_wave.shape[1]
     strip_count = lax.axis_size("strip")
     cuts_count = lax.axis_size("cuts")
-    plus, minus, unit = transform_tables(patch_size)
+    tables, units = transform_tables(patch_size)
 
     def exchanged(block, offset):
         route = [(i, ((i - offset) ^ 1) + offset) for i in range(strip_count)]
@@ -345,16 +348,16 @@
             name="cut_windows",
         )(*operands)
 
-    def chain(windows, other, probe_wave, *tables):
+    def chain(windows, other, *constants):
         return pl.pallas_call(
-            functools.partial(chain_kernel, unit),
+            functools.partial(chain_kernel, units),
             out_shape=jax.ShapeDtypeStruct((windows.shape[0], 2, patch_size, patch_size), BF16),
-            in_specs=[vmem] * 7,
+            in_specs=[vmem] * 6,
             out_specs=vmem,
             scratch_shapes=[pltpu.VMEM((cuts_count, 2, patch_size, patch_size), F32)],
             compiler_params=params,
             name="wave_chain",
-        )(windows, other, probe_wave, *tables)
+        )(windows, other, *constants)
 
     def gather(start, gradient):
         return pl.pallas_call(
@@ -388,7 +391,7 @@
 
     around = (far, note, objects, directions, second, first)
     windows, start, count = cut(chips, True, *around)
-    constants = (probe_wave, kernel_cos, kernel_sin, jnp.asarray(plus), jnp.asarray(minus))
+    constants = (probe_wave, kernel_cos, kernel_sin, jnp.asarray(tables))
     first, own, second = lax.cond(
         count[0] > chips, one_per_device, one_per_chip, windows, start, around, constants
     )

time: 75.3 us -> 76.5 us (1.016)
  Pallas kernels: 13.4 us -> 14.4 us
    pallas_call x1, Pallas kernels: 1.73 us -> 2.69 us  [cut(): pl.pallas_call(functools.partial(cut_kernel, strip_rows, near), out_shape...]
where the time goes in v9:
time: 76.5 us; the launch traced here: 76.1 us
  starting transfers between devices  29.2 us (38%)
  blocking collectives  19.7 us (26%)
  Pallas kernels  14.4 us (19%)
  waiting for transfers between devices  11.2 us (15%)
    ppermute x4, starting transfers between devices, exchanged(): lax.ppermute(block, 'strip', [(i, j % strip_count) for i, j in route])  21.9 us
    all_to_all x1, blocking collectives, one_per_chip(): lax.all_to_all(windows, 'cuts', 0, 0, axis_index_groups=same_core, tiled=...  10.9 us
    pallas_call x1, Pallas kernels, chain(): pl.pallas_call(functools.partial(chain_kernel, units), out_shape=jax.Shap...  8.86 us
    all_to_all x1, blocking collectives, one_per_chip(): lax.all_to_all(gradient, 'cuts', 0, 0, axis_index_groups=same_core, tiled...  8.81 us
    ppermute x1, waiting for transfers between devices, on_device(): lax.ppermute(note, 'strip', [(i, (i + REACH) % strip_count) for i in rang...  6.24 us
    ppermute x1, starting transfers between devices, one_per_chip(): lax.ppermute(windows, 'cuts', [(i, i ^ 1) for i in range(cuts_count)])  5.4 us
    ppermute x4, waiting for transfers between devices, exchanged(): lax.ppermute(block, 'strip', [(i, j % strip_count) for i, j in route])  3.46 us
    pallas_call x1, Pallas kernels, cut(): pl.pallas_call(functools.partial(cut_kernel, strip_rows, near), out_shape...  2.69 us
  transfers between devices with their start and end apart: 6, of which 3 were waited for; matrix products, arithmetic and copies ran while one was open for 0% of the time, Pallas kernels for 1%

profile of v9, /device:TPU:1, one launch (start us, length us, event | category | flops | bytes accessed | tf_op | source)
XLA Modules:
  0.0 76.1 jit_solution(42256307672857484)
XLA Ops:
  0.0 0.0 copy-start
  0.0 0.0 copy-start.1
  0.0 1.8 %pack_block.1 = (bf16[528,256]{1,0:T(8,128)(2,1)}, bf16[16,256]{1,0:T(8,128)(2,1)S(1)}) custom-call(s32[2]{0:T(128)} %row_any.1, s32[2]{0:T(128)} %col_any.1, bf16[256,256]{1,0:T(8,128)(2,1)} %bitcast.5, bf16[256,256]{1,0:T(8,128)(2,1)} %bitcast.8), custom_call_target="tpu_custom_call" | custom-call | tf_op jit(solution)/shard_map/pack_block/pallas_call | solution.py:303
  1.8 14.4 %collective-permute-start.3 = (bf16[528,256]{1,0:T(8,128)(2,1)}, bf16[528,256]{1,0:T(8,128)(2,1)S(1)}, u32[]{:S(2)}, u32[]{:S(2)}) collective-permute-start(bf16[528,256]{1,0:T(8,128)(2,1)} %get-tuple-element.66), channel_id=1, source_target_pairs={{0,63},{1,2},{2,1},{3,4},{4,3},{5,6},{6,5},{7,8},{8,7},{9,10},{10,... | collective-permute-start | bytes 811016 | tf_op jit(solution)/shard_map/ppermute | solution.py:293
  16.2 1.9 %collective-permute-start.2 = (bf16[528,256]{1,0:T(8,128)(2,1)}, bf16[528,256]{1,0:T(8,128)(2,1)S(1)}, u32[]{:S(2)}, u32[]{:S(2)}) collective-permute-start(bf16[528,256]{1,0:T(8,128)(2,1)} %get-tuple-element.66), channel_id=1, source_target_pairs={{0,1},{1,0},{2,3},{3,2},{4,5},{5,4},{6,7},{7,6},{8,9},{9,8},{10,11... | collective-permute-start | bytes 811016 | tf_op jit(solution)/shard_map/ppermute | solution.py:293
  18.1 1.9 %collective-permute-start.1 = (bf16[16,256]{1,0:T(8,128)(2,1)S(1)}, bf16[16,256]{1,0:T(8,128)(2,1)S(1)}, u32[]{:S(2)}, u32[]{:S(2)}) collective-permute-start(bf16[16,256]{1,0:T(8,128)(2,1)S(1)} %get-tuple-element.65.note_ref), channel_id=1, source_target_pairs={{0,2},{1,3},{2,4},{3,5},{4,6},{5,7},{6,8},{7,9},{8,10},{9,11},{10,... | collective-permute-start | bytes 24584 | tf_op jit(solution)/shard_map/ppermute | solution.py:319
  20.1 0.0 copy-done
  20.1 0.4 phase_tables.1
  20.5 6.2 %collective-permute-done.1.far_ref = bf16[16,256]{1,0:T(8,128)(2,1)S(1)} collective-permute-done((bf16[16,256]{1,0:T(8,128)(2,1)S(1)}, bf16[16,256]{1,0:T(8,128)(2,1)S(1)}, u32[]{:S(2)}, u32[]{:S(2)}) %collective-permute-start.1) | collective-permute-done | bytes 8224 | tf_op jit(solution)/shard_map/ppermute | solution.py:319
  26.8 0.0 collective-permute-done.3.first_ref
  26.8 0.0 collective-permute-done.2.second_ref
  26.8 2.7 %cut_windows.3 = (bf16[4,4,128,128]{3,2,1,0:T(8,128)(2,1)S(1)}, f32[8,128]{1,0:T(8,128)S(1)}, s32[1]{0:T(128)}) custom-call(bf16[16,256]{1,0:T(8,128)(2,1)S(1)} %collective-permute-done.1.far_ref, bf16[16,256]{1,0:T(8,128)(2,1)S(1)} %get-tuple-element.65.note_ref, bf16[256,256]{1,0:T(8,128)(2,1)} %bitcast.6, bf16[256,256]{1,0:T(8,128)(2,1)} %bitcast.9, ...), custom_call_target="tpu_custom_call" | custom-call | tf_op jit(solution)/shard_map/cut_windows/pallas_call | solution.py:342
  30.1 0.0 copy-done.1
  30.1 36.2 %conditional.1 = ((bf16[2,128,256]{2,1,0:T(8,128)(2,1)S(1)}, f32[2,128,256]{2,1,0:T(8,128)S(1)}, bf16[2,128,256]{2,1,0:T(8,128)(2,1)S(1)})) conditional(s32[]{:T(128)} %bitcast.2, (bf16[4,4,128,128]{3,2,1,0:T(8,128)(2,1)S(1)}, bf16[2,128,128]{2,1,0:T(8,128)(2,1)}, f32[128,128]{1,0:T(8,128)S(1)}, f32[128,128]{1,0:T(8,128)S(1)}, ...), branch_computations={%region_0.0_spmd, %region_1.0_spmd} | conditional | bytes 3932236 | solution.py:395
  30.1 0.0 copy-start.2
  30.1 10.9 %all_to_all.16.window_ref = bf16[4,4,128,128]{3,2,1,0:T(8,128)(2,1)S(1)} all-to-all(bf16[4,4,128,128]{3,2,1,0:T(8,128)(2,1)S(1)} %get-tuple-element.38), channel_id=1, replica_groups={{0,128,256,384},{64,192,320,448},{1,129,257,385},{65,193,321,449},{2,13..., dimensions={0} | all-to-all | bytes 1048576 | tf_op jit(solution)/shard_map/cond/branch_0_fun/all_to_all | solution.py:378
  41.1 5.4 %collective-permute-start = (bf16[4,4,128,128]{3,2,1,0:T(8,128)(2,1)S(1)}, bf16[4,4,128,128]{3,2,1,0:T(8,128)(2,1)S(1)}, u32[]{:S(2)}, u32[]{:S(2)}) collective-permute-start(bf16[4,4,128,128]{3,2,1,0:T(8,128)(2,1)S(1)} %all_to_all.16.window_ref), channel_id=1, source_target_pairs={{0,64},{64,0},{128,192},{192,128},{256,320},{320,256},{384,448},{4... | collective-permute-start | bytes 1572872 | tf_op jit(solution)/shard_map/cond/branch_0_fun/ppermute | solution.py:379
  46.5 1.5 %collective-permute-done.other_ref = bf16[4,4,128,128]{3,2,1,0:T(8,128)(2,1)S(1)} collective-permute-done((bf16[4,4,128,128]{3,2,1,0:T(8,128)(2,1)S(1)}, bf16[4,4,128,128]{3,2,1,0:T(8,128)(2,1)S(1)}, u32[]{:S(2)}, u32[]{:S(2)}) %collective-permute-start) | collective-permute-done | bytes 524320 | tf_op jit(solution)/shard_map/cond/branch_0_fun/ppermute | solution.py:379
  48.0 0.0 copy-done.2
  48.0 8.9 %wave_chain.2 = bf16[4,2,128,128]{3,2,1,0:T(8,128)(2,1)S(1)} custom-call(bf16[4,4,128,128]{3,2,1,0:T(8,128)(2,1)S(1)} %all_to_all.16.window_ref, bf16[4,4,128,128]{3,2,1,0:T(8,128)(2,1)S(1)} %collective-permute-done.other_ref, bf16[2,128,128]{2,1,0:T(8,128)(2,1)S(1)} %copy-done.2, f32[128,128]{1,0:T(8,128)S(1)} %get-tuple-element.40.cos_ref, ...), custom_call_target="tpu_custom_call" | custom-call | tf_op jit(solution)/shard_map/cond/branch_0_fun/wave_chain/pallas_call | solution.py:352
  56.9 8.8 %all_to_all.17.grad_ref = bf16[4,2,128,128]{3,2,1,0:T(8,128)(2,1)S(1)} all-to-all(bf16[4,2,128,128]{3,2,1,0:T(8,128)(2,1)S(1)} %wave_chain.2), channel_id=1, replica_groups={{0,128,256,384},{64,192,320,448},{1,129,257,385},{65,193,321,449},{2,13..., dimensions={0} | all-to-all | bytes 524288 | tf_op jit(solution)/shard_map/cond/branch_0_fun/all_to_all | solution.py:381
  65.7 0.6 add_windows.2
  66.3 2.2 %collective-permute-start.4 = (bf16[2,128,256]{2,1,0:T(8,128)(2,1)S(1)}, bf16[2,128,256]{2,1,0:T(8,128)(2,1)S(1)}, u32[]{:S(2)}, u32[]{:S(2)}) collective-permute-start(bf16[2,128,256]{2,1,0:T(8,128)(2,1)S(1)} %get-tuple-element.73), channel_id=1, source_target_pairs={{0,63},{1,2},{2,1},{3,4},{4,3},{5,6},{6,5},{7,8},{8,7},{9,10},{10,... | collective-permute-start | bytes 393224 | tf_op jit(solution)/shard_map/ppermute | solution.py:293
  68.5 3.4 %collective-permute-start.5 = (bf16[2,128,256]{2,1,0:T(8,128)(2,1)S(1)}, bf16[2,128,256]{2,1,0:T(8,128)(2,1)S(1)}, u32[]{:S(2)}, u32[]{:S(2)}) collective-permute-start(bf16[2,128,256]{2,1,0:T(8,128)(2,1)S(1)} %get-tuple-element.74), channel_id=1, source_target_pairs={{0,1},{1,0},{2,3},{3,2},{4,5},{5,4},{6,7},{7,6},{8,9},{9,8},{10,11... | collective-permute-start | bytes 393224 | tf_op jit(solution)/shard_map/ppermute | solution.py:293
  71.9 3.5 %collective-permute-done.4 = bf16[2,128,256]{2,1,0:T(8,128)(2,1)S(1)} collective-permute-done((bf16[2,128,256]{2,1,0:T(8,128)(2,1)S(1)}, bf16[2,128,256]{2,1,0:T(8,128)(2,1)S(1)}, u32[]{:S(2)}, u32[]{:S(2)}) %collective-permute-start.4) | collective-permute-done | bytes 131104 | tf_op jit(solution)/shard_map/ppermute | solution.py:293
  75.3 0.0 collective-permute-done.5
  75.3 0.7 add_bitcast_fusion
Async XLA Ops:
  0.0 20.1 %copy-start = (f32[128,128]{1,0:T(8,128)S(1)}, f32[128,128]{1,0:T(8,128)}, u32[]{:S(2)}) copy-start(f32[128,128]{1,0:T(8,128)} %phase_ref.1) | copy-start | bytes 196612
  0.0 30.1 %copy-start.1 = (bf16[4,2,256,256]{3,2,1,0:T(8,128)(2,1)S(1)}, bf16[4,2,256,256]{3,2,1,0:T(8,128)(2,1)}, u32[]{:S(2)}) copy-start(bf16[4,2,256,256]{3,2,1,0:T(8,128)(2,1)} %constant.5.clone) | copy-start | bytes 3145732
  1.8 25.0 %collective-permute-start.3 = (bf16[528,256]{1,0:T(8,128)(2,1)}, bf16[528,256]{1,0:T(8,128)(2,1)S(1)}, u32[]{:S(2)}, u32[]{:S(2)}) collective-permute-start(bf16[528,256]{1,0:T(8,128)(2,1)} %get-tuple-element.66), channel_id=1, source_target_pairs={{0,63},{1,2},{2,1},{3,4},{4,3},{5,6},{6,5},{7,8},{8,7},{9,10},{10,... | collective-permute-start | bytes 811016 | tf_op jit(solution)/shard_map/ppermute | solution.py:293
  16.2 10.5 %collective-permute-start.2 = (bf16[528,256]{1,0:T(8,128)(2,1)}, bf16[528,256]{1,0:T(8,128)(2,1)S(1)}, u32[]{:S(2)}, u32[]{:S(2)}) collective-permute-start(bf16[528,256]{1,0:T(8,128)(2,1)} %get-tuple-element.66), channel_id=1, source_target_pairs={{0,1},{1,0},{2,3},{3,2},{4,5},{5,4},{6,7},{7,6},{8,9},{9,8},{10,11... | collective-permute-start | bytes 811016 | tf_op jit(solution)/shard_map/ppermute | solution.py:293
  18.1 8.6 %collective-permute-start.1 = (bf16[16,256]{1,0:T(8,128)(2,1)S(1)}, bf16[16,256]{1,0:T(8,128)(2,1)S(1)}, u32[]{:S(2)}, u32[]{:S(2)}) collective-permute-start(bf16[16,256]{1,0:T(8,128)(2,1)S(1)} %get-tuple-element.65.note_ref), channel_id=1, source_target_pairs={{0,2},{1,3},{2,4},{3,5},{4,6},{5,7},{6,8},{7,9},{8,10},{9,11},{10,... | collective-permute-start | bytes 24584 | tf_op jit(solution)/shard_map/ppermute | solution.py:319
  30.1 17.9 %copy-start.2 = (bf16[2,128,128]{2,1,0:T(8,128)(2,1)S(1)}, bf16[2,128,128]{2,1,0:T(8,128)(2,1)}, u32[]{:S(2)}) copy-start(bf16[2,128,128]{2,1,0:T(8,128)(2,1)} %get-tuple-element.39.probe_ref) | copy-start | bytes 196612 | tf_op jit(solution)/shard_map/cond
  41.1 6.9 %collective-permute-start = (bf16[4,4,128,128]{3,2,1,0:T(8,128)(2,1)S(1)}, bf16[4,4,128,128]{3,2,1,0:T(8,128)(2,1)S(1)}, u32[]{:S(2)}, u32[]{:S(2)}) collective-permute-start(bf16[4,4,128,128]{3,2,1,0:T(8,128)(2,1)S(1)} %all_to_all.16.window_ref), channel_id=1, source_target_pairs={{0,64},{64,0},{128,192},{192,128},{256,320},{320,256},{384,448},{4... | collective-permute-start | bytes 1572872 | tf_op jit(solution)/shard_map/cond/branch_0_fun/ppermute | solution.py:379
  66.3 9.0 %collective-permute-start.4 = (bf16[2,128,256]{2,1,0:T(8,128)(2,1)S(1)}, bf16[2,128,256]{2,1,0:T(8,128)(2,1)S(1)}, u32[]{:S(2)}, u32[]{:S(2)}) collective-permute-start(bf16[2,128,256]{2,1,0:T(8,128)(2,1)S(1)} %get-tuple-element.73), channel_id=1, source_target_pairs={{0,63},{1,2},{2,1},{3,4},{4,3},{5,6},{6,5},{7,8},{8,7},{9,10},{10,... | collective-permute-start | bytes 393224 | tf_op jit(solution)/shard_map/ppermute | solution.py:293
  68.5 6.8 %collective-permute-start.5 = (bf16[2,128,256]{2,1,0:T(8,128)(2,1)S(1)}, bf16[2,128,256]{2,1,0:T(8,128)(2,1)S(1)}, u32[]{:S(2)}, u32[]{:S(2)}) collective-permute-start(bf16[2,128,256]{2,1,0:T(8,128)(2,1)S(1)} %get-tuple-element.74), channel_id=1, source_target_pairs={{0,1},{1,0},{2,3},{3,2},{4,5},{5,4},{6,7},{7,6},{8,9},{9,8},{10,11... | collective-permute-start | bytes 393224 | tf_op jit(solution)/shard_map/ppermute | solution.py:293

commit v10 on v9

--- a/solution.py
+++ b/solution.py
@@ -35,9 +35,7 @@
         kept_sin = (stretch * sine).astype(ml_dtypes.bfloat16).astype(np.float64)
         unit = np.sum(kept_cos * cosine + kept_sin * sine) / np.sum(cosine**2 + sine**2)
         units.append(float(unit * math.sqrt(size)))
-        plus = np.block([[kept_cos, kept_sin], [-kept_sin, kept_cos]])
-        minus = np.block([[kept_cos, -kept_sin], [kept_sin, kept_cos]])
-        tables.append(np.stack([plus, minus]))
+        tables.append(np.concatenate([kept_cos, kept_sin], axis=1))
     return np.stack(tables).astype(ml_dtypes.bfloat16), units
 
 
@@ -100,9 +98,18 @@
         copy.wait()
 
 
-def phase_kernel(phase_ref, cos_ref, sin_ref):
+def phase_kernel(phase_ref, half_ref, cos_ref, sin_ref, table_ref):
     cos_ref[...] = jnp.cos(phase_ref[...])
     sin_ref[...] = jnp.sin(phase_ref[...])
+    count, size, _ = half_ref.shape
+    low, high = slice(0, size), slice(size, 2 * size)
+    for table in range(count):
+        cosine, sine = half_ref[table, :, low], half_ref[table, :, high]
+        for side, upper, lower in ((0, sine, -sine), (1, -sine, sine)):
+            table_ref[table, side, low, low] = cosine
+            table_ref[table, side, low, high] = upper
+            table_ref[table, side, high, low] = lower
+            table_ref[table, side, high, high] = cosine
 
 
 def strips_around(first_ref, own, second_ref):
@@ -286,7 +293,7 @@
     patch_size = probe_wave.shape[1]
     strip_count = lax.axis_size("strip")
     cuts_count = lax.axis_size("cuts")
-    tables, units = transform_tables(patch_size)
+    halves, units = transform_tables(patch_size)
 
     def exchanged(block, offset):
         route = [(i, ((i - offset) ^ 1) + offset) for i in range(strip_count)]
@@ -318,14 +325,18 @@
     )(corner_row, corner_col, objects, directions)
     far = lax.ppermute(note, "strip", [(i, (i + REACH) % strip_count) for i in range(strip_count)])
     first, second = exchanged(block, -1), exchanged(block, 0)
-    kernel_cos, kernel_sin = pl.pallas_call(
+    kernel_cos, kernel_sin, tables = pl.pallas_call(
         phase_kernel,
-        out_shape=(jax.ShapeDtypeStruct(kernel_phase.shape, F32),) * 2,
-        in_specs=[vmem],
-        out_specs=(vmem,) * 2,
+        out_shape=(
+            jax.ShapeDtypeStruct(kernel_phase.shape, F32),
+            jax.ShapeDtypeStruct(kernel_phase.shape, F32),
+            jax.ShapeDtypeStruct((len(units), 2, 2 * patch_size, 2 * patch_size), BF16),
+        ),
+        in_specs=[vmem] * 2,
+        out_specs=(vmem,) * 3,
         compiler_params=params,
         name="phase_tables",
-    )(kernel_phase)
+    )(kernel_phase, jnp.asarray(halves))
     near = corner_row.shape[0]
     strip_shape = (2, strip_rows, column_count)
 
@@ -391,7 +402,7 @@
 
     around = (far, note, objects, directions, second, first)
     windows, start, count = cut(chips, True, *around)
-    constants = (probe_wave, kernel_cos, kernel_sin, jnp.asarray(tables))
+    constants = (probe_wave, kernel_cos, kernel_sin, tables)
     first, own, second = lax.cond(
         count[0] > chips, one_per_device, one_per_chip, windows, start, around, constants
     )

time: 76.5 us -> 75.3 us (0.984)
  Pallas kernels: 14.4 us -> 13.5 us
  waiting for transfers between devices: 11.2 us -> 10.3 us
  local copies, waits for them, and re-layouts: 0.01 us -> 0.85 us
    pallas_call x1, Pallas kernels: 2.69 us -> 1.73 us  [cut(): pl.pallas_call(functools.partial(cut_kernel, strip_rows, near), out_shape...]
    ppermute x1, waiting for transfers between devices: 6.24 us -> 5.31 us  [on_device(): lax.ppermute(note, 'strip', [(i, (i + REACH) % strip_count) for i in rang...]
    unnamed x4 -> x10, local copies, waits for them, and re-layouts: 0.01 us -> 0.85 us
where the time goes in v10:
time: 75.3 us; the launch traced here: 74.9 us
  starting transfers between devices  29.2 us (39%)
  blocking collectives  19.6 us (26%)
  Pallas kernels  13.5 us (18%)
  waiting for transfers between devices  10.3 us (14%)
  local copies, waits for them, and re-layouts  0.85 us (1%)
  between operations  0.76 us (1%)
    ppermute x4, starting transfers between devices, exchanged(): lax.ppermute(block, 'strip', [(i, j % strip_count) for i, j in route])  21.9 us
    all_to_all x1, blocking collectives, one_per_chip(): lax.all_to_all(windows, 'cuts', 0, 0, axis_index_groups=same_core, tiled=...  10.8 us
    pallas_call x1, Pallas kernels, chain(): pl.pallas_call(functools.partial(chain_kernel, units), out_shape=jax.Shap...  8.85 us
    all_to_all x1, blocking collectives, one_per_chip(): lax.all_to_all(gradient, 'cuts', 0, 0, axis_index_groups=same_core, tiled...  8.79 us
    ppermute x1, starting transfers between devices, one_per_chip(): lax.ppermute(windows, 'cuts', [(i, i ^ 1) for i in range(cuts_count)])  5.4 us
    ppermute x1, waiting for transfers between devices, on_device(): lax.ppermute(note, 'strip', [(i, (i + REACH) % strip_count) for i in rang...  5.31 us
    ppermute x4, waiting for transfers between devices, exchanged(): lax.ppermute(block, 'strip', [(i, j % strip_count) for i, j in route])  3.46 us
    ppermute x1, starting transfers between devices, on_device(): lax.ppermute(note, 'strip', [(i, (i + REACH) % strip_count) for i in rang...  1.92 us
  transfers between devices with their start and end apart: 6, of which 3 were waited for; matrix products, arithmetic and copies ran while one was open for 0% of the time, Pallas kernels for 1%

profile of v10, /device:TPU:1, one launch (start us, length us, event | category | flops | bytes accessed | tf_op | source)
XLA Modules:
  0.0 74.9 jit_solution(6152382785057755984)
XLA Ops:
  0.0 0.0 copy-start
  0.0 1.8 %pack_block.1 = (bf16[528,256]{1,0:T(8,128)(2,1)}, bf16[16,256]{1,0:T(8,128)(2,1)S(1)}) custom-call(s32[2]{0:T(128)} %row_any.1, s32[2]{0:T(128)} %col_any.1, bf16[256,256]{1,0:T(8,128)(2,1)} %bitcast.5, bf16[256,256]{1,0:T(8,128)(2,1)} %bitcast.8), custom_call_target="tpu_custom_call" | custom-call | tf_op jit(solution)/shard_map/pack_block/pallas_call | solution.py:310
  1.8 14.4 %collective-permute-start.3 = (bf16[528,256]{1,0:T(8,128)(2,1)}, bf16[528,256]{1,0:T(8,128)(2,1)S(1)}, u32[]{:S(2)}, u32[]{:S(2)}) collective-permute-start(bf16[528,256]{1,0:T(8,128)(2,1)} %get-tuple-element.67), channel_id=1, source_target_pairs={{0,63},{1,2},{2,1},{3,4},{4,3},{5,6},{6,5},{7,8},{8,7},{9,10},{10,... | collective-permute-start | bytes 811016 | tf_op jit(solution)/shard_map/ppermute | solution.py:300
  16.2 1.9 %collective-permute-start.2 = (bf16[528,256]{1,0:T(8,128)(2,1)}, bf16[528,256]{1,0:T(8,128)(2,1)S(1)}, u32[]{:S(2)}, u32[]{:S(2)}) collective-permute-start(bf16[528,256]{1,0:T(8,128)(2,1)} %get-tuple-element.67), channel_id=1, source_target_pairs={{0,1},{1,0},{2,3},{3,2},{4,5},{5,4},{6,7},{7,6},{8,9},{9,8},{10,11... | collective-permute-start | bytes 811016 | tf_op jit(solution)/shard_map/ppermute | solution.py:300
  18.1 1.9 %collective-permute-start.1 = (bf16[16,256]{1,0:T(8,128)(2,1)S(1)}, bf16[16,256]{1,0:T(8,128)(2,1)S(1)}, u32[]{:S(2)}, u32[]{:S(2)}) collective-permute-start(bf16[16,256]{1,0:T(8,128)(2,1)S(1)} %get-tuple-element.66.note_ref), channel_id=1, source_target_pairs={{0,2},{1,3},{2,4},{3,5},{4,6},{5,7},{6,8},{7,9},{8,10},{9,11},{10,... | collective-permute-start | bytes 24584 | tf_op jit(solution)/shard_map/ppermute | solution.py:326
  20.0 0.0 copy-done
  20.0 0.0 copy-start.1
  20.1 0.8 %copy-done.1 = f32[128,128]{1,0:T(8,128)S(1)} copy-done((f32[128,128]{1,0:T(8,128)S(1)}, f32[128,128]{1,0:T(8,128)}, u32[]{:S(2)}) %copy-start.1) | copy-done | bytes 65560
  20.9 0.0 copy-start.2
  20.9 0.0 copy-start.3
  20.9 0.5 phase_tables.1
  21.4 0.0 copy-start.4
  21.4 5.3 %collective-permute-done.1.far_ref = bf16[16,256]{1,0:T(8,128)(2,1)S(1)} collective-permute-done((bf16[16,256]{1,0:T(8,128)(2,1)S(1)}, bf16[16,256]{1,0:T(8,128)(2,1)S(1)}, u32[]{:S(2)}, u32[]{:S(2)}) %collective-permute-start.1) | collective-permute-done | bytes 8224 | tf_op jit(solution)/shard_map/ppermute | solution.py:326
  26.7 0.0 collective-permute-done.3.first_ref
  26.7 0.0 collective-permute-done.2.second_ref
  26.7 0.0 copy-done.2
  26.7 0.0 copy-done.3
  26.7 1.7 %cut_windows.3 = (bf16[4,4,128,128]{3,2,1,0:T(8,128)(2,1)S(1)}, f32[8,128]{1,0:T(8,128)S(1)}, s32[1]{0:T(128)}) custom-call(bf16[16,256]{1,0:T(8,128)(2,1)S(1)} %collective-permute-done.1.far_ref, bf16[16,256]{1,0:T(8,128)(2,1)S(1)} %get-tuple-element.66.note_ref, bf16[256,256]{1,0:T(8,128)(2,1)S(1)} %bitcast.6, bf16[256,256]{1,0:T(8,128)(2,1)S(1)} %bitcast.9, ...), custom_call_target="tpu_custom_call" | custom-call | tf_op jit(solution)/shard_map/cut_windows/pallas_call | solution.py:353
  29.1 0.0 copy-done.4
  29.1 36.0 %conditional.1 = ((bf16[2,128,256]{2,1,0:T(8,128)(2,1)S(1)}, f32[2,128,256]{2,1,0:T(8,128)S(1)}, bf16[2,128,256]{2,1,0:T(8,128)(2,1)S(1)})) conditional(s32[]{:T(128)} %bitcast.2, (bf16[4,4,128,128]{3,2,1,0:T(8,128)(2,1)S(1)}, bf16[2,128,128]{2,1,0:T(8,128)(2,1)S(1)}, f32[128,128]{1,0:T(8,128)S(1)}, f32[128,128]{1,0:T(8,128)S(1)}, ...), branch_computations={%region_0.0_spmd, %region_1.0_spmd} | conditional | bytes 3670064 | solution.py:406
  29.1 10.8 %all_to_all.16.window_ref = bf16[4,4,128,128]{3,2,1,0:T(8,128)(2,1)S(1)} all-to-all(bf16[4,4,128,128]{3,2,1,0:T(8,128)(2,1)S(1)} %get-tuple-element.38), channel_id=1, replica_groups={{0,128,256,384},{64,192,320,448},{1,129,257,385},{65,193,321,449},{2,13..., dimensions={0} | all-to-all | bytes 1048576 | tf_op jit(solution)/shard_map/cond/branch_0_fun/all_to_all | solution.py:389
  39.9 5.4 %collective-permute-start = (bf16[4,4,128,128]{3,2,1,0:T(8,128)(2,1)S(1)}, bf16[4,4,128,128]{3,2,1,0:T(8,128)(2,1)S(1)}, u32[]{:S(2)}, u32[]{:S(2)}) collective-permute-start(bf16[4,4,128,128]{3,2,1,0:T(8,128)(2,1)S(1)} %all_to_all.16.window_ref), channel_id=1, source_target_pairs={{0,64},{64,0},{128,192},{192,128},{256,320},{320,256},{384,448},{4... | collective-permute-start | bytes 1572872 | tf_op jit(solution)/shard_map/cond/branch_0_fun/ppermute | solution.py:390
  45.3 1.5 %collective-permute-done.other_ref = bf16[4,4,128,128]{3,2,1,0:T(8,128)(2,1)S(1)} collective-permute-done((bf16[4,4,128,128]{3,2,1,0:T(8,128)(2,1)S(1)}, bf16[4,4,128,128]{3,2,1,0:T(8,128)(2,1)S(1)}, u32[]{:S(2)}, u32[]{:S(2)}) %collective-permute-start) | collective-permute-done | bytes 524320 | tf_op jit(solution)/shard_map/cond/branch_0_fun/ppermute | solution.py:390
  46.8 8.9 %wave_chain.2 = bf16[4,2,128,128]{3,2,1,0:T(8,128)(2,1)S(1)} custom-call(bf16[4,4,128,128]{3,2,1,0:T(8,128)(2,1)S(1)} %all_to_all.16.window_ref, bf16[4,4,128,128]{3,2,1,0:T(8,128)(2,1)S(1)} %collective-permute-done.other_ref, bf16[2,128,128]{2,1,0:T(8,128)(2,1)S(1)} %get-tuple-element.39.probe_ref, f32[128,128]{1,0:T(8,128)S(1)} %get-tuple-element.40.cos_ref, ...), custom_call_target="tpu_custom_call" | custom-call | tf_op jit(solution)/shard_map/cond/branch_0_fun/wave_chain/pallas_call | solution.py:363
  55.7 8.8 %all_to_all.17.grad_ref = bf16[4,2,128,128]{3,2,1,0:T(8,128)(2,1)S(1)} all-to-all(bf16[4,2,128,128]{3,2,1,0:T(8,128)(2,1)S(1)} %wave_chain.2), channel_id=1, replica_groups={{0,128,256,384},{64,192,320,448},{1,129,257,385},{65,193,321,449},{2,13..., dimensions={0} | all-to-all | bytes 524288 | tf_op jit(solution)/shard_map/cond/branch_0_fun/all_to_all | solution.py:392
  64.5 0.6 add_windows.2
  65.1 3.0 %collective-permute-start.4 = (bf16[2,128,256]{2,1,0:T(8,128)(2,1)S(1)}, bf16[2,128,256]{2,1,0:T(8,128)(2,1)S(1)}, u32[]{:S(2)}, u32[]{:S(2)}) collective-permute-start(bf16[2,128,256]{2,1,0:T(8,128)(2,1)S(1)} %get-tuple-element.75), channel_id=1, source_target_pairs={{0,63},{1,2},{2,1},{3,4},{4,3},{5,6},{6,5},{7,8},{8,7},{9,10},{10,... | collective-permute-start | bytes 393224 | tf_op jit(solution)/shard_map/ppermute | solution.py:300
  68.1 2.6 %collective-permute-start.5 = (bf16[2,128,256]{2,1,0:T(8,128)(2,1)S(1)}, bf16[2,128,256]{2,1,0:T(8,128)(2,1)S(1)}, u32[]{:S(2)}, u32[]{:S(2)}) collective-permute-start(bf16[2,128,256]{2,1,0:T(8,128)(2,1)S(1)} %get-tuple-element.76), channel_id=1, source_target_pairs={{0,1},{1,0},{2,3},{3,2},{4,5},{5,4},{6,7},{7,6},{8,9},{9,8},{10,11... | collective-permute-start | bytes 393224 | tf_op jit(solution)/shard_map/ppermute | solution.py:300
  70.7 3.5 %collective-permute-done.4 = bf16[2,128,256]{2,1,0:T(8,128)(2,1)S(1)} collective-permute-done((bf16[2,128,256]{2,1,0:T(8,128)(2,1)S(1)}, bf16[2,128,256]{2,1,0:T(8,128)(2,1)S(1)}, u32[]{:S(2)}, u32[]{:S(2)}) %collective-permute-start.4) | collective-permute-done | bytes 131104 | tf_op jit(solution)/shard_map/ppermute | solution.py:300
  74.2 0.0 collective-permute-done.5
  74.2 0.7 add_bitcast_fusion
Async XLA Ops:
  0.0 20.0 %copy-start = (bf16[4,128,256]{2,1,0:T(8,128)(2,1)S(1)}, bf16[4,128,256]{2,1,0:T(8,128)(2,1)}, u32[]{:S(2)}) copy-start(bf16[4,128,256]{2,1,0:T(8,128)(2,1)} %constant.5.clone.half_ref) | copy-start | bytes 786436
  1.8 25.0 %collective-permute-start.3 = (bf16[528,256]{1,0:T(8,128)(2,1)}, bf16[528,256]{1,0:T(8,128)(2,1)S(1)}, u32[]{:S(2)}, u32[]{:S(2)}) collective-permute-start(bf16[528,256]{1,0:T(8,128)(2,1)} %get-tuple-element.67), channel_id=1, source_target_pairs={{0,63},{1,2},{2,1},{3,4},{4,3},{5,6},{6,5},{7,8},{8,7},{9,10},{10,... | collective-permute-start | bytes 811016 | tf_op jit(solution)/shard_map/ppermute | solution.py:300
  16.2 10.5 %collective-permute-start.2 = (bf16[528,256]{1,0:T(8,128)(2,1)}, bf16[528,256]{1,0:T(8,128)(2,1)S(1)}, u32[]{:S(2)}, u32[]{:S(2)}) collective-permute-start(bf16[528,256]{1,0:T(8,128)(2,1)} %get-tuple-element.67), channel_id=1, source_target_pairs={{0,1},{1,0},{2,3},{3,2},{4,5},{5,4},{6,7},{7,6},{8,9},{9,8},{10,11... | collective-permute-start | bytes 811016 | tf_op jit(solution)/shard_map/ppermute | solution.py:300
  18.1 8.6 %collective-permute-start.1 = (bf16[16,256]{1,0:T(8,128)(2,1)S(1)}, bf16[16,256]{1,0:T(8,128)(2,1)S(1)}, u32[]{:S(2)}, u32[]{:S(2)}) collective-permute-start(bf16[16,256]{1,0:T(8,128)(2,1)S(1)} %get-tuple-element.66.note_ref), channel_id=1, source_target_pairs={{0,2},{1,3},{2,4},{3,5},{4,6},{5,7},{6,8},{7,9},{8,10},{9,11},{10,... | collective-permute-start | bytes 24584 | tf_op jit(solution)/shard_map/ppermute | solution.py:326
  20.0 0.8 %copy-start.1 = (f32[128,128]{1,0:T(8,128)S(1)}, f32[128,128]{1,0:T(8,128)}, u32[]{:S(2)}) copy-start(f32[128,128]{1,0:T(8,128)} %phase_ref.1) | copy-start | bytes 196612
  20.9 5.8 %copy-start.2 = (bf16[1,2,128,256]{3,2,1,0:T(8,128)(2,1)S(1)}, bf16[1,2,128,256]{3,2,1,0:T(8,128)(2,1)}, u32[]{:S(2)}) copy-start(bf16[1,2,128,256]{3,2,1,0:T(8,128)(2,1)} %param.9) | copy-start | bytes 393220
  20.9 5.8 %copy-start.3 = (bf16[1,2,128,256]{3,2,1,0:T(8,128)(2,1)S(1)}, bf16[1,2,128,256]{3,2,1,0:T(8,128)(2,1)}, u32[]{:S(2)}) copy-start(bf16[1,2,128,256]{3,2,1,0:T(8,128)(2,1)} %param.10) | copy-start | bytes 393220
  21.4 7.7 %copy-start.4 = (bf16[2,128,128]{2,1,0:T(8,128)(2,1)S(1)}, bf16[2,128,128]{2,1,0:T(8,128)(2,1)}, u32[]{:S(2)}) copy-start(bf16[2,128,128]{2,1,0:T(8,128)(2,1)} %param.11) | copy-start | bytes 196612
  39.9 6.9 %collective-permute-start = (bf16[4,4,128,128]{3,2,1,0:T(8,128)(2,1)S(1)}, bf16[4,4,128,128]{3,2,1,0:T(8,128)(2,1)S(1)}, u32[]{:S(2)}, u32[]{:S(2)}) collective-permute-start(bf16[4,4,128,128]{3,2,1,0:T(8,128)(2,1)S(1)} %all_to_all.16.window_ref), channel_id=1, source_target_pairs={{0,64},{64,0},{128,192},{192,128},{256,320},{320,256},{384,448},{4... | collective-permute-start | bytes 1572872 | tf_op jit(solution)/shard_map/cond/branch_0_fun/ppermute | solution.py:390
  65.1 9.0 %collective-permute-start.4 = (bf16[2,128,256]{2,1,0:T(8,128)(2,1)S(1)}, bf16[2,128,256]{2,1,0:T(8,128)(2,1)S(1)}, u32[]{:S(2)}, u32[]{:S(2)}) collective-permute-start(bf16[2,128,256]{2,1,0:T(8,128)(2,1)S(1)} %get-tuple-element.75), channel_id=1, source_target_pairs={{0,63},{1,2},{2,1},{3,4},{4,3},{5,6},{6,5},{7,8},{8,7},{9,10},{10,... | collective-permute-start | bytes 393224 | tf_op jit(solution)/shard_map/ppermute | solution.py:300
  68.1 6.1 %collective-permute-start.5 = (bf16[2,128,256]{2,1,0:T(8,128)(2,1)S(1)}, bf16[2,128,256]{2,1,0:T(8,128)(2,1)S(1)}, u32[]{:S(2)}, u32[]{:S(2)}) collective-permute-start(bf16[2,128,256]{2,1,0:T(8,128)(2,1)S(1)} %get-tuple-element.76), channel_id=1, source_target_pairs={{0,1},{1,0},{2,3},{3,2},{4,5},{5,4},{6,7},{7,6},{8,9},{9,8},{10,11... | collective-permute-start | bytes 393224 | tf_op jit(solution)/shard_map/ppermute | solution.py:300

commit v11 on v10

--- a/solution.py
+++ b/solution.py
@@ -220,7 +220,7 @@
     tan_re, tan_im = None, None
     scales = [1.0 / unit**2 for unit in units]
     for layer in range(slices):
-        wave_ref[layer, 0], wave_ref[layer, 1] = psi_re, psi_im
+        wave_ref[layer, 0], wave_ref[layer, 1] = psi_re.astype(BF16), psi_im.astype(BF16)
         obj_re, obj_im = window(layer, 0), window(layer, 1)
         dir_re, dir_im = window(layer, 2), window(layer, 3)
         exit_re = obj_re * psi_re - obj_im * psi_im
@@ -247,7 +247,7 @@
     adjoint = inverse(kernel_times(weighted, -1.0, scales[back]), back)
     for layer in range(slices - 1, -1, -1):
         adj_re, adj_im = adjoint[:size], adjoint[size:]
-        psi_re, psi_im = wave_ref[layer, 0], wave_ref[layer, 1]
+        psi_re, psi_im = wave_ref[layer, 0].astype(F32), wave_ref[layer, 1].astype(F32)
         later = grad if layer < slices - 1 else None
         grad = [(psi_re * adj_re + psi_im * adj_im).astype(BF16), (psi_re * adj_im - psi_im * adj_re).astype(BF16)]
         for part in range(2):
@@ -365,7 +365,7 @@
             out_shape=jax.ShapeDtypeStruct((windows.shape[0], 2, patch_size, patch_size), BF16),
             in_specs=[vmem] * 6,
             out_specs=vmem,
-            scratch_shapes=[pltpu.VMEM((cuts_count, 2, patch_size, patch_size), F32)],
+            scratch_shapes=[pltpu.VMEM((cuts_count, 2, patch_size, patch_size), BF16)],
             compiler_params=params,
             name="wave_chain",
         )(windows, other, *constants)

time: 75.3 us -> 75.3 us (level)
  no operation moved by 1% of the time
where the time goes in v11:
time: 75.3 us; the launch traced here: 74.9 us
  starting transfers between devices  29.2 us (39%)
  blocking collectives  19.6 us (26%)
  Pallas kernels  13.5 us (18%)
  waiting for transfers between devices  10.3 us (14%)
  local copies, waits for them, and re-layouts  0.85 us (1%)
  between operations  0.76 us (1%)
    ppermute x4, starting transfers between devices, exchanged(): lax.ppermute(block, 'strip', [(i, j % strip_count) for i, j in route])  21.9 us
    all_to_all x1, blocking collectives, one_per_chip(): lax.all_to_all(windows, 'cuts', 0, 0, axis_index_groups=same_core, tiled=...  10.8 us
    pallas_call x1, Pallas kernels, chain(): pl.pallas_call(functools.partial(chain_kernel, units), out_shape=jax.Shap...  8.88 us
    all_to_all x1, blocking collectives, one_per_chip(): lax.all_to_all(gradient, 'cuts', 0, 0, axis_index_groups=same_core, tiled...  8.79 us
    ppermute x1, starting transfers between devices, one_per_chip(): lax.ppermute(windows, 'cuts', [(i, i ^ 1) for i in range(cuts_count)])  5.4 us
    ppermute x1, waiting for transfers between devices, on_device(): lax.ppermute(note, 'strip', [(i, (i + REACH) % strip_count) for i in rang...  5.31 us
    ppermute x4, waiting for transfers between devices, exchanged(): lax.ppermute(block, 'strip', [(i, j % strip_count) for i, j in route])  3.46 us
    ppermute x1, starting transfers between devices, on_device(): lax.ppermute(note, 'strip', [(i, (i + REACH) % strip_count) for i in rang...  1.92 us
  transfers between devices with their start and end apart: 6, of which 3 were waited for; matrix products, arithmetic and copies ran while one was open for 0% of the time, Pallas kernels for 1%

profile of v11, /device:TPU:1, one launch (start us, length us, event | category | flops | bytes accessed | tf_op | source)
XLA Modules:
  0.0 74.9 jit_solution(16966000887232678964)
XLA Ops:
  0.0 0.0 copy-start
  0.0 1.8 %pack_block.1 = (bf16[528,256]{1,0:T(8,128)(2,1)}, bf16[16,256]{1,0:T(8,128)(2,1)S(1)}) custom-call(s32[2]{0:T(128)} %row_any.1, s32[2]{0:T(128)} %col_any.1, bf16[256,256]{1,0:T(8,128)(2,1)} %bitcast.5, bf16[256,256]{1,0:T(8,128)(2,1)} %bitcast.8), custom_call_target="tpu_custom_call" | custom-call | tf_op jit(solution)/shard_map/pack_block/pallas_call | solution.py:310
  1.8 14.4 %collective-permute-start.3 = (bf16[528,256]{1,0:T(8,128)(2,1)}, bf16[528,256]{1,0:T(8,128)(2,1)S(1)}, u32[]{:S(2)}, u32[]{:S(2)}) collective-permute-start(bf16[528,256]{1,0:T(8,128)(2,1)} %get-tuple-element.67), channel_id=1, source_target_pairs={{0,63},{1,2},{2,1},{3,4},{4,3},{5,6},{6,5},{7,8},{8,7},{9,10},{10,... | collective-permute-start | bytes 811016 | tf_op jit(solution)/shard_map/ppermute | solution.py:300
  16.2 1.9 %collective-permute-start.2 = (bf16[528,256]{1,0:T(8,128)(2,1)}, bf16[528,256]{1,0:T(8,128)(2,1)S(1)}, u32[]{:S(2)}, u32[]{:S(2)}) collective-permute-start(bf16[528,256]{1,0:T(8,128)(2,1)} %get-tuple-element.67), channel_id=1, source_target_pairs={{0,1},{1,0},{2,3},{3,2},{4,5},{5,4},{6,7},{7,6},{8,9},{9,8},{10,11... | collective-permute-start | bytes 811016 | tf_op jit(solution)/shard_map/ppermute | solution.py:300
  18.1 1.9 %collective-permute-start.1 = (bf16[16,256]{1,0:T(8,128)(2,1)S(1)}, bf16[16,256]{1,0:T(8,128)(2,1)S(1)}, u32[]{:S(2)}, u32[]{:S(2)}) collective-permute-start(bf16[16,256]{1,0:T(8,128)(2,1)S(1)} %get-tuple-element.66.note_ref), channel_id=1, source_target_pairs={{0,2},{1,3},{2,4},{3,5},{4,6},{5,7},{6,8},{7,9},{8,10},{9,11},{10,... | collective-permute-start | bytes 24584 | tf_op jit(solution)/shard_map/ppermute | solution.py:326
  20.0 0.0 copy-done
  20.0 0.0 copy-start.1
  20.1 0.8 %copy-done.1 = f32[128,128]{1,0:T(8,128)S(1)} copy-done((f32[128,128]{1,0:T(8,128)S(1)}, f32[128,128]{1,0:T(8,128)}, u32[]{:S(2)}) %copy-start.1) | copy-done | bytes 65560
  20.9 0.0 copy-start.2
  20.9 0.0 copy-start.3
  20.9 0.5 phase_tables.1
  21.4 0.0 copy-start.4
  21.4 5.3 %collective-permute-done.1.far_ref = bf16[16,256]{1,0:T(8,128)(2,1)S(1)} collective-permute-done((bf16[16,256]{1,0:T(8,128)(2,1)S(1)}, bf16[16,256]{1,0:T(8,128)(2,1)S(1)}, u32[]{:S(2)}, u32[]{:S(2)}) %collective-permute-start.1) | collective-permute-done | bytes 8224 | tf_op jit(solution)/shard_map/ppermute | solution.py:326
  26.7 0.0 collective-permute-done.3.first_ref
  26.7 0.0 collective-permute-done.2.second_ref
  26.7 0.0 copy-done.2
  26.7 0.0 copy-done.3
  26.7 1.7 %cut_windows.3 = (bf16[4,4,128,128]{3,2,1,0:T(8,128)(2,1)S(1)}, f32[8,128]{1,0:T(8,128)S(1)}, s32[1]{0:T(128)}) custom-call(bf16[16,256]{1,0:T(8,128)(2,1)S(1)} %collective-permute-done.1.far_ref, bf16[16,256]{1,0:T(8,128)(2,1)S(1)} %get-tuple-element.66.note_ref, bf16[256,256]{1,0:T(8,128)(2,1)S(1)} %bitcast.6, bf16[256,256]{1,0:T(8,128)(2,1)S(1)} %bitcast.9, ...), custom_call_target="tpu_custom_call" | custom-call | tf_op jit(solution)/shard_map/cut_windows/pallas_call | solution.py:353
  29.1 0.0 copy-done.4
  29.1 36.0 %conditional.1 = ((bf16[2,128,256]{2,1,0:T(8,128)(2,1)S(1)}, f32[2,128,256]{2,1,0:T(8,128)S(1)}, bf16[2,128,256]{2,1,0:T(8,128)(2,1)S(1)})) conditional(s32[]{:T(128)} %bitcast.2, (bf16[4,4,128,128]{3,2,1,0:T(8,128)(2,1)S(1)}, bf16[2,128,128]{2,1,0:T(8,128)(2,1)S(1)}, f32[128,128]{1,0:T(8,128)S(1)}, f32[128,128]{1,0:T(8,128)S(1)}, ...), branch_computations={%region_0.0_spmd, %region_1.0_spmd} | conditional | bytes 3670064 | solution.py:406
  29.1 10.8 %all_to_all.16.window_ref = bf16[4,4,128,128]{3,2,1,0:T(8,128)(2,1)S(1)} all-to-all(bf16[4,4,128,128]{3,2,1,0:T(8,128)(2,1)S(1)} %get-tuple-element.38), channel_id=1, replica_groups={{0,128,256,384},{64,192,320,448},{1,129,257,385},{65,193,321,449},{2,13..., dimensions={0} | all-to-all | bytes 1048576 | tf_op jit(solution)/shard_map/cond/branch_0_fun/all_to_all | solution.py:389
  39.9 5.4 %collective-permute-start = (bf16[4,4,128,128]{3,2,1,0:T(8,128)(2,1)S(1)}, bf16[4,4,128,128]{3,2,1,0:T(8,128)(2,1)S(1)}, u32[]{:S(2)}, u32[]{:S(2)}) collective-permute-start(bf16[4,4,128,128]{3,2,1,0:T(8,128)(2,1)S(1)} %all_to_all.16.window_ref), channel_id=1, source_target_pairs={{0,64},{64,0},{128,192},{192,128},{256,320},{320,256},{384,448},{4... | collective-permute-start | bytes 1572872 | tf_op jit(solution)/shard_map/cond/branch_0_fun/ppermute | solution.py:390
  45.3 1.5 %collective-permute-done.other_ref = bf16[4,4,128,128]{3,2,1,0:T(8,128)(2,1)S(1)} collective-permute-done((bf16[4,4,128,128]{3,2,1,0:T(8,128)(2,1)S(1)}, bf16[4,4,128,128]{3,2,1,0:T(8,128)(2,1)S(1)}, u32[]{:S(2)}, u32[]{:S(2)}) %collective-permute-start) | collective-permute-done | bytes 524320 | tf_op jit(solution)/shard_map/cond/branch_0_fun/ppermute | solution.py:390
  46.8 8.9 %wave_chain.2 = bf16[4,2,128,128]{3,2,1,0:T(8,128)(2,1)S(1)} custom-call(bf16[4,4,128,128]{3,2,1,0:T(8,128)(2,1)S(1)} %all_to_all.16.window_ref, bf16[4,4,128,128]{3,2,1,0:T(8,128)(2,1)S(1)} %collective-permute-done.other_ref, bf16[2,128,128]{2,1,0:T(8,128)(2,1)S(1)} %get-tuple-element.39.probe_ref, f32[128,128]{1,0:T(8,128)S(1)} %get-tuple-element.40.cos_ref, ...), custom_call_target="tpu_custom_call" | custom-call | tf_op jit(solution)/shard_map/cond/branch_0_fun/wave_chain/pallas_call | solution.py:363
  55.7 8.8 %all_to_all.17.grad_ref = bf16[4,2,128,128]{3,2,1,0:T(8,128)(2,1)S(1)} all-to-all(bf16[4,2,128,128]{3,2,1,0:T(8,128)(2,1)S(1)} %wave_chain.2), channel_id=1, replica_groups={{0,128,256,384},{64,192,320,448},{1,129,257,385},{65,193,321,449},{2,13..., dimensions={0} | all-to-all | bytes 524288 | tf_op jit(solution)/shard_map/cond/branch_0_fun/all_to_all | solution.py:392
  64.5 0.6 add_windows.2
  65.1 2.9 %collective-permute-start.4 = (bf16[2,128,256]{2,1,0:T(8,128)(2,1)S(1)}, bf16[2,128,256]{2,1,0:T(8,128)(2,1)S(1)}, u32[]{:S(2)}, u32[]{:S(2)}) collective-permute-start(bf16[2,128,256]{2,1,0:T(8,128)(2,1)S(1)} %get-tuple-element.75), channel_id=1, source_target_pairs={{0,63},{1,2},{2,1},{3,4},{4,3},{5,6},{6,5},{7,8},{8,7},{9,10},{10,... | collective-permute-start | bytes 393224 | tf_op jit(solution)/shard_map/ppermute | solution.py:300
  68.1 2.6 %collective-permute-start.5 = (bf16[2,128,256]{2,1,0:T(8,128)(2,1)S(1)}, bf16[2,128,256]{2,1,0:T(8,128)(2,1)S(1)}, u32[]{:S(2)}, u32[]{:S(2)}) collective-permute-start(bf16[2,128,256]{2,1,0:T(8,128)(2,1)S(1)} %get-tuple-element.76), channel_id=1, source_target_pairs={{0,1},{1,0},{2,3},{3,2},{4,5},{5,4},{6,7},{7,6},{8,9},{9,8},{10,11... | collective-permute-start | bytes 393224 | tf_op jit(solution)/shard_map/ppermute | solution.py:300
  70.7 3.5 %collective-permute-done.4 = bf16[2,128,256]{2,1,0:T(8,128)(2,1)S(1)} collective-permute-done((bf16[2,128,256]{2,1,0:T(8,128)(2,1)S(1)}, bf16[2,128,256]{2,1,0:T(8,128)(2,1)S(1)}, u32[]{:S(2)}, u32[]{:S(2)}) %collective-permute-start.4) | collective-permute-done | bytes 131104 | tf_op jit(solution)/shard_map/ppermute | solution.py:300
  74.2 0.0 collective-permute-done.5
  74.2 0.7 add_bitcast_fusion
Async XLA Ops:
  0.0 20.0 %copy-start = (bf16[4,128,256]{2,1,0:T(8,128)(2,1)S(1)}, bf16[4,128,256]{2,1,0:T(8,128)(2,1)}, u32[]{:S(2)}) copy-start(bf16[4,128,256]{2,1,0:T(8,128)(2,1)} %constant.5.clone.half_ref) | copy-start | bytes 786436
  1.8 25.0 %collective-permute-start.3 = (bf16[528,256]{1,0:T(8,128)(2,1)}, bf16[528,256]{1,0:T(8,128)(2,1)S(1)}, u32[]{:S(2)}, u32[]{:S(2)}) collective-permute-start(bf16[528,256]{1,0:T(8,128)(2,1)} %get-tuple-element.67), channel_id=1, source_target_pairs={{0,63},{1,2},{2,1},{3,4},{4,3},{5,6},{6,5},{7,8},{8,7},{9,10},{10,... | collective-permute-start | bytes 811016 | tf_op jit(solution)/shard_map/ppermute | solution.py:300
  16.2 10.5 %collective-permute-start.2 = (bf16[528,256]{1,0:T(8,128)(2,1)}, bf16[528,256]{1,0:T(8,128)(2,1)S(1)}, u32[]{:S(2)}, u32[]{:S(2)}) collective-permute-start(bf16[528,256]{1,0:T(8,128)(2,1)} %get-tuple-element.67), channel_id=1, source_target_pairs={{0,1},{1,0},{2,3},{3,2},{4,5},{5,4},{6,7},{7,6},{8,9},{9,8},{10,11... | collective-permute-start | bytes 811016 | tf_op jit(solution)/shard_map/ppermute | solution.py:300
  18.1 8.6 %collective-permute-start.1 = (bf16[16,256]{1,0:T(8,128)(2,1)S(1)}, bf16[16,256]{1,0:T(8,128)(2,1)S(1)}, u32[]{:S(2)}, u32[]{:S(2)}) collective-permute-start(bf16[16,256]{1,0:T(8,128)(2,1)S(1)} %get-tuple-element.66.note_ref), channel_id=1, source_target_pairs={{0,2},{1,3},{2,4},{3,5},{4,6},{5,7},{6,8},{7,9},{8,10},{9,11},{10,... | collective-permute-start | bytes 24584 | tf_op jit(solution)/shard_map/ppermute | solution.py:326
  20.0 0.8 %copy-start.1 = (f32[128,128]{1,0:T(8,128)S(1)}, f32[128,128]{1,0:T(8,128)}, u32[]{:S(2)}) copy-start(f32[128,128]{1,0:T(8,128)} %phase_ref.1) | copy-start | bytes 196612
  20.9 5.8 %copy-start.2 = (bf16[1,2,128,256]{3,2,1,0:T(8,128)(2,1)S(1)}, bf16[1,2,128,256]{3,2,1,0:T(8,128)(2,1)}, u32[]{:S(2)}) copy-start(bf16[1,2,128,256]{3,2,1,0:T(8,128)(2,1)} %param.9) | copy-start | bytes 393220
  20.9 5.8 %copy-start.3 = (bf16[1,2,128,256]{3,2,1,0:T(8,128)(2,1)S(1)}, bf16[1,2,128,256]{3,2,1,0:T(8,128)(2,1)}, u32[]{:S(2)}) copy-start(bf16[1,2,128,256]{3,2,1,0:T(8,128)(2,1)} %param.10) | copy-start | bytes 393220
  21.4 7.7 %copy-start.4 = (bf16[2,128,128]{2,1,0:T(8,128)(2,1)S(1)}, bf16[2,128,128]{2,1,0:T(8,128)(2,1)}, u32[]{:S(2)}) copy-start(bf16[2,128,128]{2,1,0:T(8,128)(2,1)} %param.11) | copy-start | bytes 196612
  39.9 6.9 %collective-permute-start = (bf16[4,4,128,128]{3,2,1,0:T(8,128)(2,1)S(1)}, bf16[4,4,128,128]{3,2,1,0:T(8,128)(2,1)S(1)}, u32[]{:S(2)}, u32[]{:S(2)}) collective-permute-start(bf16[4,4,128,128]{3,2,1,0:T(8,128)(2,1)S(1)} %all_to_all.16.window_ref), channel_id=1, source_target_pairs={{0,64},{64,0},{128,192},{192,128},{256,320},{320,256},{384,448},{4... | collective-permute-start | bytes 1572872 | tf_op jit(solution)/shard_map/cond/branch_0_fun/ppermute | solution.py:390
  65.1 9.0 %collective-permute-start.4 = (bf16[2,128,256]{2,1,0:T(8,128)(2,1)S(1)}, bf16[2,128,256]{2,1,0:T(8,128)(2,1)S(1)}, u32[]{:S(2)}, u32[]{:S(2)}) collective-permute-start(bf16[2,128,256]{2,1,0:T(8,128)(2,1)S(1)} %get-tuple-element.75), channel_id=1, source_target_pairs={{0,63},{1,2},{2,1},{3,4},{4,3},{5,6},{6,5},{7,8},{8,7},{9,10},{10,... | collective-permute-start | bytes 393224 | tf_op jit(solution)/shard_map/ppermute | solution.py:300
  68.1 6.1 %collective-permute-start.5 = (bf16[2,128,256]{2,1,0:T(8,128)(2,1)S(1)}, bf16[2,128,256]{2,1,0:T(8,128)(2,1)S(1)}, u32[]{:S(2)}, u32[]{:S(2)}) collective-permute-start(bf16[2,128,256]{2,1,0:T(8,128)(2,1)S(1)} %get-tuple-element.76), channel_id=1, source_target_pairs={{0,1},{1,0},{2,3},{3,2},{4,5},{5,4},{6,7},{7,6},{8,9},{9,8},{10,11... | collective-permute-start | bytes 393224 | tf_op jit(solution)/shard_map/ppermute | solution.py:300

commit v12 on v10

--- a/solution.py
+++ b/solution.py
@@ -196,8 +196,8 @@
         return jnp.concatenate([dot(table[i * step : (i + 1) * step], columns) for i in range(2)], axis=0)
 
     def from_right(rows, table):
-        step = rows.shape[0] // 2
-        return jnp.concatenate([dot(rows[i * step : (i + 1) * step], table) for i in range(2)], axis=0)
+        pieces = [dot(rows[i : i + size], table) for i in range(0, rows.shape[0], size)]
+        return jnp.concatenate(pieces, axis=0) if len(pieces) > 1 else pieces[0]
 
     def forward(columns, table):
         half = from_left(table_ref[table, 0], columns.astype(BF16)).astype(BF16)

time: 75.3 us -> 75.3 us (level)
  no operation moved by 1% of the time
where the time goes in v12:
time: 75.3 us; the launch traced here: 74.9 us
  starting transfers between devices  29.2 us (39%)
  blocking collectives  19.6 us (26%)
  Pallas kernels  13.4 us (18%)
  waiting for transfers between devices  10.3 us (14%)
  local copies, waits for them, and re-layouts  0.85 us (1%)
  between operations  0.76 us (1%)
    ppermute x4, starting transfers between devices, exchanged(): lax.ppermute(block, 'strip', [(i, j % strip_count) for i, j in route])  21.9 us
    all_to_all x1, blocking collectives, one_per_chip(): lax.all_to_all(windows, 'cuts', 0, 0, axis_index_groups=same_core, tiled=...  10.8 us
    pallas_call x1, Pallas kernels, chain(): pl.pallas_call(functools.partial(chain_kernel, units), out_shape=jax.Shap...  8.86 us
    all_to_all x1, blocking collectives, one_per_chip(): lax.all_to_all(gradient, 'cuts', 0, 0, axis_index_groups=same_core, tiled...  8.79 us
    ppermute x1, starting transfers between devices, one_per_chip(): lax.ppermute(windows, 'cuts', [(i, i ^ 1) for i in range(cuts_count)])  5.4 us
    ppermute x1, waiting for transfers between devices, on_device(): lax.ppermute(note, 'strip', [(i, (i + REACH) % strip_count) for i in rang...  5.31 us
    ppermute x4, waiting for transfers between devices, exchanged(): lax.ppermute(block, 'strip', [(i, j % strip_count) for i, j in route])  3.46 us
    ppermute x1, starting transfers between devices, on_device(): lax.ppermute(note, 'strip', [(i, (i + REACH) % strip_count) for i in rang...  1.92 us
  transfers between devices with their start and end apart: 6, of which 3 were waited for; matrix products, arithmetic and copies ran while one was open for 0% of the time, Pallas kernels for 1%

profile of v12, /device:TPU:1, one launch (start us, length us, event | category | flops | bytes accessed | tf_op | source)
XLA Modules:
  0.0 74.9 jit_solution(10320535519477853883)
XLA Ops:
  0.0 0.0 copy-start
  0.0 1.8 %pack_block.1 = (bf16[528,256]{1,0:T(8,128)(2,1)}, bf16[16,256]{1,0:T(8,128)(2,1)S(1)}) custom-call(s32[2]{0:T(128)} %row_any.1, s32[2]{0:T(128)} %col_any.1, bf16[256,256]{1,0:T(8,128)(2,1)} %bitcast.5, bf16[256,256]{1,0:T(8,128)(2,1)} %bitcast.8), custom_call_target="tpu_custom_call" | custom-call | tf_op jit(solution)/shard_map/pack_block/pallas_call | solution.py:310
  1.8 14.4 %collective-permute-start.3 = (bf16[528,256]{1,0:T(8,128)(2,1)}, bf16[528,256]{1,0:T(8,128)(2,1)S(1)}, u32[]{:S(2)}, u32[]{:S(2)}) collective-permute-start(bf16[528,256]{1,0:T(8,128)(2,1)} %get-tuple-element.67), channel_id=1, source_target_pairs={{0,63},{1,2},{2,1},{3,4},{4,3},{5,6},{6,5},{7,8},{8,7},{9,10},{10,... | collective-permute-start | bytes 811016 | tf_op jit(solution)/shard_map/ppermute | solution.py:300
  16.2 1.9 %collective-permute-start.2 = (bf16[528,256]{1,0:T(8,128)(2,1)}, bf16[528,256]{1,0:T(8,128)(2,1)S(1)}, u32[]{:S(2)}, u32[]{:S(2)}) collective-permute-start(bf16[528,256]{1,0:T(8,128)(2,1)} %get-tuple-element.67), channel_id=1, source_target_pairs={{0,1},{1,0},{2,3},{3,2},{4,5},{5,4},{6,7},{7,6},{8,9},{9,8},{10,11... | collective-permute-start | bytes 811016 | tf_op jit(solution)/shard_map/ppermute | solution.py:300
  18.1 1.9 %collective-permute-start.1 = (bf16[16,256]{1,0:T(8,128)(2,1)S(1)}, bf16[16,256]{1,0:T(8,128)(2,1)S(1)}, u32[]{:S(2)}, u32[]{:S(2)}) collective-permute-start(bf16[16,256]{1,0:T(8,128)(2,1)S(1)} %get-tuple-element.66.note_ref), channel_id=1, source_target_pairs={{0,2},{1,3},{2,4},{3,5},{4,6},{5,7},{6,8},{7,9},{8,10},{9,11},{10,... | collective-permute-start | bytes 24584 | tf_op jit(solution)/shard_map/ppermute | solution.py:326
  20.0 0.0 copy-done
  20.0 0.0 copy-start.1
  20.1 0.8 %copy-done.1 = f32[128,128]{1,0:T(8,128)S(1)} copy-done((f32[128,128]{1,0:T(8,128)S(1)}, f32[128,128]{1,0:T(8,128)}, u32[]{:S(2)}) %copy-start.1) | copy-done | bytes 65560
  20.9 0.0 copy-start.2
  20.9 0.0 copy-start.3
  20.9 0.5 phase_tables.1
  21.4 0.0 copy-start.4
  21.4 5.3 %collective-permute-done.1.far_ref = bf16[16,256]{1,0:T(8,128)(2,1)S(1)} collective-permute-done((bf16[16,256]{1,0:T(8,128)(2,1)S(1)}, bf16[16,256]{1,0:T(8,128)(2,1)S(1)}, u32[]{:S(2)}, u32[]{:S(2)}) %collective-permute-start.1) | collective-permute-done | bytes 8224 | tf_op jit(solution)/shard_map/ppermute | solution.py:326
  26.7 0.0 collective-permute-done.3.first_ref
  26.7 0.0 collective-permute-done.2.second_ref
  26.7 0.0 copy-done.2
  26.7 0.0 copy-done.3
  26.7 1.7 %cut_windows.3 = (bf16[4,4,128,128]{3,2,1,0:T(8,128)(2,1)S(1)}, f32[8,128]{1,0:T(8,128)S(1)}, s32[1]{0:T(128)}) custom-call(bf16[16,256]{1,0:T(8,128)(2,1)S(1)} %collective-permute-done.1.far_ref, bf16[16,256]{1,0:T(8,128)(2,1)S(1)} %get-tuple-element.66.note_ref, bf16[256,256]{1,0:T(8,128)(2,1)S(1)} %bitcast.6, bf16[256,256]{1,0:T(8,128)(2,1)S(1)} %bitcast.9, ...), custom_call_target="tpu_custom_call" | custom-call | tf_op jit(solution)/shard_map/cut_windows/pallas_call | solution.py:353
  29.1 0.0 copy-done.4
  29.1 36.0 %conditional.1 = ((bf16[2,128,256]{2,1,0:T(8,128)(2,1)S(1)}, f32[2,128,256]{2,1,0:T(8,128)S(1)}, bf16[2,128,256]{2,1,0:T(8,128)(2,1)S(1)})) conditional(s32[]{:T(128)} %bitcast.2, (bf16[4,4,128,128]{3,2,1,0:T(8,128)(2,1)S(1)}, bf16[2,128,128]{2,1,0:T(8,128)(2,1)S(1)}, f32[128,128]{1,0:T(8,128)S(1)}, f32[128,128]{1,0:T(8,128)S(1)}, ...), branch_computations={%region_0.0_spmd, %region_1.0_spmd} | conditional | bytes 3670064 | solution.py:406
  29.1 10.8 %all_to_all.16.window_ref = bf16[4,4,128,128]{3,2,1,0:T(8,128)(2,1)S(1)} all-to-all(bf16[4,4,128,128]{3,2,1,0:T(8,128)(2,1)S(1)} %get-tuple-element.38), channel_id=1, replica_groups={{0,128,256,384},{64,192,320,448},{1,129,257,385},{65,193,321,449},{2,13..., dimensions={0} | all-to-all | bytes 1048576 | tf_op jit(solution)/shard_map/cond/branch_0_fun/all_to_all | solution.py:389
  39.9 5.4 %collective-permute-start = (bf16[4,4,128,128]{3,2,1,0:T(8,128)(2,1)S(1)}, bf16[4,4,128,128]{3,2,1,0:T(8,128)(2,1)S(1)}, u32[]{:S(2)}, u32[]{:S(2)}) collective-permute-start(bf16[4,4,128,128]{3,2,1,0:T(8,128)(2,1)S(1)} %all_to_all.16.window_ref), channel_id=1, source_target_pairs={{0,64},{64,0},{128,192},{192,128},{256,320},{320,256},{384,448},{4... | collective-permute-start | bytes 1572872 | tf_op jit(solution)/shard_map/cond/branch_0_fun/ppermute | solution.py:390
  45.3 1.5 %collective-permute-done.other_ref = bf16[4,4,128,128]{3,2,1,0:T(8,128)(2,1)S(1)} collective-permute-done((bf16[4,4,128,128]{3,2,1,0:T(8,128)(2,1)S(1)}, bf16[4,4,128,128]{3,2,1,0:T(8,128)(2,1)S(1)}, u32[]{:S(2)}, u32[]{:S(2)}) %collective-permute-start) | collective-permute-done | bytes 524320 | tf_op jit(solution)/shard_map/cond/branch_0_fun/ppermute | solution.py:390
  46.8 8.9 %wave_chain.2 = bf16[4,2,128,128]{3,2,1,0:T(8,128)(2,1)S(1)} custom-call(bf16[4,4,128,128]{3,2,1,0:T(8,128)(2,1)S(1)} %all_to_all.16.window_ref, bf16[4,4,128,128]{3,2,1,0:T(8,128)(2,1)S(1)} %collective-permute-done.other_ref, bf16[2,128,128]{2,1,0:T(8,128)(2,1)S(1)} %get-tuple-element.39.probe_ref, f32[128,128]{1,0:T(8,128)S(1)} %get-tuple-element.40.cos_ref, ...), custom_call_target="tpu_custom_call" | custom-call | tf_op jit(solution)/shard_map/cond/branch_0_fun/wave_chain/pallas_call | solution.py:363
  55.7 8.8 %all_to_all.17.grad_ref = bf16[4,2,128,128]{3,2,1,0:T(8,128)(2,1)S(1)} all-to-all(bf16[4,2,128,128]{3,2,1,0:T(8,128)(2,1)S(1)} %wave_chain.2), channel_id=1, replica_groups={{0,128,256,384},{64,192,320,448},{1,129,257,385},{65,193,321,449},{2,13..., dimensions={0} | all-to-all | bytes 524288 | tf_op jit(solution)/shard_map/cond/branch_0_fun/all_to_all | solution.py:392
  64.5 0.6 add_windows.2
  65.1 3.0 %collective-permute-start.4 = (bf16[2,128,256]{2,1,0:T(8,128)(2,1)S(1)}, bf16[2,128,256]{2,1,0:T(8,128)(2,1)S(1)}, u32[]{:S(2)}, u32[]{:S(2)}) collective-permute-start(bf16[2,128,256]{2,1,0:T(8,128)(2,1)S(1)} %get-tuple-element.75), channel_id=1, source_target_pairs={{0,63},{1,2},{2,1},{3,4},{4,3},{5,6},{6,5},{7,8},{8,7},{9,10},{10,... | collective-permute-start | bytes 393224 | tf_op jit(solution)/shard_map/ppermute | solution.py:300
  68.1 2.6 %collective-permute-start.5 = (bf16[2,128,256]{2,1,0:T(8,128)(2,1)S(1)}, bf16[2,128,256]{2,1,0:T(8,128)(2,1)S(1)}, u32[]{:S(2)}, u32[]{:S(2)}) collective-permute-start(bf16[2,128,256]{2,1,0:T(8,128)(2,1)S(1)} %get-tuple-element.76), channel_id=1, source_target_pairs={{0,1},{1,0},{2,3},{3,2},{4,5},{5,4},{6,7},{7,6},{8,9},{9,8},{10,11... | collective-permute-start | bytes 393224 | tf_op jit(solution)/shard_map/ppermute | solution.py:300
  70.7 3.5 %collective-permute-done.4 = bf16[2,128,256]{2,1,0:T(8,128)(2,1)S(1)} collective-permute-done((bf16[2,128,256]{2,1,0:T(8,128)(2,1)S(1)}, bf16[2,128,256]{2,1,0:T(8,128)(2,1)S(1)}, u32[]{:S(2)}, u32[]{:S(2)}) %collective-permute-start.4) | collective-permute-done | bytes 131104 | tf_op jit(solution)/shard_map/ppermute | solution.py:300
  74.2 0.0 collective-permute-done.5
  74.2 0.7 add_bitcast_fusion
Async XLA Ops:
  0.0 20.0 %copy-start = (bf16[4,128,256]{2,1,0:T(8,128)(2,1)S(1)}, bf16[4,128,256]{2,1,0:T(8,128)(2,1)}, u32[]{:S(2)}) copy-start(bf16[4,128,256]{2,1,0:T(8,128)(2,1)} %constant.5.clone.half_ref) | copy-start | bytes 786436
  1.8 25.0 %collective-permute-start.3 = (bf16[528,256]{1,0:T(8,128)(2,1)}, bf16[528,256]{1,0:T(8,128)(2,1)S(1)}, u32[]{:S(2)}, u32[]{:S(2)}) collective-permute-start(bf16[528,256]{1,0:T(8,128)(2,1)} %get-tuple-element.67), channel_id=1, source_target_pairs={{0,63},{1,2},{2,1},{3,4},{4,3},{5,6},{6,5},{7,8},{8,7},{9,10},{10,... | collective-permute-start | bytes 811016 | tf_op jit(solution)/shard_map/ppermute | solution.py:300
  16.2 10.5 %collective-permute-start.2 = (bf16[528,256]{1,0:T(8,128)(2,1)}, bf16[528,256]{1,0:T(8,128)(2,1)S(1)}, u32[]{:S(2)}, u32[]{:S(2)}) collective-permute-start(bf16[528,256]{1,0:T(8,128)(2,1)} %get-tuple-element.67), channel_id=1, source_target_pairs={{0,1},{1,0},{2,3},{3,2},{4,5},{5,4},{6,7},{7,6},{8,9},{9,8},{10,11... | collective-permute-start | bytes 811016 | tf_op jit(solution)/shard_map/ppermute | solution.py:300
  18.1 8.6 %collective-permute-start.1 = (bf16[16,256]{1,0:T(8,128)(2,1)S(1)}, bf16[16,256]{1,0:T(8,128)(2,1)S(1)}, u32[]{:S(2)}, u32[]{:S(2)}) collective-permute-start(bf16[16,256]{1,0:T(8,128)(2,1)S(1)} %get-tuple-element.66.note_ref), channel_id=1, source_target_pairs={{0,2},{1,3},{2,4},{3,5},{4,6},{5,7},{6,8},{7,9},{8,10},{9,11},{10,... | collective-permute-start | bytes 24584 | tf_op jit(solution)/shard_map/ppermute | solution.py:326
  20.0 0.8 %copy-start.1 = (f32[128,128]{1,0:T(8,128)S(1)}, f32[128,128]{1,0:T(8,128)}, u32[]{:S(2)}) copy-start(f32[128,128]{1,0:T(8,128)} %phase_ref.1) | copy-start | bytes 196612
  20.9 5.8 %copy-start.2 = (bf16[1,2,128,256]{3,2,1,0:T(8,128)(2,1)S(1)}, bf16[1,2,128,256]{3,2,1,0:T(8,128)(2,1)}, u32[]{:S(2)}) copy-start(bf16[1,2,128,256]{3,2,1,0:T(8,128)(2,1)} %param.9) | copy-start | bytes 393220
  20.9 5.8 %copy-start.3 = (bf16[1,2,128,256]{3,2,1,0:T(8,128)(2,1)S(1)}, bf16[1,2,128,256]{3,2,1,0:T(8,128)(2,1)}, u32[]{:S(2)}) copy-start(bf16[1,2,128,256]{3,2,1,0:T(8,128)(2,1)} %param.10) | copy-start | bytes 393220
  21.4 7.7 %copy-start.4 = (bf16[2,128,128]{2,1,0:T(8,128)(2,1)S(1)}, bf16[2,128,128]{2,1,0:T(8,128)(2,1)}, u32[]{:S(2)}) copy-start(bf16[2,128,128]{2,1,0:T(8,128)(2,1)} %param.11) | copy-start | bytes 196612
  39.9 6.9 %collective-permute-start = (bf16[4,4,128,128]{3,2,1,0:T(8,128)(2,1)S(1)}, bf16[4,4,128,128]{3,2,1,0:T(8,128)(2,1)S(1)}, u32[]{:S(2)}, u32[]{:S(2)}) collective-permute-start(bf16[4,4,128,128]{3,2,1,0:T(8,128)(2,1)S(1)} %all_to_all.16.window_ref), channel_id=1, source_target_pairs={{0,64},{64,0},{128,192},{192,128},{256,320},{320,256},{384,448},{4... | collective-permute-start | bytes 1572872 | tf_op jit(solution)/shard_map/cond/branch_0_fun/ppermute | solution.py:390
  65.1 9.0 %collective-permute-start.4 = (bf16[2,128,256]{2,1,0:T(8,128)(2,1)S(1)}, bf16[2,128,256]{2,1,0:T(8,128)(2,1)S(1)}, u32[]{:S(2)}, u32[]{:S(2)}) collective-permute-start(bf16[2,128,256]{2,1,0:T(8,128)(2,1)S(1)} %get-tuple-element.75), channel_id=1, source_target_pairs={{0,63},{1,2},{2,1},{3,4},{4,3},{5,6},{6,5},{7,8},{8,7},{9,10},{10,... | collective-permute-start | bytes 393224 | tf_op jit(solution)/shard_map/ppermute | solution.py:300
  68.1 6.1 %collective-permute-start.5 = (bf16[2,128,256]{2,1,0:T(8,128)(2,1)S(1)}, bf16[2,128,256]{2,1,0:T(8,128)(2,1)S(1)}, u32[]{:S(2)}, u32[]{:S(2)}) collective-permute-start(bf16[2,128,256]{2,1,0:T(8,128)(2,1)S(1)} %get-tuple-element.76), channel_id=1, source_target_pairs={{0,1},{1,0},{2,3},{3,2},{4,5},{5,4},{6,7},{7,6},{8,9},{9,8},{10,11... | collective-permute-start | bytes 393224 | tf_op jit(solution)/shard_map/ppermute | solution.py:300
